TPU v7x, 256 devices: a whole 4x4x8 slice. The times are simulated.
256 devices in a mesh: batch: 8 (over y_hi, x), tile: 32 (over z, y_lo, core).
Axes of the slice: x: 4, y: 4 (y_hi: 2, y_lo: 2; y = y_hi * 2 + y_lo), z: 8, core: 2. Of those that a mesh axis runs over, the one named last changes fastest.
Arguments:
- queries: bfloat16 [8, 4096, 2048], P('batch', 'tile'), may hold values from -120 to 120
- keys: bfloat16 [8, 4096, 2048], P('batch', 'tile'), may hold values from -6 to 6
- values: bfloat16 [8, 4096, 2048], P('batch', 'tile'), may hold values from -6 to 6
- grad_out: bfloat16 [8, 4096, 2048], P('batch', 'tile'), may hold values from -6 to 6
- valid: int32 [8, 4096], P('batch'), may hold values from 0 to 1, as said below
- scale_ids: int32 [4096], replicated, may hold values from 0 to 12, as said below
- scale_bias: float32 [16, 13, 13], replicated, may hold values from -6 to 6
Outputs:
- attended: bfloat16 [8, 4096, 2048], P('batch', 'tile')
- grad_queries: bfloat16 [8, 4096, 2048], P('batch', 'tile')
- grad_keys: bfloat16 [8, 4096, 2048], P('batch', 'tile')
- grad_values: bfloat16 [8, 4096, 2048], P('batch', 'tile')
- grad_bias: float32 [16, 13, 13], replicated
Inputs may be any that keep to these rules, and one draw needn't show every extreme that they name: Coarse tokens are always valid; in each tile the valid fine tokens form a leading run of 30 to 120 tokens, and in every image some tile has all its fine tokens valid. `scale_ids`: over the coarse tokens taken tile by tile in order, scale ids never fall, start at 0 and end at 8; within each tile the fine tokens carry scales 9 to 12, never falling, the first one 9 and the last 12.
All inputs are finite; a program needn't handle non-finite values.
Results may differ from a plain program's by a relative error of at most 0.0059.
Values may be sent and summed in bfloat16 or wider, within the bound.
No kernel may reach another device: no remote copies, remote signals or barrier semaphores. Data moves between devices by JAX's collectives and lax.ppermute only.
A program may use at most 128 MiB of HBM per device.

v0:
```python
import math

import jax
import jax.numpy as jnp
from jax import lax
from jax.sharding import PartitionSpec as P

C_DEV = 8


masked_value = -1e30
head_block = 4


def with_halo(shard, sides, width):
    for axis, dim in sides:
        count, length = (lax.axis_size(axis), shard.shape[dim])
        up = [(i, (i + 1) % count) for i in range(count - 1)]
        down = [(j, i) for i, j in up]
        last = lax.slice_in_dim(shard, length - width, length, axis=dim)
        first = lax.slice_in_dim(shard, 0, width, axis=dim)
        before = lax.ppermute(last, axis, up)
        after = lax.ppermute(first, axis, down)
        shard = jnp.concatenate([before, shard, after], axis=dim)
    return shard


def shifted(block, axis, distance):
    devices = range(lax.axis_size(axis))
    route = [(i - distance, i) for i in devices if i - distance in devices]
    return lax.ppermute(block, axis, route)


def split_heads(array, group_count):
    return array.reshape(array.shape[0], group_count, head_block, -1).transpose(1, 0, 2, 3)


def merge_heads(array):
    return array.transpose(1, 0, 2, 3).reshape(array.shape[1], -1)


def attention_scores(
    query_block, key_block, bias_block, onehot_rows, onehot_cols, admitted, inv_scale
):
    raw_scores = jnp.einsum(
        "rhd,khd->hrk", query_block, key_block, preferred_element_type=jnp.float32
    )
    row_bias = jnp.einsum("rs,hsb->hrb", onehot_rows, bias_block, precision=lax.Precision.HIGHEST)
    pair_bias = jnp.einsum("hrb,kb->hrk", row_bias, onehot_cols, precision=lax.Precision.HIGHEST)
    return jnp.where(admitted[None], raw_scores * inv_scale + pair_bias, masked_value)


def shards(queries, keys, values, grad_out, valid, scale_ids, scale_bias):
    row_count = queries.shape[1]
    feature_width = queries.shape[2]
    head_count = scale_bias.shape[0]
    level_count = scale_bias.shape[1]
    head_size = feature_width // head_count
    group_count = head_count // head_block
    tile_count = lax.axis_size("tile")
    tile_here = lax.axis_index("tile")
    coarse_count = C_DEV
    fine_count = row_count - coarse_count
    coarse_total = coarse_count * tile_count
    inv_scale = 1.0 / math.sqrt(head_size)
    highest = lax.Precision.HIGHEST
    valid_grid = valid[0].reshape(tile_count, row_count)
    scale_grid = scale_ids.reshape(tile_count, row_count)
    own_valid = lax.dynamic_index_in_dim(valid_grid, tile_here, 0, keepdims=False)
    own_scale = lax.dynamic_index_in_dim(scale_grid, tile_here, 0, keepdims=False)
    coarse_scale = scale_grid[:, :coarse_count].reshape(-1)
    coarse_valid = valid_grid[:, :coarse_count].reshape(-1)
    padded_valid = jnp.pad(valid_grid[:, coarse_count:], ((1, 1), (0, 0)))
    padded_scale = jnp.pad(scale_grid[:, coarse_count:], ((1, 1), (0, 0)))
    near_valid = lax.dynamic_slice_in_dim(padded_valid, tile_here, 3, 0).reshape(-1)
    near_scale = lax.dynamic_slice_in_dim(padded_scale, tile_here, 3, 0).reshape(-1)
    allowed_coarse = (coarse_scale[None, :] <= own_scale[:, None]) & (coarse_valid[None, :] > 0)
    allowed_near = (near_scale[None, :] <= own_scale[:, None]) & (near_valid[None, :] > 0)
    level_ids = jnp.arange(level_count, dtype=jnp.int32)
    onehot_own = (own_scale[:, None] == level_ids[None, :]).astype(jnp.float32)
    onehot_coarse = (coarse_scale[:, None] == level_ids[None, :]).astype(jnp.float32)
    onehot_near = (near_scale[:, None] == level_ids[None, :]).astype(jnp.float32)
    gathered = (
        lax.all_gather(keys[0, :coarse_count], "tile", axis=0, tiled=True),
        lax.all_gather(values[0, :coarse_count], "tile", axis=0, tiled=True),
    )
    near_pair = with_halo(
        jnp.stack([keys[0, coarse_count:], values[0, coarse_count:]]), (("tile", 1),), fine_count
    )
    query_groups = split_heads(queries[0], group_count)
    bias_groups = scale_bias.reshape(group_count, head_block, level_count, level_count)
    coarse_keys = split_heads(gathered[0], group_count)
    coarse_values = split_heads(gathered[1], group_count)
    near_keys = split_heads(near_pair[0], group_count)
    near_values = split_heads(near_pair[1], group_count)

    def forward_group(inputs):
        query_block, key_coarse, value_coarse, key_near, value_near, bias_block = inputs
        scores_coarse = attention_scores(
            query_block,
            key_coarse,
            bias_block,
            onehot_own,
            onehot_coarse,
            allowed_coarse,
            inv_scale,
        )
        scores_near = attention_scores(
            query_block, key_near, bias_block, onehot_own, onehot_near, allowed_near, inv_scale
        )
        row_peak = jnp.maximum(jnp.max(scores_coarse, axis=-1), jnp.max(scores_near, axis=-1))
        exp_coarse = jnp.exp(scores_coarse - row_peak[:, :, None])
        exp_near = jnp.exp(scores_near - row_peak[:, :, None])
        row_total = jnp.sum(exp_coarse, axis=-1) + jnp.sum(exp_near, axis=-1)
        probs_coarse = (exp_coarse / row_total[:, :, None]).astype(jnp.bfloat16)
        probs_near = (exp_near / row_total[:, :, None]).astype(jnp.bfloat16)
        mixed = jnp.einsum(
            "hrk,khd->rhd", probs_coarse, value_coarse, preferred_element_type=jnp.float32
        )
        mixed = mixed + jnp.einsum(
            "hrk,khd->rhd", probs_near, value_near, preferred_element_type=jnp.float32
        )
        return (mixed, row_peak, row_total)

    mixed_groups, peak_groups, total_groups = lax.map(
        forward_group,
        (query_groups, coarse_keys, coarse_values, near_keys, near_values, bias_groups),
    )
    keep_row = own_valid > 0
    attended = jnp.where(keep_row[:, None], merge_heads(mixed_groups), 0.0).astype(jnp.bfloat16)[
        None
    ]
    grad_in = jnp.where(keep_row[:, None], grad_out[0], jnp.zeros_like(grad_out[0]))
    grad_groups = split_heads(grad_in, group_count)
    delta_groups = jnp.sum(grad_groups.astype(jnp.float32) * mixed_groups, axis=-1).transpose(
        0, 2, 1
    )

    def backward_group(inputs):
        (
            query_block,
            key_coarse,
            value_coarse,
            key_near,
            value_near,
            bias_block,
            grad_block,
            delta_row,
            row_peak,
            row_total,
        ) = inputs
        scores_coarse = attention_scores(
            query_block,
            key_coarse,
            bias_block,
            onehot_own,
            onehot_coarse,
            allowed_coarse,
            inv_scale,
        )
        scores_near = attention_scores(
            query_block, key_near, bias_block, onehot_own, onehot_near, allowed_near, inv_scale
        )
        probs_coarse = jnp.exp(scores_coarse - row_peak[:, :, None]) / row_total[:, :, None]
        probs_near = jnp.exp(scores_near - row_peak[:, :, None]) / row_total[:, :, None]
        grad_pc = jnp.einsum(
            "rhd,khd->hrk", grad_block, value_coarse, preferred_element_type=jnp.float32
        )
        grad_pn = jnp.einsum(
            "rhd,khd->hrk", grad_block, value_near, preferred_element_type=jnp.float32
        )
        grad_sc = probs_coarse * (grad_pc - delta_row[:, :, None])
        grad_sn = probs_near * (grad_pn - delta_row[:, :, None])
        by_level = jnp.einsum("hrk,kb->hrb", grad_sc, onehot_coarse, precision=highest)
        by_level = by_level + jnp.einsum("hrk,kb->hrb", grad_sn, onehot_near, precision=highest)
        bias_term = jnp.einsum("rs,hrb->hsb", onehot_own, by_level, precision=highest)
        scores_cb = grad_sc.astype(jnp.bfloat16)
        scores_nb = grad_sn.astype(jnp.bfloat16)
        probs_cb = probs_coarse.astype(jnp.bfloat16)
        probs_nb = probs_near.astype(jnp.bfloat16)
        grad_q = jnp.einsum(
            "hrk,khd->rhd", scores_cb, key_coarse, preferred_element_type=jnp.float32
        )
        grad_q = (
            (
                grad_q
                + jnp.einsum(
                    "hrk,khd->rhd", scores_nb, key_near, preferred_element_type=jnp.float32
                )
            )
            * inv_scale
        ).astype(jnp.bfloat16)
        near_key_term = (
            jnp.einsum("hrk,rhd->khd", scores_nb, query_block, preferred_element_type=jnp.float32)
            * inv_scale
        )
        near_value_term = jnp.einsum(
            "hrk,rhd->khd", probs_nb, grad_block, preferred_element_type=jnp.float32
        )
        return (grad_q, scores_cb, probs_cb, near_key_term, near_value_term, bias_term)

    results = lax.map(
        backward_group,
        (
            query_groups,
            coarse_keys,
            coarse_values,
            near_keys,
            near_values,
            bias_groups,
            grad_groups,
            delta_groups,
            peak_groups,
            total_groups,
        ),
    )
    coarse_scores_all = results[1].reshape(head_count, row_count, coarse_total)
    coarse_probs_all = results[2].reshape(head_count, row_count, coarse_total)
    query_heads = queries[0].reshape(row_count, head_count, head_size)
    grad_heads = grad_in.reshape(row_count, head_count, head_size)
    key_term = (
        jnp.einsum(
            "hrk,rhd->khd", coarse_scores_all, query_heads, preferred_element_type=jnp.float32
        )
        * inv_scale
    )
    value_term = jnp.einsum(
        "hrk,rhd->khd", coarse_probs_all, grad_heads, preferred_element_type=jnp.float32
    )
    coarse_grad_k, coarse_grad_v = (
        lax.psum_scatter(
            key_term.reshape(coarse_total, feature_width), "tile", scatter_dimension=0, tiled=True
        ),
        lax.psum_scatter(
            value_term.reshape(coarse_total, feature_width), "tile", scatter_dimension=0, tiled=True
        ),
    )
    near_terms = jnp.stack([merge_heads(results[3]), merge_heads(results[4])])
    from_next = shifted(near_terms[:, :fine_count].astype(jnp.bfloat16), "tile", -1).astype(
        jnp.float32
    )
    from_prev = shifted(near_terms[:, 2 * fine_count :].astype(jnp.bfloat16), "tile", 1).astype(
        jnp.float32
    )
    near_total = near_terms[:, fine_count : 2 * fine_count] + from_next + from_prev
    grad_keys = jnp.concatenate([coarse_grad_k, near_total[0]], axis=0).astype(jnp.bfloat16)[None]
    grad_values = jnp.concatenate([coarse_grad_v, near_total[1]], axis=0).astype(jnp.bfloat16)[None]
    grad_queries = merge_heads(results[0])[None]
    grad_bias = lax.psum(
        results[5].reshape(head_count, level_count, level_count), ("batch", "tile")
    )
    return (attended, grad_queries, grad_keys, grad_values, grad_bias)


def solution(mesh):
    return jax.shard_map(
        shards,
        mesh=mesh,
        in_specs=(
            P("batch", "tile", None),
            P("batch", "tile", None),
            P("batch", "tile", None),
            P("batch", "tile", None),
            P("batch", None),
            P(),
            P(),
        ),
        out_specs=(
            P("batch", "tile", None),
            P("batch", "tile", None),
            P("batch", "tile", None),
            P("batch", "tile", None),
            P(),
        ),
        check_vma=False,
    )
```

profile of v0, /device:TPU:1, one launch (start us, length us, event | category | flops | bytes accessed | tf_op | source)
XLA Modules:
  0.0 514.5 jit_solution(1203547039156469669)
XLA Ops:
  13.4 5.1 collective-permute-start.1
  18.5 1.9 collective-permute-start
  22.6 2.0 copy.60
  24.7 5.7 %collective-permute-done.1 = bf16[2,120,2048]{2,1,0:T(8,128)(2,1)S(1)} collective-permute-done((bf16[2,120,2048]{2,1,0:T(8,128)(2,1)}, bf16[2,120,2048]{2,1,0:T(8,128)(2,1)S(1)}, u32[]{:S(2)}, u32[]{:S(2)}) %collective-permute-start.1) | collective-permute-done | bytes 983072 | tf_op jit(solution)/shard_map/ppermute | solution.py:23
  30.3 12.4 %collective-permute-done = bf16[2,120,2048]{2,1,0:T(8,128)(2,1)} collective-permute-done((bf16[2,120,2048]{2,1,0:T(8,128)(2,1)}, bf16[2,120,2048]{2,1,0:T(8,128)(2,1)}, u32[]{:S(2)}, u32[]{:S(2)}) %collective-permute-start) | collective-permute-done | bytes 983072 | tf_op jit(solution)/shard_map/ppermute | solution.py:22
  44.3 2.3 reshape_squeeze.18
  46.6 2.9 copy.58
  50.9 28.8 %all-gather.7.cloned.1.call-done = bf16[1,256,2048]{2,1,0:T(8,128)(2,1)} async-done(((bf16[1,8,2048]{2,1,0:T(8,128)(2,1)}), bf16[1,256,2048]{2,1,0:T(8,128)(2,1)}) %all-gather.7.cloned.1.call-update) | async-done | bytes 1048592 | tf_op jit(solution)/shard_map/all_gather | solution.py:84
  82.6 63.1 %all-gather.5.cloned.1.call-done = bf16[1,256,2048]{2,1,0:T(8,128)(2,1)} async-done(((bf16[1,8,2048]{2,1,0:T(8,128)(2,1)}), bf16[1,256,2048]{2,1,0:T(8,128)(2,1)}) %all-gather.5.cloned.1.call-update) | async-done | bytes 1048592 | tf_op jit(solution)/shard_map/all_gather | solution.py:85
  145.7 2.3 copy.51
  148.0 36.9 %while.38 = (s32[]{:T(128)}, f32[4,128,4,128]{1,3,2,0:T(8,128)}, f32[4,4,128]{2,1,0:T(4,128)}, f32[4,4,128]{2,1,0:T(4,128)}, bf16[4,256,4,128]{1,3,2,0:T(8,128)(...) while((s32[]{:T(128)}, f32[4,128,4,128]{1,3,2,0:T(8,128)}, ...), condition=%wide.region_5.6_spmd.clone.clone, body=%wide.region_0.5_spmd.clone.clone.sunk | while | flops 214800272 | bytes 8935509 | solution.py:125
  155.2 2.1 fusion.226
  164.5 2.0 fusion.226
  173.6 2.0 fusion.226
  182.9 2.0 fusion.226
  184.9 2.8 multiply_reduce_fusion
  187.7 75.9 %while.39 = (s32[]{:T(128)}, bf16[4,128,4,128]{1,3,2,0:T(8,128)(2,1)}, bf16[4,4,128,256]{3,2,1,0:T(8,128)(2,1)}, bf16[4,4,128,256]{3,2,1,0:T(8,128)(2,1)}, f32[4...) while((s32[]{:T(128)}, ...), condition=%wide.region_8.9_spmd.clone.clone, body=%wide.region_7.8_spmd.clone.clone.sunk | while | flops 440809728 | bytes 18192528 | solution.py:202
  195.5 2.0 bitcast_dynamic-update-slice_fusion.5
  198.0 1.9 fusion.254
  201.4 1.9 fusion.257
  204.6 2.1 fusion.259
  214.6 1.9 bitcast_dynamic-update-slice_fusion.5
  217.0 1.9 fusion.254
  220.4 1.9 fusion.257
  223.6 2.1 fusion.259
  233.6 1.9 bitcast_dynamic-update-slice_fusion.5
  236.0 1.9 fusion.254
  239.4 1.9 fusion.257
  242.5 2.1 fusion.259
  252.5 1.9 bitcast_dynamic-update-slice_fusion.5
  255.0 1.9 fusion.254
  258.3 1.9 fusion.257
  261.5 2.1 fusion.259
  263.7 1.8 fusion.139
  265.5 1.8 copy.73
  267.6 1.6 convolution_multiply_fusion.5
  269.2 1.9 copy.69
  271.2 4.2 copy.70
  275.4 3.2 stack_reshape.6
  278.6 4.2 copy.71
  282.8 4.8 stack_reshape.7
  290.2 2.1 copy-done
  293.6 2.2 collective-permute-start.2
  295.8 3.4 collective-permute-start.3
  299.4 2.0 copy.77
  301.5 92.3 %psum.7 = f32[16,13,13]{2,0,1:T(8,128)} all-reduce(f32[16,13,13]{2,0,1:T(8,128)} %bitcast.307), channel_id=1, replica_groups=mesh['batch'=8,'tile'=32] {'batch','tile'}, use_global_device_ids=true, to_apply=%region_11.12 | all-reduce | flops 2704 | bytes 21632 | tf_op jit(solution)/shard_map/psum | solution.py:249
  394.7 2.0 fusion.138
  398.5 107.9 %reduce-scatter.3.cloned.1.call-done = f32[8,2048]{1,0:T(8,128)} async-done(((f32[256,2048]{1,0:T(8,128)}), f32[8,2048]{1,0:T(8,128)}) %reduce-scatter.3.cloned.1.call-update) | async-done | bytes 65552 | tf_op jit(solution)/shard_map/reduce_scatter | solution.py:231
  (199 shorter events, 95.3 us)
Async XLA Ops:
  7.2 13.4 %copy-start.10 = (s32[4096]{0:T(1024)S(1)}, s32[4096]{0:T(1024)}, u32[]{:S(2)}) copy-start(s32[4096]{0:T(1024)} %param.16) | copy-start | bytes 49156
  7.2 13.6 %copy-start.9 = (s32[1,4096]{1,0:T(1,128)S(1)}, s32[1,4096]{1,0:T(1,128)}, u32[]{:S(2)}) copy-start(s32[1,4096]{1,0:T(1,128)} %param.15) | copy-start | bytes 49156
  7.2 14.0 %copy-start.8 = (f32[16,13,13]{2,0,1:T(8,128)S(1)}, f32[16,13,13]{2,0,1:T(8,128)}, u32[]{:S(2)}) copy-start(f32[16,13,13]{2,0,1:T(8,128)} %param.17) | copy-start | bytes 32452
  7.2 14.8 %copy-start.7 = (bf16[1,128,2048]{2,1,0:T(8,128)(2,1)S(1)}, bf16[1,128,2048]{2,1,0:T(8,128)(2,1)}, u32[]{:S(2)}) copy-start(bf16[1,128,2048]{2,1,0:T(8,128)(2,1)} %param.11) | copy-start | bytes 1572868
  7.2 72.5 %all-gather.7.cloned.1.call-start = ((), (), s32[]{:S(2)}) async-start(), calls=%async_computation.5 | async-start | bytes 1081344 | tf_op jit(solution)/shard_map/all_gather | solution.py:84
  8.7 137.0 %all-gather.5.cloned.1.call-start = ((), (), s32[]{:S(2)}) async-start(), calls=%async_computation.4 | async-start | bytes 1081344 | tf_op jit(solution)/shard_map/all_gather | solution.py:85
  10.2 386.6 %reduce-scatter.5.cloned.1.call-start = ((), (), s32[]{:S(2)}) async-start(), calls=%async_computation.3 | async-start | bytes 2162688 | tf_op jit(solution)/shard_map/reduce_scatter | solution.py:234
  13.4 16.9 %collective-permute-start.1 = (bf16[2,120,2048]{2,1,0:T(8,128)(2,1)}, bf16[2,120,2048]{2,1,0:T(8,128)(2,1)S(1)}, u32[]{:S(2)}, u32[]{:S(2)}) collective-permute-start(bf16[2,120,2048]{2,1,0:T(8,128)(2,1)} %pad_maximum_fusion.1), channel_id=1, source_target_pairs={{1,0},{2,1},{3,2},{4,3},{5,4},{6,5},{7,6},{8,7},{9,8},{10,9},{11,1... | collective-permute-start | bytes 2949128 | tf_op jit(solution)/shard_map/ppermute | solution.py:23
  18.5 24.2 %collective-permute-start = (bf16[2,120,2048]{2,1,0:T(8,128)(2,1)}, bf16[2,120,2048]{2,1,0:T(8,128)(2,1)}, u32[]{:S(2)}, u32[]{:S(2)}) collective-permute-start(bf16[2,120,2048]{2,1,0:T(8,128)(2,1)} %pad_maximum_fusion.1), channel_id=1, source_target_pairs={{0,1},{1,2},{2,3},{3,4},{4,5},{5,6},{6,7},{7,8},{8,9},{9,10},{10,1... | collective-permute-start | bytes 2949128 | tf_op jit(solution)/shard_map/ppermute | solution.py:22
  22.3 20.5 %copy-start.3 = (bf16[1,128,2048]{1,2,0:T(8,128)(2,1)}, bf16[1,128,2048]{1,2,0:T(8,128)(2,1)S(1)}, u32[]{:S(2)}) copy-start(bf16[1,128,2048]{1,2,0:T(8,128)(2,1)S(1)} %copy.52) | copy-start | bytes 1572868
  24.6 160.3 %copy-start.11 = (pred[128]{0:T(512)(128)(4,1)}, pred[128]{0:T(512)(128)(4,1)S(1)}, u32[]{:S(2)}) copy-start(pred[128]{0:T(512)(128)(4,1)S(1)} %compare_bitcast_fusion) | copy-start | bytes 388
  148.0 36.9 %copy-start.5 = (bf16[1,128,2048]{1,2,0:T(8,128)(2,1)S(1)}, bf16[1,128,2048]{1,2,0:T(8,128)(2,1)}, u32[]{:S(2)}) copy-start(bf16[1,128,2048]{1,2,0:T(8,128)(2,1)} %copy.60) | copy-start | bytes 1572868
  187.7 5.0 copy-start.1
  206.7 5.1 copy-start.1
  225.7 5.1 copy-start.1
  244.6 5.1 copy-start.1
  265.5 2.1 copy-start.4
  267.3 239.0 %reduce-scatter.3.cloned.1.call-start = ((), (), s32[]{:S(2)}) async-start(), calls=%async_computation.2 | async-start | bytes 2162688 | tf_op jit(solution)/shard_map/reduce_scatter | solution.py:231
  287.5 1.8 copy-start.2
  289.7 2.5 copy-start
  292.2 7.0 %copy-start.6 = (f32[4,128,4,128]{1,3,2,0:T(8,128)S(1)}, f32[4,128,4,128]{1,3,2,0:T(8,128)}, u32[]{:S(2)}) copy-start(f32[4,128,4,128]{1,3,2,0:T(8,128)} %get-tuple-element.201) | copy-start | bytes 3145732
  292.2 101.5 %copy-start.12 = (pred[128]{0:T(512)(128)(4,1)S(1)}, pred[128]{0:T(512)(128)(4,1)}, u32[]{:S(2)}) copy-start(pred[128]{0:T(512)(128)(4,1)} %copy-done.11) | copy-start | bytes 388
  293.6 101.1 %collective-permute-start.2 = (bf16[2,120,2048]{2,1,0:T(8,128)(2,1)}, bf16[2,120,2048]{2,1,0:T(8,128)(2,1)S(1)}, u32[]{:S(2)}, u32[]{:S(2)}) collective-permute-start(bf16[2,120,2048]{2,1,0:T(8,128)(2,1)} %get-tuple-element.605), channel_id=1, source_target_pairs={{1,0},{2,1},{3,2},{4,3},{5,4},{6,5},{7,6},{8,7},{9,8},{10,9},{11,1... | collective-permute-start | bytes 2949128 | tf_op jit(solution)/shard_map/ppermute | solution.py:31
  295.8 98.9 %collective-permute-start.3 = (bf16[2,120,2048]{2,1,0:T(8,128)(2,1)}, bf16[2,120,2048]{2,1,0:T(8,128)(2,1)S(1)}, u32[]{:S(2)}, u32[]{:S(2)}) collective-permute-start(bf16[2,120,2048]{2,1,0:T(8,128)(2,1)} %get-tuple-element.606), channel_id=1, source_target_pairs={{0,1},{1,2},{2,3},{3,4},{4,5},{5,6},{6,7},{7,8},{8,9},{9,10},{10,1... | collective-permute-start | bytes 2949128 | tf_op jit(solution)/shard_map/ppermute | solution.py:31
Sparse Core Ops, SparseCore 0:
  9.9 69.7 all-gather.6
  82.1 63.5 all-gather.4
  267.5 120.0 reduce-scatter.4
  390.1 116.1 reduce-scatter.2
where the time goes:
time: 520 us; the launch traced here: 515 us
  waiting for transfers between devices  218 us (42%)
  matrix products  99.2 us (19%)
  blocking collectives  92.3 us (18%)
  local copies, waits for them, and re-layouts  57.5 us (11%)
  other arithmetic  20.1 us (4%)
  between operations  14.1 us (3%)
  starting transfers between devices  12.9 us (2%)
    reduce_scatter x1, waiting for transfers between devices, shards(): lax.psum_scatter(key_term.reshape(coarse_total, feature_width), 'tile', s...  108 us
    psum x1, blocking collectives, shards(): lax.psum(results[5].reshape(head_count, level_count, level_count), ('batc...  92.3 us
    all_gather x1, waiting for transfers between devices, shards(): lax.all_gather(values[0, :coarse_count], 'tile', axis=0, tiled=True)  63.1 us
    all_gather x1, waiting for transfers between devices, shards(): lax.all_gather(keys[0, :coarse_count], 'tile', axis=0, tiled=True)  28.8 us
    dot_general x16, matrix products, attention_scores(): jnp.einsum('hrb,kb->hrk', row_bias, onehot_cols, precision=lax.Precision....  15.6 us
    ppermute x1, waiting for transfers between devices, with_halo(): before = lax.ppermute(last, axis, up)  12.4 us
    dot_general x16, matrix products, attention_scores(): jnp.einsum('rhd,khd->hrk', query_block, key_block, preferred_element_type...  12.3 us
    unnamed x32, local copies, waits for them, and re-layouts  12 us
  transfers between devices with their start and end apart: 8, of which 5 were waited for; matrix products, arithmetic and copies ran while one was open for 9% of the time, Pallas kernels for 0%

commit v1 on v0

v1 whole, which is shorter than its diff:
```python
import functools
import math

import jax
import jax.numpy as jnp
from jax import lax
from jax.experimental import pallas as pl
from jax.experimental.pallas import tpu as pltpu
from jax.sharding import PartitionSpec as P

COARSE = 8
MASKED = -1e30
LANES = 128
SLOT = 16
BF16 = jnp.bfloat16
F32 = jnp.float32
OFFSETS = (0, 1, 2, 3, 4, -3, -2, -1)


def mm(a, b, contract):
    return lax.dot_general(a, b, (contract, ((), ())), preferred_element_type=F32)


ROW_COL = ((1,), (0,))
ROW_ROW = ((1,), (1,))
COL_COL = ((0,), (0,))


def attention_kernel(inv_scale, half_ref, *refs):
    (q_ref, k_ref, v_ref, g_ref, kv_par, qg_par, kv_own_out, kv_par_out) = refs[:8]
    coarse_refs = refs[8:16]
    row_hot_ref, key_hot_ref, table_ref, keep_ref = refs[16:20]
    own_ref, par_ref, own_out_ref, par_out_ref = refs[20:24]
    coarse_out = refs[24:32]
    bias_ref = refs[32]
    step = pl.program_id(0)
    rows = q_ref.shape[0]
    part = coarse_refs[0].shape[0] // 2
    total = part * len(coarse_refs)
    keep = keep_ref[...] > 0.0
    q = jnp.concatenate([q_ref[...], qg_par[:rows]], axis=0)
    g_all = jnp.concatenate([g_ref[...], qg_par[rows:]], axis=0)
    g = jnp.where(keep, g_all.astype(F32), 0.0).astype(BF16)
    row_hot = row_hot_ref[...]
    key_hot = key_hot_ref[...]
    k_main = jnp.concatenate([r[:part] for r in coarse_refs] + [k_ref[...], kv_par[:rows]], axis=0)
    v_main = jnp.concatenate([r[part:] for r in coarse_refs] + [v_ref[...], kv_par[rows:]], axis=0)
    main = k_main.shape[0]
    hot_main = key_hot[:main]
    hot_own = key_hot[main : main + rows]
    hot_par = key_hot[main + rows :]
    row_bias = mm(row_hot, table_ref[0], ROW_COL).astype(BF16)
    q_ext = jnp.concatenate([q, row_bias], axis=1)
    k_main_ext = jnp.concatenate([k_main, hot_main], axis=1)
    k_own_ext = jnp.concatenate([kv_own_out[:rows], hot_own], axis=1)
    k_par_ext = jnp.concatenate([kv_par_out[:rows], hot_par], axis=1)
    v_own = kv_own_out[rows:]
    v_par = kv_par_out[rows:]

    def stacked(a, own, par, contract):
        return jnp.concatenate([mm(a[:rows], own, contract), mm(a[rows:], par, contract)], axis=0)

    s_main = mm(q_ext, k_main_ext, ROW_ROW) * inv_scale
    s_out = stacked(q_ext, k_own_ext, k_par_ext, ROW_ROW) * inv_scale
    peak = jnp.maximum(
        jnp.max(s_main, axis=1, keepdims=True), jnp.max(s_out, axis=1, keepdims=True)
    )
    e_main = jnp.exp(s_main - peak)
    e_out = jnp.exp(s_out - peak)
    norm = 1.0 / (
        jnp.sum(e_main, axis=1, keepdims=True) + jnp.sum(e_out, axis=1, keepdims=True)
    )
    p_main = e_main * norm
    p_out = e_out * norm
    pb_main = p_main.astype(BF16)
    pb_out = p_out.astype(BF16)
    mixed = mm(pb_main, v_main, ROW_COL) + stacked(pb_out, v_own, v_par, ROW_COL)
    attended = jnp.where(keep, mixed, 0.0).astype(BF16)
    delta = jnp.sum(g.astype(F32) * mixed, axis=1, keepdims=True)
    d_main = p_main * (mm(g, v_main, ROW_ROW) - delta)
    d_out = p_out * (stacked(g, v_own, v_par, ROW_ROW) - delta)
    db_main = d_main.astype(BF16)
    db_out = d_out.astype(BF16)
    dl_main = (d_main - db_main.astype(F32)).astype(BF16)
    dl_out = (d_out - db_out.astype(F32)).astype(BF16)
    q_terms = mm(db_main, k_main_ext, ROW_COL) + stacked(db_out, k_own_ext, k_par_ext, ROW_COL)
    grad_q = (q_terms[:, :LANES] * inv_scale).astype(BF16)
    by_level = q_terms[:, LANES:] + (
        mm(dl_main, hot_main, ROW_COL) + stacked(dl_out, hot_own, hot_par, ROW_COL)
    )
    bias = lax.dot_general(
        row_hot.astype(F32),
        by_level,
        (COL_COL, ((), ())),
        precision=lax.Precision.HIGHEST,
        preferred_element_type=F32,
    )
    lane = lax.broadcasted_iota(jnp.int32, bias.shape, 1)
    bias = jnp.where(lane < SLOT, bias, 0.0)
    bias = pltpu.roll(bias, step * SLOT, 1)

    @pl.when(step == 0)
    def _():
        bias_ref[...] = bias

    @pl.when(step > 0)
    def _():
        bias_ref[...] = bias_ref[...] + bias

    gk_main = (mm(db_main, q, COL_COL) * inv_scale).astype(BF16)
    gv_main = mm(pb_main, g, COL_COL).astype(BF16)
    gk_own = (mm(db_out[:rows], q[:rows], COL_COL) * inv_scale).astype(BF16)
    gk_par = (mm(db_out[rows:], q[rows:], COL_COL) * inv_scale).astype(BF16)
    gv_own = mm(pb_out[:rows], g[:rows], COL_COL).astype(BF16)
    gv_par = mm(pb_out[rows:], g[rows:], COL_COL).astype(BF16)
    for place, ref in ((0, own_ref), (1, par_ref)):
        here = slice(place * rows, (place + 1) * rows)
        there = slice(total + place * rows, total + (place + 1) * rows)
        ref[0 * rows : 1 * rows] = attended[here]
        ref[1 * rows : 2 * rows] = grad_q[here]
        ref[2 * rows : 3 * rows] = gk_main[there]
        ref[3 * rows : 4 * rows] = gv_main[there]
    own_out_ref[:rows] = gk_own
    own_out_ref[rows:] = gv_own
    par_out_ref[:rows] = gk_par
    par_out_ref[rows:] = gv_par
    for j, ref in enumerate(coarse_out):
        ref[:part] = gk_main[j * part : (j + 1) * part]
        ref[part:] = gv_main[j * part : (j + 1) * part]


def call_kernel(inv_scale, half, full, pairs, coarse, tables, heads):
    rows, width = full[0].shape
    half_width = width // 2
    steps = heads // 2
    part2 = coarse[0].shape[0]
    row_hot, key_hot, table, keep = tables

    def mine(h, half_ref):
        return (0, half_ref[0] * steps + h)

    def at(h, half_ref):
        return (0, h)

    def fixed(h, half_ref):
        return (0, 0)

    in_specs = (
        [pl.BlockSpec((rows, LANES), mine)] * 4
        + [pl.BlockSpec((2 * rows, LANES), at)] * 4
        + [pl.BlockSpec((part2, LANES), at)] * len(coarse)
        + [
            pl.BlockSpec(row_hot.shape, fixed),
            pl.BlockSpec(key_hot.shape, fixed),
            pl.BlockSpec((1, SLOT, LANES), lambda h, half_ref: (half_ref[0] * steps + h, 0, 0)),
            pl.BlockSpec(keep.shape, fixed),
        ]
    )
    out_rows = [4 * rows] * 2 + [2 * rows] * 2 + [part2] * len(coarse)
    out_shape = [jax.ShapeDtypeStruct((r, half_width), BF16) for r in out_rows]
    out_shape.append(jax.ShapeDtypeStruct((SLOT, LANES), F32))
    out_specs = [pl.BlockSpec((r, LANES), at) for r in out_rows]
    out_specs.append(pl.BlockSpec((SLOT, LANES), fixed))
    return pl.pallas_call(
        functools.partial(attention_kernel, inv_scale),
        grid_spec=pltpu.PrefetchScalarGridSpec(
            num_scalar_prefetch=1, grid=(steps,), in_specs=in_specs, out_specs=out_specs
        ),
        out_shape=out_shape,
        compiler_params=pltpu.CompilerParams(
            dimension_semantics=("arbitrary",), vmem_limit_bytes=48 * 1024 * 1024
        ),
        cost_estimate=pl.CostEstimate(
            flops=12 * 2 * rows * 640 * half_width,
            bytes_accessed=10 * 1024 * 1024,
            transcendentals=steps * 2 * rows * 640,
        ),
    )(half, *full, *pairs, *coarse, row_hot, key_hot, table, keep)


def shards(queries, keys, values, grad_out, valid, scale_ids, scale_bias):
    q, k, v, g = queries[0], keys[0], values[0], grad_out[0]
    rows, width = q.shape
    half_width = width // 2
    heads, levels = scale_bias.shape[:2]
    tiles = lax.axis_size("tile")
    depth = tiles // 4
    images = lax.axis_size("batch")
    tile = lax.axis_index("tile")
    core = tile % 2
    inv_scale = 1.0 / math.sqrt(width // heads)

    def send(x, target):
        return lax.ppermute(x, "tile", [(i, target(i)) for i in range(tiles)])

    def to_core(x):
        return send(x, lambda i: i ^ 1)

    def to_side(x):
        return send(x, lambda i: i ^ 2)

    def to_depth(x, distance):
        return send(x, lambda i: (i + 4 * distance) % tiles)

    edge = []
    jump = []
    for i in range(tiles):
        near = i + 1 if i % 2 else i - 1
        far = i + 2 if i % 2 else i - 2
        if 0 <= near < tiles:
            edge.append((i, near))
        if 0 <= far < tiles:
            jump.append((i, far))

    def cut(x, which):
        return lax.dynamic_slice_in_dim(x, which * half_width, half_width, 1)

    small = jnp.stack([k[:COARSE], v[:COARSE]])
    small_mine = lax.dynamic_slice_in_dim(small, core * half_width, half_width, 2)
    small_other = lax.dynamic_slice_in_dim(small, (1 - core) * half_width, half_width, 2)
    chip = jnp.concatenate([small_mine, to_core(small_other)], axis=1).reshape(-1, half_width)
    side = to_side(chip)
    group = jnp.concatenate(
        [x[a : a + 2 * COARSE] for a in (0, 2 * COARSE) for x in (chip, side)], axis=0
    )
    blocks = {0: group}
    for d in (1, -1, 2, -2):
        blocks[d] = to_depth(group, -d)
    blocks[3] = to_depth(blocks[2], -1)
    blocks[-3] = to_depth(blocks[-2], 1)
    blocks[4] = send(
        jnp.where(core == 0, blocks[2], blocks[-2]),
        lambda i: (i + (8 if i % 2 else -8)) % tiles,
    )
    coarse = [blocks[d] for d in OFFSETS]

    kv_other = jnp.concatenate([cut(k, 1 - core), cut(v, 1 - core)], axis=0)
    kv_mine = jnp.concatenate([cut(k, core), cut(v, core)], axis=0)
    qg_other = jnp.concatenate([cut(q, 1 - core), cut(g, 1 - core)], axis=0)
    kv_own_out = lax.ppermute(kv_other, "tile", edge)
    kv_par_out = lax.ppermute(kv_mine, "tile", jump)
    kv_par = to_core(kv_other)
    qg_par = to_core(qg_other)

    valid_grid = valid[0].reshape(tiles, rows)
    scale_grid = scale_ids.reshape(tiles, rows)
    level_grid = jnp.where(valid_grid > 0, scale_grid, levels)
    inner = jnp.arange(rows, dtype=jnp.int32)
    fine_grid = jnp.where(inner[None, :] >= COARSE, level_grid, levels)
    near_grid = jnp.pad(fine_grid, ((1, 1), (0, 0)), constant_values=levels)
    partner = tile ^ 1
    outward = 2 * core - 1

    def line(grid, index):
        return lax.dynamic_index_in_dim(grid, index, 0, keepdims=False)

    z_here = tile // 4
    spots = jnp.stack([((z_here + d) % depth) * 4 + (j ^ (tile % 4)) for d in OFFSETS for j in range(4)])
    pick = (spots[:, None] == jnp.arange(tiles, dtype=jnp.int32)[None, :]).astype(F32)
    coarse_level = jnp.dot(
        pick, level_grid[:, :COARSE].astype(F32), precision=lax.Precision.HIGHEST
    ).astype(jnp.int32)
    key_level = jnp.concatenate(
        [
            coarse_level.reshape(-1),
            line(near_grid, tile + 1),
            line(near_grid, partner + 1),
            line(near_grid, tile + 1 + outward),
            line(near_grid, partner + 1 - outward),
        ]
    )
    column = jnp.arange(LANES, dtype=jnp.int32)
    key_hot = (
        (key_level[:, None] == (column % SLOT)[None, :]) & (column < 3 * SLOT)[None, :]
    ).astype(BF16)
    row_level = jnp.concatenate([line(scale_grid, tile), line(scale_grid, partner)])
    row_hot = (row_level[:, None] == jnp.arange(SLOT, dtype=jnp.int32)[None, :]).astype(BF16)
    keep = jnp.concatenate([line(valid_grid, tile), line(valid_grid, partner)]).astype(F32)[:, None]

    level_ids = jnp.arange(levels, dtype=jnp.int32)
    scaled = jnp.where(
        (level_ids[None, :] <= level_ids[:, None])[None], scale_bias / inv_scale, MASKED
    )
    scaled = jnp.pad(
        scaled,
        ((0, 0), (0, SLOT - levels), (0, SLOT - levels)),
        constant_values=MASKED,
    )
    parts = []
    rest = scaled
    for _ in range(3):
        piece = lax.reduce_precision(rest, 8, 7)
        parts.append(piece)
        rest = rest - piece
    table = jnp.pad(
        jnp.concatenate(parts, axis=2), ((0, 0), (0, 0), (0, LANES - 3 * SLOT))
    ).astype(BF16)

    results = call_kernel(
        inv_scale,
        core.reshape(1),
        (q, k, v, g),
        (kv_par, qg_par, kv_own_out, kv_par_out),
        coarse,
        (row_hot, key_hot, table, keep),
        heads,
    )
    own, par, own_out, par_out = results[:4]
    terms = dict(zip(OFFSETS, results[4:12]))
    bias = results[12]

    from_below = to_depth(terms[3], 1)
    from_above = to_depth(terms[-3], -1)
    across = send(terms[4], lambda i: (i + (-8 if i % 2 else 8)) % tiles)
    one_up = to_depth(terms[1], 1)
    one_down = to_depth(terms[-1], -1)

    def wide(x):
        return x.astype(F32)

    zero = jnp.zeros((), F32)
    two_up = wide(terms[2]) + wide(from_below) + jnp.where(core == 0, wide(across), zero)
    two_down = wide(terms[-2]) + wide(from_above) + jnp.where(core == 1, wide(across), zero)
    two_up = to_depth(two_up.astype(BF16), 2)
    two_down = to_depth(two_down.astype(BF16), -2)
    summed = wide(terms[0]) + wide(one_up) + wide(one_down) + wide(two_up) + wide(two_down)
    summed = summed.reshape(2, 2, 2 * COARSE, half_width)
    coarse_chip = summed[:, 0] + wide(to_side(summed[:, 1].astype(BF16)))
    coarse_mine = coarse_chip[:, :COARSE]
    coarse_other = wide(to_core(coarse_chip[:, COARSE:].astype(BF16)))

    back_other = lax.ppermute(own_out, "tile", edge)
    back_mine = lax.ppermute(par_out, "tile", [(b, a) for a, b in jump])
    other = to_core(par)

    both = ("batch", "tile")

    def everywhere(x, target):
        pairs = []
        for b in range(images):
            for i in range(tiles):
                b2, i2 = target(b, i)
                pairs.append((b * tiles + i, b2 * tiles + i2))
        return lax.ppermute(x, both, pairs)

    for shifts in ((2, 4, 6), (1,)):
        got = []
        for s in shifts:
            got.append(to_depth(bias, s))
        if len(shifts) == 1:
            got = [send(bias, lambda i: i ^ 2)]
            got.append(send(bias, lambda i: (i + 4) % tiles if (i // 4) % 2 == 0 else i - 4))
            got.append(send(bias, lambda i: ((i + 4) if (i // 4) % 2 == 0 else (i - 4)) ^ 2))
        for x in got:
            bias = bias + x
    x_count = images // 2
    got = [
        everywhere(bias, lambda b, i, s=s: ((b // x_count) * x_count + (b + s) % x_count, i))
        for s in range(1, x_count)
    ]
    for x in got:
        bias = bias + x
    same = everywhere(bias, lambda b, i: ((b + x_count) % images, i))
    swap = everywhere(bias, lambda b, i: (b, i ^ 1))
    cross = everywhere(bias, lambda b, i: ((b + x_count) % images, i ^ 1))
    mine_bias = bias + same
    other_bias = swap + cross
    bias_halves = jnp.where(
        core == 0, jnp.stack([mine_bias, other_bias]), jnp.stack([other_bias, mine_bias])
    )
    grad_bias = (
        bias_halves.reshape(2, SLOT, heads // 2, SLOT)
        .transpose(0, 2, 1, 3)
        .reshape(heads, SLOT, SLOT)[:, :levels, :levels]
    )

    def joined(mine, other_half):
        return jnp.where(
            core == 0,
            jnp.concatenate([mine, other_half], axis=-1),
            jnp.concatenate([other_half, mine], axis=-1),
        )

    attended = joined(own[:rows], other[:rows])
    grad_q = joined(own[rows : 2 * rows], other[rows : 2 * rows])
    fine_mine = wide(own[2 * rows :]) + wide(back_mine)
    fine_other = wide(other[2 * rows :]) + wide(back_other)
    fine = joined(fine_mine, fine_other).reshape(2, rows, width)
    coarse_rows = joined(coarse_mine, coarse_other)
    grads = jnp.concatenate([coarse_rows, fine[:, COARSE:]], axis=1).astype(BF16)
    return (attended[None], grad_q[None], grads[0][None], grads[1][None], grad_bias)


def solution(mesh):
    block = P("batch", "tile", None)
    return jax.shard_map(
        shards,
        mesh=mesh,
        in_specs=(block, block, block, block, P("batch", None), P(), P()),
        out_specs=(block, block, block, block, P()),
        check_vma=False,
    )
```

time: 520 us -> 165 us (0.32)
  waiting for transfers between devices: 218 us -> 47.6 us
  matrix products: 99.2 us -> 0.2 us
  blocking collectives: 92.3 us -> 0 us
  starting transfers between devices: 12.9 us -> 71.5 us
  local copies, waits for them, and re-layouts: 57.5 us -> 12.2 us
  Pallas kernels: 0 us -> 17.7 us
  between operations: 14.1 us -> 1.28 us
  other arithmetic: 20.1 us -> 12.9 us
    reduce_scatter x2 -> x0, waiting for transfers between devices: 108 us -> none  [the longest x1 108 us: shards(): lax.psum_scatter(key_term.reshape(coarse_total, feature_width), 'tile', s...]
    dot_general x86 -> x1, matrix products: 99.2 us -> 0.2 us  [shards(): jnp.dot(pick, level_grid[:, :COARSE].astype(F32), precision=lax.Precision...]
    psum x1 -> x0, blocking collectives: 92.3 us -> none  [shards(): lax.psum(results[5].reshape(head_count, level_count, level_count), ('batc...]
    all_gather x2 -> x0, waiting for transfers between devices: 91.9 us -> none  [the longest x1 63.1 us: shards(): lax.all_gather(values[0, :coarse_count], 'tile', axis=0, tiled=True)]
    ppermute x4 -> x37, starting transfers between devices: 12.6 us -> 71.5 us  [the longest x27 39.8 us: send(): return lax.ppermute(x, 'tile', [(i, target(i)) for i in range(tiles)])]
    ppermute x4 -> x37, waiting for transfers between devices: 18.1 us -> 47.6 us  [the longest x27 39.4 us: send(): return lax.ppermute(x, 'tile', [(i, target(i)) for i in range(tiles)])]
    pallas_call x0 -> x1, Pallas kernels: none -> 17.7 us  [call_kernel(): pl.pallas_call(functools.partial(attention_kernel, inv_scale), grid_spec=...]
    another operation x6 -> x3, local copies, waits for them, and re-layouts: 13.6 us -> 0.27 us  [the longest x2 0.15 us: shards(): jnp.stack([mine_bias, other_bias])]
  transfers between devices with their start and end apart: 8 -> 37, of which waited for: 5 -> 10; matrix products, arithmetic and copies ran while one was open for 9% -> 6% of each run, Pallas kernels for 0% -> 0%
where the time goes in v1:
time: 165 us; the launch traced here: 163 us
  starting transfers between devices  71.5 us (43%)
  waiting for transfers between devices  47.6 us (29%)
  Pallas kernels  17.7 us (11%)
  other arithmetic  12.9 us (8%)
  local copies, waits for them, and re-layouts  12.2 us (7%)
    ppermute x27, starting transfers between devices, send(): return lax.ppermute(x, 'tile', [(i, target(i)) for i in range(tiles)])  39.8 us
    ppermute x27, waiting for transfers between devices, send(): return lax.ppermute(x, 'tile', [(i, target(i)) for i in range(tiles)])  39.4 us
    ppermute x6, starting transfers between devices, everywhere(): return lax.ppermute(x, both, pairs)  21.5 us
    pallas_call x1, Pallas kernels, call_kernel(): pl.pallas_call(functools.partial(attention_kernel, inv_scale), grid_spec=...  17.7 us
    unnamed x56, local copies, waits for them, and re-layouts  8.84 us
    ppermute x1, waiting for transfers between devices, shards(): back_other = lax.ppermute(own_out, 'tile', edge)  8.16 us
    ppermute x1, starting transfers between devices, shards(): kv_par_out = lax.ppermute(kv_mine, 'tile', jump)  4.67 us
  transfers between devices with their start and end apart: 37, of which 10 were waited for; matrix products, arithmetic and copies ran while one was open for 6% of the time, Pallas kernels for 0%

profile of v1, /device:TPU:1, one launch (start us, length us, event | category | flops | bytes accessed | tf_op | source)
XLA Modules:
  0.0 163.5 jit_solution(1779686587271797002)
XLA Ops:
  0.7 1.3 dynamic-slice_bitcast_fusion
  2.0 0.8 pad_maximum_fusion.3
  2.8 3.3 %collective-permute-start = (bf16[256,1024]{1,0:T(8,128)(2,1)}, bf16[256,1024]{1,0:T(8,128)(2,1)}, u32[]{:S(2)}, u32[]{:S(2)}) collective-permute-start(bf16[256,1024]{1,0:T(8,128)(2,1)} %pad_maximum_fusion.3), channel_id=1, source_target_pairs={{0,1},{1,0},{2,3},{3,2},{4,5},{5,4},{6,7},{7,6},{8,9},{9,8},{10,11... | collective-permute-start | bytes 1572872 | tf_op jit(solution)/shard_map/ppermute | solution.py:194
  6.1 1.9 %collective-permute-start.2 = (bf16[256,1024]{1,0:T(8,128)(2,1)}, bf16[256,1024]{1,0:T(8,128)(2,1)}, u32[]{:S(2)}, u32[]{:S(2)}) collective-permute-start(bf16[256,1024]{1,0:T(8,128)(2,1)} %pad_maximum_fusion.3), channel_id=1, source_target_pairs={{1,2},{2,1},{3,4},{4,3},{5,6},{6,5},{7,8},{8,7},{9,10},{10,9},{11,... | collective-permute-start | bytes 1572872 | tf_op jit(solution)/shard_map/ppermute | solution.py:240
  8.2 0.8 pad_maximum_fusion.5
  9.0 4.7 %collective-permute-start.3 = (bf16[256,1024]{1,0:T(8,128)(2,1)}, bf16[256,1024]{1,0:T(8,128)(2,1)}, u32[]{:S(2)}, u32[]{:S(2)}) collective-permute-start(bf16[256,1024]{1,0:T(8,128)(2,1)} %pad_maximum_fusion.5), channel_id=1, source_target_pairs={{1,3},{2,0},{3,5},{4,2},{5,7},{6,4},{7,9},{8,6},{9,11},{10,8},{11,... | collective-permute-start | bytes 1572872 | tf_op jit(solution)/shard_map/ppermute | solution.py:241
  15.5 17.1 %collective-permute-done.5 = bf16[32,1024]{1,0:T(8,128)(2,1)S(1)} collective-permute-done((bf16[32,1024]{1,0:T(8,128)(2,1)S(1)}, bf16[32,1024]{1,0:T(8,128)(2,1)S(1)}, u32[]{:S(2)}, u32[]{:S(2)}) %collective-permute-start.5) | collective-permute-done | bytes 65568 | tf_op jit(solution)/shard_map/ppermute | solution.py:194
  32.6 5.7 %collective-permute-start.7 = (bf16[64,1024]{1,0:T(8,128)(2,1)S(1)}, bf16[64,1024]{1,0:T(8,128)(2,1)S(1)}, u32[]{:S(2)}, u32[]{:S(2)}) collective-permute-start(bf16[64,1024]{1,0:T(8,128)(2,1)S(1)} %pad_maximum_fusion.6.refs_8_), channel_id=1, source_target_pairs={{0,24},{1,25},{2,26},{3,27},{4,28},{5,29},{6,30},{7,31},{8,0},{9,1... | collective-permute-start | bytes 393224 | tf_op jit(solution)/shard_map/ppermute | solution.py:194
  38.4 0.8 pad_maximum_fusion.4
  39.2 1.1 collective-permute-done.7.refs_10_
  40.3 6.1 %collective-permute-done.9.refs_14_ = bf16[64,1024]{1,0:T(8,128)(2,1)S(1)} collective-permute-done((bf16[64,1024]{1,0:T(8,128)(2,1)S(1)}, bf16[64,1024]{1,0:T(8,128)(2,1)S(1)}, u32[]{:S(2)}, u32[]{:S(2)}) %collective-permute-start.9) | collective-permute-done | bytes 131104 | tf_op jit(solution)/shard_map/ppermute | solution.py:194
  46.4 1.2 collective-permute-done.12.refs_15_
  47.6 3.4 %collective-permute-start.1 = (bf16[256,1024]{1,0:T(8,128)(2,1)}, bf16[256,1024]{1,0:T(8,128)(2,1)}, u32[]{:S(2)}, u32[]{:S(2)}) collective-permute-start(bf16[256,1024]{1,0:T(8,128)(2,1)} %pad_maximum_fusion.4), channel_id=1, source_target_pairs={{0,1},{1,0},{2,3},{3,2},{4,5},{5,4},{6,7},{7,6},{8,9},{9,8},{10,11... | collective-permute-start | bytes 1572872 | tf_op jit(solution)/shard_map/ppermute | solution.py:194
  51.8 6.2 %collective-permute-done.10.refs_12_ = bf16[64,1024]{1,0:T(8,128)(2,1)S(1)} collective-permute-done((bf16[64,1024]{1,0:T(8,128)(2,1)S(1)}, bf16[64,1024]{1,0:T(8,128)(2,1)S(1)}, u32[]{:S(2)}, u32[]{:S(2)}) %collective-permute-start.10) | collective-permute-done | bytes 131104 | tf_op jit(solution)/shard_map/ppermute | solution.py:194
  58.0 1.6 reduce-precision_convert_fusion.1
  59.7 3.4 %collective-permute-done.11.refs_13_ = bf16[64,1024]{1,0:T(8,128)(2,1)S(1)} collective-permute-done((bf16[64,1024]{1,0:T(8,128)(2,1)S(1)}, bf16[64,1024]{1,0:T(8,128)(2,1)S(1)}, u32[]{:S(2)}, u32[]{:S(2)}) %collective-permute-start.11) | collective-permute-done | bytes 131104 | tf_op jit(solution)/shard_map/ppermute | solution.py:194
  63.2 1.0 fusion.18.refs_18_
  64.2 3.0 %collective-permute-done.8.refs_11_ = bf16[64,1024]{1,0:T(8,128)(2,1)S(1)} collective-permute-done((bf16[64,1024]{1,0:T(8,128)(2,1)S(1)}, bf16[64,1024]{1,0:T(8,128)(2,1)S(1)}, u32[]{:S(2)}, u32[]{:S(2)}) %collective-permute-start.8) | collective-permute-done | bytes 131104 | tf_op jit(solution)/shard_map/ppermute | solution.py:194
  67.9 0.9 copy-done.11
  68.8 0.9 copy-done.13
  69.7 0.9 copy-done.15
  70.6 0.9 copy-done.17
  71.5 0.9 copy-done.19
  72.4 17.7 %shard_map.110 = (bf16[512,1024]{1,0:T(8,128)(2,1)}, bf16[512,1024]{1,0:T(8,128)(2,1)}, bf16[256,1024]{1,0:T(8,128)(2,1)S(1)}, bf16[256,1024]{1,0:T(8,128)(2,1)S...) custom-call(s32[1]{0:T(128)} %bitcast.half_ref, ...), custom_call_target="tpu_custom_call" | custom-call | flops 2013265920 | bytes 10485760 | tf_op jit(solution)/shard_map/pallas_call | solution.py:164
  90.2 0.8 copy-done.4
  93.7 3.8 %collective-permute-start.26 = (f32[16,128]{1,0:T(8,128)S(1)}, f32[16,128]{1,0:T(8,128)S(1)}, u32[]{:S(2)}, u32[]{:S(2)}) collective-permute-start(f32[16,128]{1,0:T(8,128)S(1)} %get-tuple-element.30), channel_id=1, source_target_pairs={{0,16},{1,17},{2,18},{3,19},{4,20},{5,21},{6,22},{7,23},{8,24},{9,... | collective-permute-start | bytes 24584 | tf_op jit(solution)/shard_map/ppermute | solution.py:194
  97.5 3.6 %collective-permute-start.27 = (f32[16,128]{1,0:T(8,128)S(1)}, f32[16,128]{1,0:T(8,128)S(1)}, u32[]{:S(2)}, u32[]{:S(2)}) collective-permute-start(f32[16,128]{1,0:T(8,128)S(1)} %get-tuple-element.30), channel_id=1, source_target_pairs={{0,24},{1,25},{2,26},{3,27},{4,28},{5,29},{6,30},{7,31},{8,0},{9,1... | collective-permute-start | bytes 24584 | tf_op jit(solution)/shard_map/ppermute | solution.py:194
  101.9 4.3 %collective-permute-start.28 = (f32[16,128]{1,0:T(8,128)S(1)}, f32[16,128]{1,0:T(8,128)S(1)}, u32[]{:S(2)}, u32[]{:S(2)}) collective-permute-start(f32[16,128]{1,0:T(8,128)S(1)} %add_add_fusion.2), channel_id=1, source_target_pairs={{0,2},{1,3},{2,0},{3,1},{4,6},{5,7},{6,4},{7,5},{8,10},{9,11},{10,... | collective-permute-start | bytes 24584 | tf_op jit(solution)/shard_map/ppermute | solution.py:194
  108.0 3.4 %collective-permute-start.17 = (bf16[64,1024]{1,0:T(8,128)(2,1)}, bf16[64,1024]{1,0:T(8,128)(2,1)S(1)}, u32[]{:S(2)}, u32[]{:S(2)}) collective-permute-start(bf16[64,1024]{1,0:T(8,128)(2,1)} %copy-done.8), channel_id=1, source_target_pairs={{0,8},{1,25},{2,10},{3,27},{4,12},{5,29},{6,14},{7,31},{8,16},{9,1... | collective-permute-start | bytes 393224 | tf_op jit(solution)/shard_map/ppermute | solution.py:194
  111.5 1.3 collective-permute-start.19
  112.9 2.5 %collective-permute-start.15 = (bf16[64,1024]{1,0:T(8,128)(2,1)S(1)}, bf16[64,1024]{1,0:T(8,128)(2,1)S(1)}, u32[]{:S(2)}, u32[]{:S(2)}) collective-permute-start(bf16[64,1024]{1,0:T(8,128)(2,1)S(1)} %get-tuple-element.22), channel_id=1, source_target_pairs={{0,28},{1,29},{2,30},{3,31},{4,0},{5,1},{6,2},{7,3},{8,4},{9,5},{1... | collective-permute-start | bytes 393224 | tf_op jit(solution)/shard_map/ppermute | solution.py:194
  115.4 1.3 collective-permute-start.31
  116.7 2.5 %collective-permute-start.32 = (f32[16,128]{1,0:T(8,128)S(1)}, f32[16,128]{1,0:T(8,128)S(1)}, u32[]{:S(2)}, u32[]{:S(2)}) collective-permute-start(f32[16,128]{1,0:T(8,128)S(1)} %add_add_fusion.1), channel_id=1, source_target_pairs={{0,64},{1,65},{2,66},{3,67},{4,68},{5,69},{6,70},{7,71},{8,72},{9,... | collective-permute-start | bytes 24584 | tf_op jit(solution)/shard_map/ppermute | solution.py:344
  119.2 1.1 collective-permute-start.33
  120.5 1.3 collective-permute-start.23
  121.8 3.0 %collective-permute-start.18 = (bf16[64,1024]{1,0:T(8,128)(2,1)S(1)}, bf16[64,1024]{1,0:T(8,128)(2,1)S(1)}, u32[]{:S(2)}, u32[]{:S(2)}) collective-permute-start(bf16[64,1024]{1,0:T(8,128)(2,1)S(1)} %get-tuple-element.43), channel_id=1, source_target_pairs={{0,8},{1,9},{2,10},{3,11},{4,12},{5,13},{6,14},{7,15},{8,16},{9,17... | collective-permute-start | bytes 393224 | tf_op jit(solution)/shard_map/ppermute | solution.py:194
  125.4 1.9 %collective-permute-start.34 = (f32[16,128]{1,0:T(8,128)S(1)}, f32[16,128]{1,0:T(8,128)S(1)}, u32[]{:S(2)}, u32[]{:S(2)}) collective-permute-start(f32[16,128]{1,0:T(8,128)S(1)} %add_add_fusion), channel_id=1, source_target_pairs={{0,128},{1,129},{2,130},{3,131},{4,132},{5,133},{6,134},{7,135},{8... | collective-permute-start | bytes 24584 | tf_op jit(solution)/shard_map/ppermute | solution.py:344
  127.4 11.2 %collective-permute-start.35 = (f32[16,128]{1,0:T(8,128)S(1)}, f32[16,128]{1,0:T(8,128)S(1)}, u32[]{:S(2)}, u32[]{:S(2)}) collective-permute-start(f32[16,128]{1,0:T(8,128)S(1)} %add_add_fusion), channel_id=1, source_target_pairs={{0,1},{1,0},{2,3},{3,2},{4,5},{5,4},{6,7},{7,6},{8,9},{9,8},{10,11... | collective-permute-start | bytes 24584 | tf_op jit(solution)/shard_map/ppermute | solution.py:344
  138.6 3.5 %collective-permute-start.36 = (f32[16,128]{1,0:T(8,128)S(1)}, f32[16,128]{1,0:T(8,128)S(1)}, u32[]{:S(2)}, u32[]{:S(2)}) collective-permute-start(f32[16,128]{1,0:T(8,128)S(1)} %add_add_fusion), channel_id=1, source_target_pairs={{0,129},{1,128},{2,131},{3,130},{4,133},{5,132},{6,135},{7,134},{8... | collective-permute-start | bytes 24584 | tf_op jit(solution)/shard_map/ppermute | solution.py:344
  142.8 1.8 %collective-permute-start.21 = (bf16[2,16,1024]{2,1,0:T(8,128)(2,1)}, bf16[2,16,1024]{2,1,0:T(8,128)(2,1)}, u32[]{:S(2)}, u32[]{:S(2)}) collective-permute-start(bf16[2,16,1024]{2,1,0:T(8,128)(2,1)} %fusion.19), channel_id=1, source_target_pairs={{0,2},{1,3},{2,0},{3,1},{4,6},{5,7},{6,4},{7,5},{8,10},{9,11},{10,... | collective-permute-start | bytes 196616 | tf_op jit(solution)/shard_map/ppermute | solution.py:194
  144.8 2.4 %collective-permute-start.24 = (bf16[256,1024]{1,0:T(8,128)(2,1)S(1)}, bf16[256,1024]{1,0:T(8,128)(2,1)}, u32[]{:S(2)}, u32[]{:S(2)}) collective-permute-start(bf16[256,1024]{1,0:T(8,128)(2,1)S(1)} %copy-done.5), channel_id=1, source_target_pairs={{1,2},{2,1},{3,4},{4,3},{5,6},{6,5},{7,8},{8,7},{9,10},{10,9},{11,... | collective-permute-start | bytes 1572872 | tf_op jit(solution)/shard_map/ppermute | solution.py:332
  147.3 0.9 fusion.9
  149.5 1.2 convert_add_fusion.1
  150.8 8.2 %collective-permute-done.24 = bf16[256,1024]{1,0:T(8,128)(2,1)} collective-permute-done((bf16[256,1024]{1,0:T(8,128)(2,1)S(1)}, bf16[256,1024]{1,0:T(8,128)(2,1)}, u32[]{:S(2)}, u32[]{:S(2)}) %collective-permute-start.24) | collective-permute-done | bytes 524320 | tf_op jit(solution)/shard_map/ppermute | solution.py:332
  158.9 1.2 convert_add_fusion
  160.5 1.0 pad_maximum_fusion.2
  161.6 0.9 maximum_select_fusion.1
  162.5 0.9 maximum_select_fusion
  (141 shorter events, 12.7 us)
Async XLA Ops:
  1.9 6.1 %slice-start = ((bf16[1,128,2048]{2,1,0:T(8,128)(2,1)}), bf16[1,8,2048]{2,1,0:T(8,128)(2,1)S(1)}, s32[]{:S(2)}) async-start(bf16[1,128,2048]{2,1,0:T(8,128)(2,1)} %param.8), calls=%async_computation | async-start | bytes 65536 | tf_op jit(solution)/shard_map/slice | solution.py:218
  2.8 10.9 %copy-start.24 = (s32[4096]{0:T(1024)S(1)}, s32[4096]{0:T(1024)}, u32[]{:S(2)}) copy-start(s32[4096]{0:T(1024)} %param.12) | copy-start | bytes 49156
  2.8 10.9 %copy-start.25 = (s32[1,4096]{1,0:T(1,128)S(1)}, s32[1,4096]{1,0:T(1,128)}, u32[]{:S(2)}) copy-start(s32[1,4096]{1,0:T(1,128)} %param.11) | copy-start | bytes 49156
  2.8 11.6 %copy-start.2 = (bf16[1,128,2048]{2,1,0:T(8,128)(2,1)S(1)}, bf16[1,128,2048]{2,1,0:T(8,128)(2,1)}, u32[]{:S(2)}) copy-start(bf16[1,128,2048]{2,1,0:T(8,128)(2,1)} %param.7) | copy-start | bytes 1572868
  2.8 11.6 %copy-start.3 = (bf16[1,128,2048]{2,1,0:T(8,128)(2,1)S(1)}, bf16[1,128,2048]{2,1,0:T(8,128)(2,1)}, u32[]{:S(2)}) copy-start(bf16[1,128,2048]{2,1,0:T(8,128)(2,1)} %param.10) | copy-start | bytes 1572868
  2.8 65.0 %collective-permute-start = (bf16[256,1024]{1,0:T(8,128)(2,1)}, bf16[256,1024]{1,0:T(8,128)(2,1)}, u32[]{:S(2)}, u32[]{:S(2)}) collective-permute-start(bf16[256,1024]{1,0:T(8,128)(2,1)} %pad_maximum_fusion.3), channel_id=1, source_target_pairs={{0,1},{1,0},{2,3},{3,2},{4,5},{5,4},{6,7},{7,6},{8,9},{9,8},{10,11... | collective-permute-start | bytes 1572872 | tf_op jit(solution)/shard_map/ppermute | solution.py:194
  6.1 61.7 %collective-permute-start.2 = (bf16[256,1024]{1,0:T(8,128)(2,1)}, bf16[256,1024]{1,0:T(8,128)(2,1)}, u32[]{:S(2)}, u32[]{:S(2)}) collective-permute-start(bf16[256,1024]{1,0:T(8,128)(2,1)} %pad_maximum_fusion.3), channel_id=1, source_target_pairs={{1,2},{2,1},{3,4},{4,3},{5,6},{6,5},{7,8},{8,7},{9,10},{10,9},{11,... | collective-permute-start | bytes 1572872 | tf_op jit(solution)/shard_map/ppermute | solution.py:240
  8.1 7.3 %collective-permute-start.4 = (bf16[2,8,1024]{2,1,0:T(8,128)(2,1)S(1)}, bf16[2,8,1024]{2,1,0:T(8,128)(2,1)S(1)}, u32[]{:S(2)}, u32[]{:S(2)}) collective-permute-start(bf16[2,8,1024]{2,1,0:T(8,128)(2,1)S(1)} %get-tuple-element.55), channel_id=1, source_target_pairs={{0,1},{1,0},{2,3},{3,2},{4,5},{5,4},{6,7},{7,6},{8,9},{9,8},{10,11... | collective-permute-start | bytes 98312 | tf_op jit(solution)/shard_map/ppermute | solution.py:194
  9.0 58.8 %collective-permute-start.3 = (bf16[256,1024]{1,0:T(8,128)(2,1)}, bf16[256,1024]{1,0:T(8,128)(2,1)}, u32[]{:S(2)}, u32[]{:S(2)}) collective-permute-start(bf16[256,1024]{1,0:T(8,128)(2,1)} %pad_maximum_fusion.5), channel_id=1, source_target_pairs={{1,3},{2,0},{3,5},{4,2},{5,7},{6,4},{7,9},{8,6},{9,11},{10,8},{11,... | collective-permute-start | bytes 1572872 | tf_op jit(solution)/shard_map/ppermute | solution.py:241
  15.4 17.2 %collective-permute-start.5 = (bf16[32,1024]{1,0:T(8,128)(2,1)S(1)}, bf16[32,1024]{1,0:T(8,128)(2,1)S(1)}, u32[]{:S(2)}, u32[]{:S(2)}) collective-permute-start(bf16[32,1024]{1,0:T(8,128)(2,1)S(1)} %bitcast.104), channel_id=1, source_target_pairs={{0,2},{1,3},{2,0},{3,1},{4,6},{5,7},{6,4},{7,5},{8,10},{9,11},{10,... | collective-permute-start | bytes 196616 | tf_op jit(solution)/shard_map/ppermute | solution.py:194
  32.6 7.6 %collective-permute-start.7 = (bf16[64,1024]{1,0:T(8,128)(2,1)S(1)}, bf16[64,1024]{1,0:T(8,128)(2,1)S(1)}, u32[]{:S(2)}, u32[]{:S(2)}) collective-permute-start(bf16[64,1024]{1,0:T(8,128)(2,1)S(1)} %pad_maximum_fusion.6.refs_8_), channel_id=1, source_target_pairs={{0,24},{1,25},{2,26},{3,27},{4,28},{5,29},{6,30},{7,31},{8,0},{9,1... | collective-permute-start | bytes 393224 | tf_op jit(solution)/shard_map/ppermute | solution.py:194
  38.3 8.0 %collective-permute-start.9 = (bf16[64,1024]{1,0:T(8,128)(2,1)S(1)}, bf16[64,1024]{1,0:T(8,128)(2,1)S(1)}, u32[]{:S(2)}, u32[]{:S(2)}) collective-permute-start(bf16[64,1024]{1,0:T(8,128)(2,1)S(1)} %pad_maximum_fusion.6.refs_8_), channel_id=1, source_target_pairs={{0,8},{1,9},{2,10},{3,11},{4,12},{5,13},{6,14},{7,15},{8,16},{9,17... | collective-permute-start | bytes 393224 | tf_op jit(solution)/shard_map/ppermute | solution.py:194
  38.4 29.5 %copy-start = (bf16[1,128,2048]{2,1,0:T(8,128)(2,1)S(1)}, bf16[1,128,2048]{2,1,0:T(8,128)(2,1)}, u32[]{:S(2)}) copy-start(bf16[1,128,2048]{2,1,0:T(8,128)(2,1)} %param.8) | copy-start | bytes 1572868
  38.4 29.5 %copy-start.1 = (bf16[1,128,2048]{2,1,0:T(8,128)(2,1)S(1)}, bf16[1,128,2048]{2,1,0:T(8,128)(2,1)}, u32[]{:S(2)}) copy-start(bf16[1,128,2048]{2,1,0:T(8,128)(2,1)} %param.9) | copy-start | bytes 1572868
  40.3 7.3 %collective-permute-start.12 = (bf16[64,1024]{1,0:T(8,128)(2,1)S(1)}, bf16[64,1024]{1,0:T(8,128)(2,1)S(1)}, u32[]{:S(2)}, u32[]{:S(2)}) collective-permute-start(bf16[64,1024]{1,0:T(8,128)(2,1)S(1)} %pad_maximum_fusion.6.refs_8_), channel_id=1, source_target_pairs={{0,4},{1,5},{2,6},{3,7},{4,8},{5,9},{6,10},{7,11},{8,12},{9,13},{1... | collective-permute-start | bytes 393224 | tf_op jit(solution)/shard_map/ppermute | solution.py:194
  46.4 4.6 %collective-permute-start.6 = (bf16[64,1024]{1,0:T(8,128)(2,1)S(1)}, bf16[64,1024]{1,0:T(8,128)(2,1)S(1)}, u32[]{:S(2)}, u32[]{:S(2)}) collective-permute-start(bf16[64,1024]{1,0:T(8,128)(2,1)S(1)} %pad_maximum_fusion.6.refs_8_), channel_id=1, source_target_pairs={{0,28},{1,29},{2,30},{3,31},{4,0},{5,1},{6,2},{7,3},{8,4},{9,5},{1... | collective-permute-start | bytes 393224 | tf_op jit(solution)/shard_map/ppermute | solution.py:194
  47.6 20.3 %copy-start.10 = (bf16[64,1024]{1,0:T(8,128)(2,1)}, bf16[64,1024]{1,0:T(8,128)(2,1)S(1)}, u32[]{:S(2)}) copy-start(bf16[64,1024]{1,0:T(8,128)(2,1)S(1)} %collective-permute-done.12.refs_15_) | copy-start | bytes 393220
  47.6 20.2 %collective-permute-start.1 = (bf16[256,1024]{1,0:T(8,128)(2,1)}, bf16[256,1024]{1,0:T(8,128)(2,1)}, u32[]{:S(2)}, u32[]{:S(2)}) collective-permute-start(bf16[256,1024]{1,0:T(8,128)(2,1)} %pad_maximum_fusion.4), channel_id=1, source_target_pairs={{0,1},{1,0},{2,3},{3,2},{4,5},{5,4},{6,7},{7,6},{8,9},{9,8},{10,11... | collective-permute-start | bytes 1572872 | tf_op jit(solution)/shard_map/ppermute | solution.py:194
  51.0 12.1 %copy-start.12 = (bf16[64,1024]{1,0:T(8,128)(2,1)}, bf16[64,1024]{1,0:T(8,128)(2,1)S(1)}, u32[]{:S(2)}) copy-start(bf16[64,1024]{1,0:T(8,128)(2,1)S(1)} %collective-permute-done.6.refs_9_) | copy-start | bytes 393220
  51.0 7.1 %collective-permute-start.10 = (bf16[64,1024]{1,0:T(8,128)(2,1)S(1)}, bf16[64,1024]{1,0:T(8,128)(2,1)S(1)}, u32[]{:S(2)}, u32[]{:S(2)}) collective-permute-start(bf16[64,1024]{1,0:T(8,128)(2,1)S(1)} %broadcast_select_fusion), channel_id=1, source_target_pairs={{0,24},{1,9},{2,26},{3,11},{4,28},{5,13},{6,30},{7,15},{8,0},{9,17... | collective-permute-start | bytes 393224 | tf_op jit(solution)/shard_map/ppermute | solution.py:194
  58.0 9.8 %copy-start.14 = (bf16[64,1024]{1,0:T(8,128)(2,1)}, bf16[64,1024]{1,0:T(8,128)(2,1)S(1)}, u32[]{:S(2)}) copy-start(bf16[64,1024]{1,0:T(8,128)(2,1)S(1)} %collective-permute-done.10.refs_12_) | copy-start | bytes 393220
  58.0 5.0 %collective-permute-start.11 = (bf16[64,1024]{1,0:T(8,128)(2,1)S(1)}, bf16[64,1024]{1,0:T(8,128)(2,1)S(1)}, u32[]{:S(2)}, u32[]{:S(2)}) collective-permute-start(bf16[64,1024]{1,0:T(8,128)(2,1)S(1)} %collective-permute-done.9.refs_14_), channel_id=1, source_target_pairs={{0,4},{1,5},{2,6},{3,7},{4,8},{5,9},{6,10},{7,11},{8,12},{9,13},{1... | collective-permute-start | bytes 393224 | tf_op jit(solution)/shard_map/ppermute | solution.py:194
  63.1 4.1 %collective-permute-start.8 = (bf16[64,1024]{1,0:T(8,128)(2,1)S(1)}, bf16[64,1024]{1,0:T(8,128)(2,1)S(1)}, u32[]{:S(2)}, u32[]{:S(2)}) collective-permute-start(bf16[64,1024]{1,0:T(8,128)(2,1)S(1)} %collective-permute-done.7.refs_10_), channel_id=1, source_target_pairs={{0,28},{1,29},{2,30},{3,31},{4,0},{5,1},{6,2},{7,3},{8,4},{9,5},{1... | collective-permute-start | bytes 393224 | tf_op jit(solution)/shard_map/ppermute | solution.py:194
  93.7 50.9 %copy-start.20 = (bf16[512,1024]{1,0:T(8,128)(2,1)S(1)}, bf16[512,1024]{1,0:T(8,128)(2,1)}, u32[]{:S(2)}) copy-start(bf16[512,1024]{1,0:T(8,128)(2,1)} %get-tuple-element.18) | copy-start | bytes 3145732
  93.7 7.4 %collective-permute-start.25 = (f32[16,128]{1,0:T(8,128)S(1)}, f32[16,128]{1,0:T(8,128)S(1)}, u32[]{:S(2)}, u32[]{:S(2)}) collective-permute-start(f32[16,128]{1,0:T(8,128)S(1)} %get-tuple-element.30), channel_id=1, source_target_pairs={{0,8},{1,9},{2,10},{3,11},{4,12},{5,13},{6,14},{7,15},{8,16},{9,17... | collective-permute-start | bytes 24584 | tf_op jit(solution)/shard_map/ppermute | solution.py:194
  93.7 7.4 %collective-permute-start.26 = (f32[16,128]{1,0:T(8,128)S(1)}, f32[16,128]{1,0:T(8,128)S(1)}, u32[]{:S(2)}, u32[]{:S(2)}) collective-permute-start(f32[16,128]{1,0:T(8,128)S(1)} %get-tuple-element.30), channel_id=1, source_target_pairs={{0,16},{1,17},{2,18},{3,19},{4,20},{5,21},{6,22},{7,23},{8,24},{9,... | collective-permute-start | bytes 24584 | tf_op jit(solution)/shard_map/ppermute | solution.py:194
  97.5 4.4 %collective-permute-start.27 = (f32[16,128]{1,0:T(8,128)S(1)}, f32[16,128]{1,0:T(8,128)S(1)}, u32[]{:S(2)}, u32[]{:S(2)}) collective-permute-start(f32[16,128]{1,0:T(8,128)S(1)} %get-tuple-element.30), channel_id=1, source_target_pairs={{0,24},{1,25},{2,26},{3,27},{4,28},{5,29},{6,30},{7,31},{8,0},{9,1... | collective-permute-start | bytes 24584 | tf_op jit(solution)/shard_map/ppermute | solution.py:194
  101.9 9.6 %collective-permute-start.28 = (f32[16,128]{1,0:T(8,128)S(1)}, f32[16,128]{1,0:T(8,128)S(1)}, u32[]{:S(2)}, u32[]{:S(2)}) collective-permute-start(f32[16,128]{1,0:T(8,128)S(1)} %add_add_fusion.2), channel_id=1, source_target_pairs={{0,2},{1,3},{2,0},{3,1},{4,6},{5,7},{6,4},{7,5},{8,10},{9,11},{10,... | collective-permute-start | bytes 24584 | tf_op jit(solution)/shard_map/ppermute | solution.py:194
  106.2 6.6 %collective-permute-start.29 = (f32[16,128]{1,0:T(8,128)S(1)}, f32[16,128]{1,0:T(8,128)S(1)}, u32[]{:S(2)}, u32[]{:S(2)}) collective-permute-start(f32[16,128]{1,0:T(8,128)S(1)} %add_add_fusion.2), channel_id=1, source_target_pairs={{0,4},{1,5},{2,6},{3,7},{4,0},{5,1},{6,2},{7,3},{8,12},{9,13},{10,... | collective-permute-start | bytes 24584 | tf_op jit(solution)/shard_map/ppermute | solution.py:194
  106.7 6.2 %collective-permute-start.30 = (f32[16,128]{1,0:T(8,128)S(1)}, f32[16,128]{1,0:T(8,128)S(1)}, u32[]{:S(2)}, u32[]{:S(2)}) collective-permute-start(f32[16,128]{1,0:T(8,128)S(1)} %add_add_fusion.2), channel_id=1, source_target_pairs={{0,6},{1,7},{2,4},{3,5},{4,2},{5,3},{6,0},{7,1},{8,14},{9,15},{10,... | collective-permute-start | bytes 24584 | tf_op jit(solution)/shard_map/ppermute | solution.py:194
  107.4 8.1 %collective-permute-start.16 = (bf16[64,1024]{1,0:T(8,128)(2,1)}, bf16[64,1024]{1,0:T(8,128)(2,1)S(1)}, u32[]{:S(2)}, u32[]{:S(2)}) collective-permute-start(bf16[64,1024]{1,0:T(8,128)(2,1)} %copy-done.9), channel_id=1, source_target_pairs={{0,4},{1,5},{2,6},{3,7},{4,8},{5,9},{6,10},{7,11},{8,12},{9,13},{1... | collective-permute-start | bytes 393224 | tf_op jit(solution)/shard_map/ppermute | solution.py:194
  108.0 8.7 %collective-permute-start.17 = (bf16[64,1024]{1,0:T(8,128)(2,1)}, bf16[64,1024]{1,0:T(8,128)(2,1)S(1)}, u32[]{:S(2)}, u32[]{:S(2)}) collective-permute-start(bf16[64,1024]{1,0:T(8,128)(2,1)} %copy-done.8), channel_id=1, source_target_pairs={{0,8},{1,25},{2,10},{3,27},{4,12},{5,29},{6,14},{7,31},{8,16},{9,1... | collective-permute-start | bytes 393224 | tf_op jit(solution)/shard_map/ppermute | solution.py:194
  111.5 7.7 %collective-permute-start.19 = (bf16[64,1024]{1,0:T(8,128)(2,1)}, bf16[64,1024]{1,0:T(8,128)(2,1)S(1)}, u32[]{:S(2)}, u32[]{:S(2)}) collective-permute-start(bf16[64,1024]{1,0:T(8,128)(2,1)} %copy-done.7), channel_id=1, source_target_pairs={{0,28},{1,29},{2,30},{3,31},{4,0},{5,1},{6,2},{7,3},{8,4},{9,5},{1... | collective-permute-start | bytes 393224 | tf_op jit(solution)/shard_map/ppermute | solution.py:194
  112.8 12.7 %collective-permute-start.14 = (bf16[64,1024]{1,0:T(8,128)(2,1)S(1)}, bf16[64,1024]{1,0:T(8,128)(2,1)S(1)}, u32[]{:S(2)}, u32[]{:S(2)}) collective-permute-start(bf16[64,1024]{1,0:T(8,128)(2,1)S(1)} %get-tuple-element.21), channel_id=1, source_target_pairs={{0,4},{1,5},{2,6},{3,7},{4,8},{5,9},{6,10},{7,11},{8,12},{9,13},{1... | collective-permute-start | bytes 393224 | tf_op jit(solution)/shard_map/ppermute | solution.py:194
  112.9 14.4 %collective-permute-start.15 = (bf16[64,1024]{1,0:T(8,128)(2,1)S(1)}, bf16[64,1024]{1,0:T(8,128)(2,1)S(1)}, u32[]{:S(2)}, u32[]{:S(2)}) collective-permute-start(bf16[64,1024]{1,0:T(8,128)(2,1)S(1)} %get-tuple-element.22), channel_id=1, source_target_pairs={{0,28},{1,29},{2,30},{3,31},{4,0},{5,1},{6,2},{7,3},{8,4},{9,5},{1... | collective-permute-start | bytes 393224 | tf_op jit(solution)/shard_map/ppermute | solution.py:194
  115.4 5.0 %collective-permute-start.31 = (f32[16,128]{1,0:T(8,128)S(1)}, f32[16,128]{1,0:T(8,128)S(1)}, u32[]{:S(2)}, u32[]{:S(2)}) collective-permute-start(f32[16,128]{1,0:T(8,128)S(1)} %add_add_fusion.1), channel_id=1, source_target_pairs={{0,32},{1,33},{2,34},{3,35},{4,36},{5,37},{6,38},{7,39},{8,40},{9,... | collective-permute-start | bytes 24584 | tf_op jit(solution)/shard_map/ppermute | solution.py:344
  116.7 5.0 %collective-permute-start.32 = (f32[16,128]{1,0:T(8,128)S(1)}, f32[16,128]{1,0:T(8,128)S(1)}, u32[]{:S(2)}, u32[]{:S(2)}) collective-permute-start(f32[16,128]{1,0:T(8,128)S(1)} %add_add_fusion.1), channel_id=1, source_target_pairs={{0,64},{1,65},{2,66},{3,67},{4,68},{5,69},{6,70},{7,71},{8,72},{9,... | collective-permute-start | bytes 24584 | tf_op jit(solution)/shard_map/ppermute | solution.py:344
  119.2 5.5 %collective-permute-start.33 = (f32[16,128]{1,0:T(8,128)S(1)}, f32[16,128]{1,0:T(8,128)S(1)}, u32[]{:S(2)}, u32[]{:S(2)}) collective-permute-start(f32[16,128]{1,0:T(8,128)S(1)} %add_add_fusion.1), channel_id=1, source_target_pairs={{0,96},{1,97},{2,98},{3,99},{4,100},{5,101},{6,102},{7,103},{8,104... | collective-permute-start | bytes 24584 | tf_op jit(solution)/shard_map/ppermute | solution.py:344
  120.5 29.1 %collective-permute-start.23 = (bf16[256,1024]{1,0:T(8,128)(2,1)}, bf16[256,1024]{1,0:T(8,128)(2,1)}, u32[]{:S(2)}, u32[]{:S(2)}) collective-permute-start(bf16[256,1024]{1,0:T(8,128)(2,1)} %copy-done.6), channel_id=1, source_target_pairs={{3,1},{0,2},{5,3},{2,4},{7,5},{4,6},{9,7},{6,8},{11,9},{8,10},{13,... | collective-permute-start | bytes 1572872 | tf_op jit(solution)/shard_map/ppermute | solution.py:333
  121.8 16.8 %collective-permute-start.18 = (bf16[64,1024]{1,0:T(8,128)(2,1)S(1)}, bf16[64,1024]{1,0:T(8,128)(2,1)S(1)}, u32[]{:S(2)}, u32[]{:S(2)}) collective-permute-start(bf16[64,1024]{1,0:T(8,128)(2,1)S(1)} %get-tuple-element.43), channel_id=1, source_target_pairs={{0,8},{1,9},{2,10},{3,11},{4,12},{5,13},{6,14},{7,15},{8,16},{9,17... | collective-permute-start | bytes 393224 | tf_op jit(solution)/shard_map/ppermute | solution.py:194
  124.7 17.3 %collective-permute-start.20 = (bf16[64,1024]{1,0:T(8,128)(2,1)S(1)}, bf16[64,1024]{1,0:T(8,128)(2,1)S(1)}, u32[]{:S(2)}, u32[]{:S(2)}) collective-permute-start(bf16[64,1024]{1,0:T(8,128)(2,1)S(1)} %get-tuple-element.44), channel_id=1, source_target_pairs={{0,24},{1,25},{2,26},{3,27},{4,28},{5,29},{6,30},{7,31},{8,0},{9,1... | collective-permute-start | bytes 393224 | tf_op jit(solution)/shard_map/ppermute | solution.py:194
  125.4 19.2 %collective-permute-start.34 = (f32[16,128]{1,0:T(8,128)S(1)}, f32[16,128]{1,0:T(8,128)S(1)}, u32[]{:S(2)}, u32[]{:S(2)}) collective-permute-start(f32[16,128]{1,0:T(8,128)S(1)} %add_add_fusion), channel_id=1, source_target_pairs={{0,128},{1,129},{2,130},{3,131},{4,132},{5,133},{6,134},{7,135},{8... | collective-permute-start | bytes 24584 | tf_op jit(solution)/shard_map/ppermute | solution.py:344
  127.4 17.5 %collective-permute-start.35 = (f32[16,128]{1,0:T(8,128)S(1)}, f32[16,128]{1,0:T(8,128)S(1)}, u32[]{:S(2)}, u32[]{:S(2)}) collective-permute-start(f32[16,128]{1,0:T(8,128)S(1)} %add_add_fusion), channel_id=1, source_target_pairs={{0,1},{1,0},{2,3},{3,2},{4,5},{5,4},{6,7},{7,6},{8,9},{9,8},{10,11... | collective-permute-start | bytes 24584 | tf_op jit(solution)/shard_map/ppermute | solution.py:344
  138.6 8.7 %collective-permute-start.36 = (f32[16,128]{1,0:T(8,128)S(1)}, f32[16,128]{1,0:T(8,128)S(1)}, u32[]{:S(2)}, u32[]{:S(2)}) collective-permute-start(f32[16,128]{1,0:T(8,128)S(1)} %add_add_fusion), channel_id=1, source_target_pairs={{0,129},{1,128},{2,131},{3,130},{4,133},{5,132},{6,135},{7,134},{8... | collective-permute-start | bytes 24584 | tf_op jit(solution)/shard_map/ppermute | solution.py:344
  142.8 4.5 %collective-permute-start.21 = (bf16[2,16,1024]{2,1,0:T(8,128)(2,1)}, bf16[2,16,1024]{2,1,0:T(8,128)(2,1)}, u32[]{:S(2)}, u32[]{:S(2)}) collective-permute-start(bf16[2,16,1024]{2,1,0:T(8,128)(2,1)} %fusion.19), channel_id=1, source_target_pairs={{0,2},{1,3},{2,0},{3,1},{4,6},{5,7},{6,4},{7,5},{8,10},{9,11},{10,... | collective-permute-start | bytes 196616 | tf_op jit(solution)/shard_map/ppermute | solution.py:194
  144.6 14.3 %collective-permute-start.13 = (bf16[512,1024]{1,0:T(8,128)(2,1)}, bf16[512,1024]{1,0:T(8,128)(2,1)S(1)}, u32[]{:S(2)}, u32[]{:S(2)}) collective-permute-start(bf16[512,1024]{1,0:T(8,128)(2,1)} %get-tuple-element.19), channel_id=1, source_target_pairs={{0,1},{1,0},{2,3},{3,2},{4,5},{5,4},{6,7},{7,6},{8,9},{9,8},{10,11... | collective-permute-start | bytes 3145736 | tf_op jit(solution)/shard_map/ppermute | solution.py:194
  144.8 14.1 %collective-permute-start.24 = (bf16[256,1024]{1,0:T(8,128)(2,1)S(1)}, bf16[256,1024]{1,0:T(8,128)(2,1)}, u32[]{:S(2)}, u32[]{:S(2)}) collective-permute-start(bf16[256,1024]{1,0:T(8,128)(2,1)S(1)} %copy-done.5), channel_id=1, source_target_pairs={{1,2},{2,1},{3,4},{4,3},{5,6},{6,5},{7,8},{8,7},{9,10},{10,9},{11,... | collective-permute-start | bytes 1572872 | tf_op jit(solution)/shard_map/ppermute | solution.py:332
  148.2 1.3 collective-permute-start.22
  (17 other events, 33.1 us)

commit v2 on v1

--- a/solution.py
+++ b/solution.py
@@ -14,7 +14,11 @@
 SLOT = 16
 BF16 = jnp.bfloat16
 F32 = jnp.float32
-OFFSETS = (0, 1, 2, 3, 4, -3, -2, -1)
+OFFSETS = (0, 2, -2, 4, 1, 3, -1, -3)
+
+
+def after(x, *done):
+    return lax.optimization_barrier((x, *done))[0]
 
 
 def mm(a, b, contract):
@@ -28,23 +32,24 @@
 
 def attention_kernel(inv_scale, half_ref, *refs):
     (q_ref, k_ref, v_ref, g_ref, kv_par, qg_par, kv_own_out, kv_par_out) = refs[:8]
-    coarse_refs = refs[8:16]
-    row_hot_ref, key_hot_ref, table_ref, keep_ref = refs[16:20]
-    own_ref, par_ref, own_out_ref, par_out_ref = refs[20:24]
-    coarse_out = refs[24:32]
-    bias_ref = refs[32]
+    coarse_refs = refs[8:14]
+    row_hot_ref, key_hot_ref, table_ref, keep_ref = refs[14:18]
+    own_ref, par_ref, own_out_ref, par_out_ref = refs[18:22]
+    coarse_out = refs[22:28]
+    bias_ref = refs[28]
     step = pl.program_id(0)
     rows = q_ref.shape[0]
     part = coarse_refs[0].shape[0] // 2
-    total = part * len(coarse_refs)
+    places = [(r, a) for r in range(len(coarse_refs)) for a in range(0, coarse_refs[r].shape[0], 2 * part)]
+    total = part * len(places)
     keep = keep_ref[...] > 0.0
     q = jnp.concatenate([q_ref[...], qg_par[:rows]], axis=0)
     g_all = jnp.concatenate([g_ref[...], qg_par[rows:]], axis=0)
     g = jnp.where(keep, g_all.astype(F32), 0.0).astype(BF16)
     row_hot = row_hot_ref[...]
     key_hot = key_hot_ref[...]
-    k_main = jnp.concatenate([r[:part] for r in coarse_refs] + [k_ref[...], kv_par[:rows]], axis=0)
-    v_main = jnp.concatenate([r[part:] for r in coarse_refs] + [v_ref[...], kv_par[rows:]], axis=0)
+    k_main = jnp.concatenate([coarse_refs[r][a : a + part] for r, a in places] + [k_ref[...], kv_par[:rows]], axis=0)
+    v_main = jnp.concatenate([coarse_refs[r][a + part : a + 2 * part] for r, a in places] + [v_ref[...], kv_par[rows:]], axis=0)
     main = k_main.shape[0]
     hot_main = key_hot[:main]
     hot_own = key_hot[main : main + rows]
@@ -124,16 +129,15 @@
     own_out_ref[rows:] = gv_own
     par_out_ref[:rows] = gk_par
     par_out_ref[rows:] = gv_par
-    for j, ref in enumerate(coarse_out):
-        ref[:part] = gk_main[j * part : (j + 1) * part]
-        ref[part:] = gv_main[j * part : (j + 1) * part]
+    for j, (r, a) in enumerate(places):
+        coarse_out[r][a : a + part] = gk_main[j * part : (j + 1) * part]
+        coarse_out[r][a + part : a + 2 * part] = gv_main[j * part : (j + 1) * part]
 
 
 def call_kernel(inv_scale, half, full, pairs, coarse, tables, heads):
     rows, width = full[0].shape
     half_width = width // 2
     steps = heads // 2
-    part2 = coarse[0].shape[0]
     row_hot, key_hot, table, keep = tables
 
     def mine(h, half_ref):
@@ -148,7 +152,7 @@
     in_specs = (
         [pl.BlockSpec((rows, LANES), mine)] * 4
         + [pl.BlockSpec((2 * rows, LANES), at)] * 4
-        + [pl.BlockSpec((part2, LANES), at)] * len(coarse)
+        + [pl.BlockSpec((x.shape[0], LANES), at) for x in coarse]
         + [
             pl.BlockSpec(row_hot.shape, fixed),
             pl.BlockSpec(key_hot.shape, fixed),
@@ -156,7 +160,7 @@
             pl.BlockSpec(keep.shape, fixed),
         ]
     )
-    out_rows = [4 * rows] * 2 + [2 * rows] * 2 + [part2] * len(coarse)
+    out_rows = [4 * rows] * 2 + [2 * rows] * 2 + [x.shape[0] for x in coarse]
     out_shape = [jax.ShapeDtypeStruct((r, half_width), BF16) for r in out_rows]
     out_shape.append(jax.ShapeDtypeStruct((SLOT, LANES), F32))
     out_specs = [pl.BlockSpec((r, LANES), at) for r in out_rows]
@@ -168,7 +172,7 @@
         ),
         out_shape=out_shape,
         compiler_params=pltpu.CompilerParams(
-            dimension_semantics=("arbitrary",), vmem_limit_bytes=48 * 1024 * 1024
+            dimension_semantics=("arbitrary",), vmem_limit_bytes=60 * 1024 * 1024
         ),
         cost_estimate=pl.CostEstimate(
             flops=12 * 2 * rows * 640 * half_width,
@@ -199,6 +203,9 @@
     def to_side(x):
         return send(x, lambda i: i ^ 2)
 
+    def to_corner(x):
+        return send(x, lambda i: i ^ 3)
+
     def to_depth(x, distance):
         return send(x, lambda i: (i + 4 * distance) % tiles)
 
@@ -218,29 +225,28 @@
     small = jnp.stack([k[:COARSE], v[:COARSE]])
     small_mine = lax.dynamic_slice_in_dim(small, core * half_width, half_width, 2)
     small_other = lax.dynamic_slice_in_dim(small, (1 - core) * half_width, half_width, 2)
-    chip = jnp.concatenate([small_mine, to_core(small_other)], axis=1).reshape(-1, half_width)
-    side = to_side(chip)
-    group = jnp.concatenate(
-        [x[a : a + 2 * COARSE] for a in (0, 2 * COARSE) for x in (chip, side)], axis=0
-    )
-    blocks = {0: group}
-    for d in (1, -1, 2, -2):
-        blocks[d] = to_depth(group, -d)
-    blocks[3] = to_depth(blocks[2], -1)
-    blocks[-3] = to_depth(blocks[-2], 1)
-    blocks[4] = send(
-        jnp.where(core == 0, blocks[2], blocks[-2]),
+    first = [small_mine, to_core(small_other), to_side(small_mine), to_corner(small_other)]
+    group = jnp.concatenate(first, axis=1).reshape(-1, half_width)
+    up_two = to_depth(group, -2)
+    down_two = to_depth(group, 2)
+    four = send(
+        jnp.where(core == 0, up_two, down_two),
         lambda i: (i + (8 if i % 2 else -8)) % tiles,
     )
-    coarse = [blocks[d] for d in OFFSETS]
+    up_odd = to_depth(jnp.concatenate([group, up_two], axis=0), -1)
 
     kv_other = jnp.concatenate([cut(k, 1 - core), cut(v, 1 - core)], axis=0)
     kv_mine = jnp.concatenate([cut(k, core), cut(v, core)], axis=0)
     qg_other = jnp.concatenate([cut(q, 1 - core), cut(g, 1 - core)], axis=0)
+    kv_other, kv_mine, qg_other, _ = lax.optimization_barrier((kv_other, kv_mine, qg_other, group))
     kv_own_out = lax.ppermute(kv_other, "tile", edge)
     kv_par_out = lax.ppermute(kv_mine, "tile", jump)
     kv_par = to_core(kv_other)
     qg_par = to_core(qg_other)
+    down_pair = jnp.concatenate([group, down_two], axis=0)
+    down_pair, kv_own_out = lax.optimization_barrier((down_pair, kv_own_out))
+    down_odd = to_depth(down_pair, 1)
+    coarse = [group, up_two, down_two, four, up_odd, down_odd]
 
     valid_grid = valid[0].reshape(tiles, rows)
     scale_grid = scale_ids.reshape(tiles, rows)
@@ -306,63 +312,48 @@
         heads,
     )
     own, par, own_out, par_out = results[:4]
-    terms = dict(zip(OFFSETS, results[4:12]))
-    bias = results[12]
-
-    from_below = to_depth(terms[3], 1)
-    from_above = to_depth(terms[-3], -1)
-    across = send(terms[4], lambda i: (i + (-8 if i % 2 else 8)) % tiles)
-    one_up = to_depth(terms[1], 1)
-    one_down = to_depth(terms[-1], -1)
+    here, up_two, down_two, four, up_odd, down_odd = results[4:10]
+    bias = results[10]
 
     def wide(x):
         return x.astype(F32)
 
+    def xor_sum(x, axis, count, bits):
+        got = [lax.ppermute(x, axis, [(i, i ^ b) for i in range(count)]) for b in bits]
+        return sum(got, x)
+
+    both = ("batch", "tile")
     zero = jnp.zeros((), F32)
-    two_up = wide(terms[2]) + wide(from_below) + jnp.where(core == 0, wide(across), zero)
-    two_down = wide(terms[-2]) + wide(from_above) + jnp.where(core == 1, wide(across), zero)
-    two_up = to_depth(two_up.astype(BF16), 2)
-    two_down = to_depth(two_down.astype(BF16), -2)
-    summed = wide(terms[0]) + wide(one_up) + wide(one_down) + wide(two_up) + wide(two_down)
-    summed = summed.reshape(2, 2, 2 * COARSE, half_width)
-    coarse_chip = summed[:, 0] + wide(to_side(summed[:, 1].astype(BF16)))
-    coarse_mine = coarse_chip[:, :COARSE]
-    coarse_other = wide(to_core(coarse_chip[:, COARSE:].astype(BF16)))
-
+    block = here.shape[0]
     back_other = lax.ppermute(own_out, "tile", edge)
     back_mine = lax.ppermute(par_out, "tile", [(b, a) for a, b in jump])
     other = to_core(par)
-
-    both = ("batch", "tile")
-
-    def everywhere(x, target):
-        pairs = []
-        for b in range(images):
-            for i in range(tiles):
-                b2, i2 = target(b, i)
-                pairs.append((b * tiles + i, b2 * tiles + i2))
-        return lax.ppermute(x, both, pairs)
-
-    for shifts in ((2, 4, 6), (1,)):
-        got = []
-        for s in shifts:
-            got.append(to_depth(bias, s))
-        if len(shifts) == 1:
-            got = [send(bias, lambda i: i ^ 2)]
-            got.append(send(bias, lambda i: (i + 4) % tiles if (i // 4) % 2 == 0 else i - 4))
-            got.append(send(bias, lambda i: ((i + 4) if (i // 4) % 2 == 0 else (i - 4)) ^ 2))
-        for x in got:
-            bias = bias + x
-    x_count = images // 2
-    got = [
-        everywhere(bias, lambda b, i, s=s: ((b // x_count) * x_count + (b + s) % x_count, i))
-        for s in range(1, x_count)
-    ]
-    for x in got:
-        bias = bias + x
-    same = everywhere(bias, lambda b, i: ((b + x_count) % images, i))
-    swap = everywhere(bias, lambda b, i: (b, i ^ 1))
-    cross = everywhere(bias, lambda b, i: ((b + x_count) % images, i ^ 1))
+    up_odd = to_depth(up_odd, 1)
+    down_odd = to_depth(down_odd, -1)
+    four = send(four, lambda i: (i + (-8 if i % 2 else 8)) % tiles)
+    bias = xor_sum(bias, "tile", tiles, (4, 8, 12))
+    up_odd, down_odd, four, bias = lax.optimization_barrier((up_odd, down_odd, four, bias))
+    up_two = wide(up_two) + wide(up_odd[block:]) + jnp.where(core == 0, wide(four), zero)
+    down_two = wide(down_two) + wide(down_odd[block:]) + jnp.where(core == 1, wide(four), zero)
+    up_two = to_depth(up_two.astype(BF16), 2)
+    down_two = to_depth(down_two.astype(BF16), -2)
+    bias = xor_sum(bias, "tile", tiles, (16, 2, 18))
+    up_two, down_two, bias = lax.optimization_barrier((up_two, down_two, bias))
+    summed = wide(here) + wide(up_odd[:block]) + wide(down_odd[:block])
+    summed = summed + wide(up_two) + wide(down_two)
+    summed = summed.reshape(2, 4, COARSE, half_width)
+    narrow = summed.astype(BF16)
+    quad = [to_core(narrow[:, 1]), to_side(narrow[:, 2]), to_corner(narrow[:, 3])]
+    bias, back_other = lax.optimization_barrier((bias, back_other))
+    bias = xor_sum(bias, "batch", images, (1, 2, 3))
+    quad[0], quad[1], quad[2], bias = lax.optimization_barrier((*quad, bias))
+    coarse_mine = summed[:, 0] + wide(quad[1])
+    coarse_other = wide(quad[0]) + wide(quad[2])
+    every = images * tiles
+    half_count = every // 2
+    same = lax.ppermute(bias, both, [(i, i ^ half_count) for i in range(every)])
+    swap = to_core(bias)
+    cross = lax.ppermute(bias, both, [(i, i ^ half_count ^ 1) for i in range(every)])
     mine_bias = bias + same
     other_bias = swap + cross
     bias_halves = jnp.where(

time: 165 us -> 136 us (0.82)
  starting transfers between devices: 71.5 us -> 61.4 us
  other arithmetic: 12.9 us -> 6.54 us
  local copies, waits for them, and re-layouts: 12.2 us -> 6.72 us
  waiting for transfers between devices: 47.6 us -> 42.2 us
    ppermute x27 -> x20, waiting for transfers between devices: 39.4 us -> 18.8 us  [send(): return lax.ppermute(x, 'tile', [(i, target(i)) for i in range(tiles)])]
    ppermute x6 -> x11, waiting for transfers between devices: 0.02 us -> 12.6 us  [the longest x9 8.89 us: xor_sum(): lax.ppermute(x, axis, [(i, i ^ b) for i in range(count)])]
    ppermute x1, waiting for transfers between devices: 0.01 us -> 10.8 us  [shards(): kv_own_out = lax.ppermute(kv_other, 'tile', edge)]
    ppermute x1, waiting for transfers between devices: 8.16 us -> 0.01 us  [shards(): back_other = lax.ppermute(own_out, 'tile', edge)]
    unnamed x56 -> x40, local copies, waits for them, and re-layouts: 8.84 us -> 0.79 us
    ppermute x27 -> x20, starting transfers between devices: 39.8 us -> 32.2 us  [send(): return lax.ppermute(x, 'tile', [(i, target(i)) for i in range(tiles)])]
    ppermute x6 -> x11, starting transfers between devices: 21.5 us -> 17.1 us  [the longest x9 14.2 us: xor_sum(): lax.ppermute(x, axis, [(i, i ^ b) for i in range(count)])]
    ppermute x1, starting transfers between devices: 1.91 us -> 4.08 us  [shards(): kv_own_out = lax.ppermute(kv_other, 'tile', edge)]
  transfers between devices with their start and end apart: 37 -> 35, of which waited for: 10 -> 12; matrix products, arithmetic and copies ran while one was open for 6% -> 6% of each run, Pallas kernels for 0% -> 0%
where the time goes in v2:
time: 136 us
  starting transfers between devices  61.4 us (45%)
  waiting for transfers between devices  42.2 us (31%)
  Pallas kernels  17.5 us (13%)
  local copies, waits for them, and re-layouts  6.72 us (5%)
  other arithmetic  6.54 us (5%)
    ppermute x20, starting transfers between devices, send(): return lax.ppermute(x, 'tile', [(i, target(i)) for i in range(tiles)])  32.2 us
    ppermute x20, waiting for transfers between devices, send(): return lax.ppermute(x, 'tile', [(i, target(i)) for i in range(tiles)])  18.8 us
    pallas_call x1, Pallas kernels, call_kernel(): pl.pallas_call(functools.partial(attention_kernel, inv_scale), grid_spec=...  17.5 us
    ppermute x9, starting transfers between devices, xor_sum(): lax.ppermute(x, axis, [(i, i ^ b) for i in range(count)])  14.2 us
    ppermute x1, waiting for transfers between devices, shards(): kv_own_out = lax.ppermute(kv_other, 'tile', edge)  10.8 us
    ppermute x9, waiting for transfers between devices, xor_sum(): lax.ppermute(x, axis, [(i, i ^ b) for i in range(count)])  8.89 us
    ppermute x1, starting transfers between devices, shards(): kv_own_out = lax.ppermute(kv_other, 'tile', edge)  4.08 us
    ppermute x1, waiting for transfers between devices, shards(): lax.ppermute(bias, both, [(i, i ^ half_count ^ 1) for i in range(every)])  3.75 us
  transfers between devices with their start and end apart: 35, of which 12 were waited for; matrix products, arithmetic and copies ran while one was open for 6% of the time, Pallas kernels for 0%

profile of v2, /device:TPU:1, one launch (start us, length us, event | category | flops | bytes accessed | tf_op | source)
XLA Modules:
  0.0 135.9 jit_solution(2206674916095312718)
XLA Ops:
  0.7 0.8 slice.66
  1.4 0.8 slice.67
  2.2 3.3 %collective-permute-start = (bf16[2,8,1024]{2,1,0:T(8,128)(2,1)S(1)}, bf16[2,8,1024]{2,1,0:T(8,128)(2,1)S(1)}, u32[]{:S(2)}, u32[]{:S(2)}) collective-permute-start(bf16[2,8,1024]{2,1,0:T(8,128)(2,1)S(1)} %get-tuple-element.86), channel_id=1, source_target_pairs={{0,1},{1,0},{2,3},{3,2},{4,5},{5,4},{6,7},{7,6},{8,9},{9,8},{10,11... | collective-permute-start | bytes 98312 | tf_op jit(solution)/shard_map/ppermute | solution.py:198
  5.5 1.4 %collective-permute-start.1 = (bf16[2,8,1024]{2,1,0:T(8,128)(2,1)S(1)}, bf16[2,8,1024]{2,1,0:T(8,128)(2,1)S(1)}, u32[]{:S(2)}, u32[]{:S(2)}) collective-permute-start(bf16[2,8,1024]{2,1,0:T(8,128)(2,1)S(1)} %get-tuple-element.85), channel_id=1, source_target_pairs={{0,2},{1,3},{2,0},{3,1},{4,6},{5,7},{6,4},{7,5},{8,10},{9,11},{10,... | collective-permute-start | bytes 98312 | tf_op jit(solution)/shard_map/ppermute | solution.py:198
  7.0 1.3 dynamic-slice_bitcast_fusion.2
  9.0 0.7 fusion.15.refs_14_
  10.1 0.7 fusion.17.refs_16_
  10.9 1.3 collective-permute-start.5
  12.2 3.1 %collective-permute-start.8 = (bf16[64,1024]{1,0:T(8,128)(2,1)S(1)}, bf16[64,1024]{1,0:T(8,128)(2,1)S(1)}, u32[]{:S(2)}, u32[]{:S(2)}) collective-permute-start(bf16[64,1024]{1,0:T(8,128)(2,1)S(1)} %bitcast.103), channel_id=1, source_target_pairs={{0,24},{1,25},{2,26},{3,27},{4,28},{5,29},{6,30},{7,31},{8,0},{9,1... | collective-permute-start | bytes 393224 | tf_op jit(solution)/shard_map/ppermute | solution.py:198
  15.3 4.1 %collective-permute-start.6 = (bf16[256,1024]{1,0:T(8,128)(2,1)S(1)}, bf16[256,1024]{1,0:T(8,128)(2,1)}, u32[]{:S(2)}, u32[]{:S(2)}) collective-permute-start(bf16[256,1024]{1,0:T(8,128)(2,1)S(1)} %pad_maximum_fusion.3), channel_id=1, source_target_pairs={{1,2},{2,1},{3,4},{4,3},{5,6},{6,5},{7,8},{8,7},{9,10},{10,9},{11,... | collective-permute-start | bytes 1572872 | tf_op jit(solution)/shard_map/ppermute | solution.py:242
  20.1 3.3 %collective-permute-start.7 = (bf16[256,1024]{1,0:T(8,128)(2,1)S(1)}, bf16[256,1024]{1,0:T(8,128)(2,1)}, u32[]{:S(2)}, u32[]{:S(2)}) collective-permute-start(bf16[256,1024]{1,0:T(8,128)(2,1)S(1)} %pad_maximum_fusion.4), channel_id=1, source_target_pairs={{1,3},{2,0},{3,5},{4,2},{5,7},{6,4},{7,9},{8,6},{9,11},{10,8},{11,... | collective-permute-start | bytes 1572872 | tf_op jit(solution)/shard_map/ppermute | solution.py:243
  23.4 2.5 %collective-permute-start.9 = (bf16[64,1024]{1,0:T(8,128)(2,1)S(1)}, bf16[64,1024]{1,0:T(8,128)(2,1)S(1)}, u32[]{:S(2)}, u32[]{:S(2)}) collective-permute-start(bf16[64,1024]{1,0:T(8,128)(2,1)S(1)} %broadcast_select_fusion), channel_id=1, source_target_pairs={{0,24},{1,9},{2,26},{3,11},{4,28},{5,13},{6,30},{7,15},{8,0},{9,17... | collective-permute-start | bytes 393224 | tf_op jit(solution)/shard_map/ppermute | solution.py:198
  26.0 10.8 %collective-permute-done.6.refs_6_ = bf16[256,1024]{1,0:T(8,128)(2,1)} collective-permute-done((bf16[256,1024]{1,0:T(8,128)(2,1)S(1)}, bf16[256,1024]{1,0:T(8,128)(2,1)}, u32[]{:S(2)}, u32[]{:S(2)}) %collective-permute-start.6) | collective-permute-done | bytes 524320 | tf_op jit(solution)/shard_map/ppermute | solution.py:242
  36.8 3.2 %collective-permute-start.10 = (bf16[128,1024]{1,0:T(8,128)(2,1)S(1)}, bf16[128,1024]{1,0:T(8,128)(2,1)S(1)}, u32[]{:S(2)}, u32[]{:S(2)}) collective-permute-start(bf16[128,1024]{1,0:T(8,128)(2,1)S(1)} %get-tuple-element.83), channel_id=1, source_target_pairs={{0,28},{1,29},{2,30},{3,31},{4,0},{5,1},{6,2},{7,3},{8,4},{9,5},{1... | collective-permute-start | bytes 786440 | tf_op jit(solution)/shard_map/ppermute | solution.py:198
  40.0 0.8 copy.33.refs_17_
  40.7 0.9 and_convert_fusion.refs_15_
  41.6 1.6 %collective-permute-done.10.refs_12_ = bf16[128,1024]{1,0:T(8,128)(2,1)S(1)} collective-permute-done((bf16[128,1024]{1,0:T(8,128)(2,1)S(1)}, bf16[128,1024]{1,0:T(8,128)(2,1)S(1)}, u32[]{:S(2)}, u32[]{:S(2)}) %collective-permute-start.10) | collective-permute-done | bytes 262176 | tf_op jit(solution)/shard_map/ppermute | solution.py:198
  43.3 4.5 %collective-permute-done.11.refs_13_ = bf16[128,1024]{1,0:T(8,128)(2,1)S(1)} collective-permute-done((bf16[128,1024]{1,0:T(8,128)(2,1)S(1)}, bf16[128,1024]{1,0:T(8,128)(2,1)S(1)}, u32[]{:S(2)}, u32[]{:S(2)}) %collective-permute-start.11) | collective-permute-done | bytes 262176 | tf_op jit(solution)/shard_map/ppermute | solution.py:198
  47.8 0.7 copy-done.15
  48.5 17.5 %shard_map.110 = (bf16[512,1024]{1,0:T(8,128)(2,1)}, bf16[512,1024]{1,0:T(8,128)(2,1)}, bf16[256,1024]{1,0:T(8,128)(2,1)}, bf16[256,1024]{1,0:T(8,128)(2,1)}, bf...) custom-call(s32[1]{0:T(128)} %bitcast.half_ref, ...), custom_call_target="tpu_custom_call" | custom-call | flops 2013265920 | bytes 10485760 | tf_op jit(solution)/shard_map/pallas_call | solution.py:168
  66.1 1.4 %collective-permute-start.17 = (f32[16,128]{1,0:T(8,128)}, f32[16,128]{1,0:T(8,128)S(1)}, u32[]{:S(2)}, u32[]{:S(2)}) collective-permute-start(f32[16,128]{1,0:T(8,128)} %get-tuple-element.45), channel_id=1, source_target_pairs={{0,8},{1,9},{2,10},{3,11},{4,12},{5,13},{6,14},{7,15},{8,0},{9,1},... | collective-permute-start | bytes 24584 | tf_op jit(solution)/shard_map/ppermute | solution.py:322
  67.6 2.1 %collective-permute-start.18 = (f32[16,128]{1,0:T(8,128)}, f32[16,128]{1,0:T(8,128)S(1)}, u32[]{:S(2)}, u32[]{:S(2)}) collective-permute-start(f32[16,128]{1,0:T(8,128)} %get-tuple-element.45), channel_id=1, source_target_pairs={{0,12},{1,13},{2,14},{3,15},{4,8},{5,9},{6,10},{7,11},{8,4},{9,5},... | collective-permute-start | bytes 24584 | tf_op jit(solution)/shard_map/ppermute | solution.py:322
  69.7 2.7 %collective-permute-start.14 = (bf16[128,1024]{1,0:T(8,128)(2,1)}, bf16[128,1024]{1,0:T(8,128)(2,1)S(1)}, u32[]{:S(2)}, u32[]{:S(2)}) collective-permute-start(bf16[128,1024]{1,0:T(8,128)(2,1)} %get-tuple-element.43), channel_id=1, source_target_pairs={{0,28},{1,29},{2,30},{3,31},{4,0},{5,1},{6,2},{7,3},{8,4},{9,5},{1... | collective-permute-start | bytes 786440 | tf_op jit(solution)/shard_map/ppermute | solution.py:198
  72.4 1.1 slice_bitcast_fusion.2
  73.5 3.4 %collective-permute-start.27 = (bf16[256,1024]{1,0:T(8,128)(2,1)}, bf16[256,1024]{1,0:T(8,128)(2,1)S(1)}, u32[]{:S(2)}, u32[]{:S(2)}) collective-permute-start(bf16[256,1024]{1,0:T(8,128)(2,1)} %get-tuple-element.55), channel_id=1, source_target_pairs={{1,2},{2,1},{3,4},{4,3},{5,6},{6,5},{7,8},{8,7},{9,10},{10,9},{11,... | collective-permute-start | bytes 1572872 | tf_op jit(solution)/shard_map/ppermute | solution.py:328
  77.0 1.3 collective-permute-start.31
  78.4 3.2 %collective-permute-done.15 = bf16[64,1024]{1,0:T(8,128)(2,1)S(1)} collective-permute-done((bf16[64,1024]{1,0:T(8,128)(2,1)S(1)}, bf16[64,1024]{1,0:T(8,128)(2,1)S(1)}, u32[]{:S(2)}, u32[]{:S(2)}) %collective-permute-start.15) | collective-permute-done | bytes 131104 | tf_op jit(solution)/shard_map/ppermute | solution.py:198
  81.5 5.4 %collective-permute-start.21 = (f32[16,128]{1,0:T(8,128)S(1)}, f32[16,128]{1,0:T(8,128)S(1)}, u32[]{:S(2)}, u32[]{:S(2)}) collective-permute-start(f32[16,128]{1,0:T(8,128)S(1)} %add_add_fusion.2), channel_id=1, source_target_pairs={{0,16},{1,17},{2,18},{3,19},{4,20},{5,21},{6,22},{7,23},{8,24},{9,... | collective-permute-start | bytes 24584 | tf_op jit(solution)/shard_map/ppermute | solution.py:322
  86.9 1.3 collective-permute-start.23
  88.3 1.9 %collective-permute-start.12 = (bf16[512,1024]{1,0:T(8,128)(2,1)}, bf16[512,1024]{1,0:T(8,128)(2,1)S(1)}, u32[]{:S(2)}, u32[]{:S(2)}) collective-permute-start(bf16[512,1024]{1,0:T(8,128)(2,1)} %get-tuple-element.40), channel_id=1, source_target_pairs={{0,1},{1,0},{2,3},{3,2},{4,5},{5,4},{6,7},{7,6},{8,9},{9,8},{10,11... | collective-permute-start | bytes 3145736 | tf_op jit(solution)/shard_map/ppermute | solution.py:198
  90.3 7.8 %collective-permute-done.22 = f32[16,128]{1,0:T(8,128)S(1)} collective-permute-done((f32[16,128]{1,0:T(8,128)S(1)}, f32[16,128]{1,0:T(8,128)S(1)}, u32[]{:S(2)}, u32[]{:S(2)}) %collective-permute-start.22) | collective-permute-done | bytes 8224 | tf_op jit(solution)/shard_map/ppermute | solution.py:322
  98.1 7.5 %collective-permute-start.19 = (bf16[64,1024]{1,0:T(8,128)(2,1)S(1)}, bf16[64,1024]{1,0:T(8,128)(2,1)S(1)}, u32[]{:S(2)}, u32[]{:S(2)}) collective-permute-start(bf16[64,1024]{1,0:T(8,128)(2,1)S(1)} %get-tuple-element.79), channel_id=1, source_target_pairs={{0,8},{1,9},{2,10},{3,11},{4,12},{5,13},{6,14},{7,15},{8,16},{9,17... | collective-permute-start | bytes 393224 | tf_op jit(solution)/shard_map/ppermute | solution.py:198
  105.8 6.6 %collective-permute-done.19 = bf16[64,1024]{1,0:T(8,128)(2,1)S(1)} collective-permute-done((bf16[64,1024]{1,0:T(8,128)(2,1)S(1)}, bf16[64,1024]{1,0:T(8,128)(2,1)S(1)}, u32[]{:S(2)}, u32[]{:S(2)}) %collective-permute-start.19) | collective-permute-done | bytes 131104 | tf_op jit(solution)/shard_map/ppermute | solution.py:198
  112.4 1.2 collective-permute-done.20
  113.7 0.5 collective-permute-start.24
  114.2 1.2 collective-permute-start.28
  115.5 2.5 %collective-permute-start.29 = (f32[16,128]{1,0:T(8,128)S(1)}, f32[16,128]{1,0:T(8,128)S(1)}, u32[]{:S(2)}, u32[]{:S(2)}) collective-permute-start(f32[16,128]{1,0:T(8,128)S(1)} %add_add_fusion.1), channel_id=1, source_target_pairs={{0,64},{32,96},{64,0},{96,32},{128,192},{160,224},{192,128},{224,1... | collective-permute-start | bytes 24584 | tf_op jit(solution)/shard_map/ppermute | solution.py:322
  118.3 0.5 collective-permute-start.25
  118.9 0.7 collective-permute-done.29
  119.5 1.8 %collective-permute-start.26 = (bf16[2,8,1024]{2,1,0:T(8,128)(2,1)S(1)}, bf16[2,8,1024]{2,1,0:T(8,128)(2,1)S(1)}, u32[]{:S(2)}, u32[]{:S(2)}) collective-permute-start(bf16[2,8,1024]{2,1,0:T(8,128)(2,1)S(1)} %get-tuple-element.75), channel_id=1, source_target_pairs={{0,3},{1,2},{2,1},{3,0},{4,7},{5,6},{6,5},{7,4},{8,11},{9,10},{10,... | collective-permute-start | bytes 98312 | tf_op jit(solution)/shard_map/ppermute | solution.py:198
  121.7 1.4 %collective-permute-done.26 = bf16[2,8,1024]{2,1,0:T(8,128)(2,1)S(1)} collective-permute-done((bf16[2,8,1024]{2,1,0:T(8,128)(2,1)S(1)}, bf16[2,8,1024]{2,1,0:T(8,128)(2,1)S(1)}, u32[]{:S(2)}, u32[]{:S(2)}) %collective-permute-start.26) | collective-permute-done | bytes 32800 | tf_op jit(solution)/shard_map/ppermute | solution.py:198
  123.0 2.5 %collective-permute-start.32 = (f32[16,128]{1,0:T(8,128)S(1)}, f32[16,128]{1,0:T(8,128)S(1)}, u32[]{:S(2)}, u32[]{:S(2)}) collective-permute-start(f32[16,128]{1,0:T(8,128)S(1)} %add_add_fusion), channel_id=1, source_target_pairs={{0,128},{1,129},{2,130},{3,131},{4,132},{5,133},{6,134},{7,135},{8... | collective-permute-start | bytes 24584 | tf_op jit(solution)/shard_map/ppermute | solution.py:354
  125.5 1.6 %collective-permute-start.33 = (f32[16,128]{1,0:T(8,128)S(1)}, f32[16,128]{1,0:T(8,128)S(1)}, u32[]{:S(2)}, u32[]{:S(2)}) collective-permute-start(f32[16,128]{1,0:T(8,128)S(1)} %add_add_fusion), channel_id=1, source_target_pairs={{0,1},{1,0},{2,3},{3,2},{4,5},{5,4},{6,7},{7,6},{8,9},{9,8},{10,11... | collective-permute-start | bytes 24584 | tf_op jit(solution)/shard_map/ppermute | solution.py:198
  127.9 3.8 %collective-permute-done.34 = f32[16,128]{1,0:T(8,128)S(1)} collective-permute-done((f32[16,128]{1,0:T(8,128)S(1)}, f32[16,128]{1,0:T(8,128)S(1)}, u32[]{:S(2)}, u32[]{:S(2)}) %collective-permute-start.34) | collective-permute-done | bytes 8224 | tf_op jit(solution)/shard_map/ppermute | solution.py:356
  131.8 0.7 slice.97
  133.0 1.0 pad_maximum_fusion.2
  134.1 0.9 maximum_select_fusion.1
  135.0 0.9 maximum_select_fusion
  (117 shorter events, 4.5 us)
Async XLA Ops:
  2.2 8.6 %collective-permute-start = (bf16[2,8,1024]{2,1,0:T(8,128)(2,1)S(1)}, bf16[2,8,1024]{2,1,0:T(8,128)(2,1)S(1)}, u32[]{:S(2)}, u32[]{:S(2)}) collective-permute-start(bf16[2,8,1024]{2,1,0:T(8,128)(2,1)S(1)} %get-tuple-element.86), channel_id=1, source_target_pairs={{0,1},{1,0},{2,3},{3,2},{4,5},{5,4},{6,7},{7,6},{8,9},{9,8},{10,11... | collective-permute-start | bytes 98312 | tf_op jit(solution)/shard_map/ppermute | solution.py:198
  5.5 5.3 %collective-permute-start.2 = (bf16[2,8,1024]{2,1,0:T(8,128)(2,1)S(1)}, bf16[2,8,1024]{2,1,0:T(8,128)(2,1)S(1)}, u32[]{:S(2)}, u32[]{:S(2)}) collective-permute-start(bf16[2,8,1024]{2,1,0:T(8,128)(2,1)S(1)} %get-tuple-element.86), channel_id=1, source_target_pairs={{0,3},{1,2},{2,1},{3,0},{4,7},{5,6},{6,5},{7,4},{8,11},{9,10},{10,... | collective-permute-start | bytes 98312 | tf_op jit(solution)/shard_map/ppermute | solution.py:198
  5.5 5.3 %collective-permute-start.1 = (bf16[2,8,1024]{2,1,0:T(8,128)(2,1)S(1)}, bf16[2,8,1024]{2,1,0:T(8,128)(2,1)S(1)}, u32[]{:S(2)}, u32[]{:S(2)}) collective-permute-start(bf16[2,8,1024]{2,1,0:T(8,128)(2,1)S(1)} %get-tuple-element.85), channel_id=1, source_target_pairs={{0,2},{1,3},{2,0},{3,1},{4,6},{5,7},{6,4},{7,5},{8,10},{9,11},{10,... | collective-permute-start | bytes 98312 | tf_op jit(solution)/shard_map/ppermute | solution.py:198
  7.0 2.7 %copy-start.9 = (f32[16,13,13]{2,0,1:T(8,128)S(1)}, f32[16,13,13]{2,0,1:T(8,128)}, u32[]{:S(2)}) copy-start(f32[16,13,13]{2,0,1:T(8,128)} %param.13) | copy-start | bytes 32452
  10.9 36.9 %copy-start.1 = (bf16[2,32,1024]{2,1,0:T(8,128)(2,1)}, bf16[2,32,1024]{2,1,0:T(8,128)(2,1)S(1)}, u32[]{:S(2)}) copy-start(bf16[2,32,1024]{2,1,0:T(8,128)(2,1)S(1)} %pad_maximum_fusion.8) | copy-start | bytes 393220
  10.9 9.2 %collective-permute-start.5 = (bf16[64,1024]{1,0:T(8,128)(2,1)S(1)}, bf16[64,1024]{1,0:T(8,128)(2,1)S(1)}, u32[]{:S(2)}, u32[]{:S(2)}) collective-permute-start(bf16[64,1024]{1,0:T(8,128)(2,1)S(1)} %bitcast.102), channel_id=1, source_target_pairs={{0,8},{1,9},{2,10},{3,11},{4,12},{5,13},{6,14},{7,15},{8,16},{9,17... | collective-permute-start | bytes 393224 | tf_op jit(solution)/shard_map/ppermute | solution.py:198
  12.2 11.2 %collective-permute-start.8 = (bf16[64,1024]{1,0:T(8,128)(2,1)S(1)}, bf16[64,1024]{1,0:T(8,128)(2,1)S(1)}, u32[]{:S(2)}, u32[]{:S(2)}) collective-permute-start(bf16[64,1024]{1,0:T(8,128)(2,1)S(1)} %bitcast.103), channel_id=1, source_target_pairs={{0,24},{1,25},{2,26},{3,27},{4,28},{5,29},{6,30},{7,31},{8,0},{9,1... | collective-permute-start | bytes 393224 | tf_op jit(solution)/shard_map/ppermute | solution.py:198
  15.3 21.4 %collective-permute-start.6 = (bf16[256,1024]{1,0:T(8,128)(2,1)S(1)}, bf16[256,1024]{1,0:T(8,128)(2,1)}, u32[]{:S(2)}, u32[]{:S(2)}) collective-permute-start(bf16[256,1024]{1,0:T(8,128)(2,1)S(1)} %pad_maximum_fusion.3), channel_id=1, source_target_pairs={{1,2},{2,1},{3,4},{4,3},{5,6},{6,5},{7,8},{8,7},{9,10},{10,9},{11,... | collective-permute-start | bytes 1572872 | tf_op jit(solution)/shard_map/ppermute | solution.py:242
  19.5 23.8 %collective-permute-start.3 = (bf16[256,1024]{1,0:T(8,128)(2,1)S(1)}, bf16[256,1024]{1,0:T(8,128)(2,1)}, u32[]{:S(2)}, u32[]{:S(2)}) collective-permute-start(bf16[256,1024]{1,0:T(8,128)(2,1)S(1)} %pad_maximum_fusion.3), channel_id=1, source_target_pairs={{0,1},{1,0},{2,3},{3,2},{4,5},{5,4},{6,7},{7,6},{8,9},{9,8},{10,11... | collective-permute-start | bytes 1572872 | tf_op jit(solution)/shard_map/ppermute | solution.py:198
  19.6 23.7 %collective-permute-start.4 = (bf16[256,1024]{1,0:T(8,128)(2,1)S(1)}, bf16[256,1024]{1,0:T(8,128)(2,1)}, u32[]{:S(2)}, u32[]{:S(2)}) collective-permute-start(bf16[256,1024]{1,0:T(8,128)(2,1)S(1)} %pad_maximum_fusion.5), channel_id=1, source_target_pairs={{0,1},{1,0},{2,3},{3,2},{4,5},{5,4},{6,7},{7,6},{8,9},{9,8},{10,11... | collective-permute-start | bytes 1572872 | tf_op jit(solution)/shard_map/ppermute | solution.py:198
  20.1 27.7 %copy-start.2 = (bf16[64,1024]{1,0:T(8,128)(2,1)}, bf16[64,1024]{1,0:T(8,128)(2,1)S(1)}, u32[]{:S(2)}) copy-start(bf16[64,1024]{1,0:T(8,128)(2,1)S(1)} %collective-permute-done.5.refs_10_) | copy-start | bytes 393220
  20.1 23.2 %collective-permute-start.7 = (bf16[256,1024]{1,0:T(8,128)(2,1)S(1)}, bf16[256,1024]{1,0:T(8,128)(2,1)}, u32[]{:S(2)}, u32[]{:S(2)}) collective-permute-start(bf16[256,1024]{1,0:T(8,128)(2,1)S(1)} %pad_maximum_fusion.4), channel_id=1, source_target_pairs={{1,3},{2,0},{3,5},{4,2},{5,7},{6,4},{7,9},{8,6},{9,11},{10,8},{11,... | collective-permute-start | bytes 1572872 | tf_op jit(solution)/shard_map/ppermute | solution.py:243
  23.4 24.3 %copy-start.3 = (bf16[64,1024]{1,0:T(8,128)(2,1)}, bf16[64,1024]{1,0:T(8,128)(2,1)S(1)}, u32[]{:S(2)}) copy-start(bf16[64,1024]{1,0:T(8,128)(2,1)S(1)} %collective-permute-done.8.refs_9_) | copy-start | bytes 393220
  23.4 16.5 %collective-permute-start.9 = (bf16[64,1024]{1,0:T(8,128)(2,1)S(1)}, bf16[64,1024]{1,0:T(8,128)(2,1)S(1)}, u32[]{:S(2)}, u32[]{:S(2)}) collective-permute-start(bf16[64,1024]{1,0:T(8,128)(2,1)S(1)} %broadcast_select_fusion), channel_id=1, source_target_pairs={{0,24},{1,9},{2,26},{3,11},{4,28},{5,13},{6,30},{7,15},{8,0},{9,17... | collective-permute-start | bytes 393224 | tf_op jit(solution)/shard_map/ppermute | solution.py:198
  36.8 6.5 %collective-permute-start.10 = (bf16[128,1024]{1,0:T(8,128)(2,1)S(1)}, bf16[128,1024]{1,0:T(8,128)(2,1)S(1)}, u32[]{:S(2)}, u32[]{:S(2)}) collective-permute-start(bf16[128,1024]{1,0:T(8,128)(2,1)S(1)} %get-tuple-element.83), channel_id=1, source_target_pairs={{0,28},{1,29},{2,30},{3,31},{4,0},{5,1},{6,2},{7,3},{8,4},{9,5},{1... | collective-permute-start | bytes 786440 | tf_op jit(solution)/shard_map/ppermute | solution.py:198
  39.9 7.8 %copy-start.16 = (bf16[64,1024]{1,0:T(8,128)(2,1)}, bf16[64,1024]{1,0:T(8,128)(2,1)S(1)}, u32[]{:S(2)}) copy-start(bf16[64,1024]{1,0:T(8,128)(2,1)S(1)} %collective-permute-done.9.refs_11_) | copy-start | bytes 393220
  39.9 7.8 %collective-permute-start.11 = (bf16[128,1024]{1,0:T(8,128)(2,1)S(1)}, bf16[128,1024]{1,0:T(8,128)(2,1)S(1)}, u32[]{:S(2)}, u32[]{:S(2)}) collective-permute-start(bf16[128,1024]{1,0:T(8,128)(2,1)S(1)} %get-tuple-element.38), channel_id=1, source_target_pairs={{0,4},{1,5},{2,6},{3,7},{4,8},{5,9},{6,10},{7,11},{8,12},{9,13},{1... | collective-permute-start | bytes 786440 | tf_op jit(solution)/shard_map/ppermute | solution.py:198
  43.2 4.5 %copy-start.14 = (bf16[128,1024]{1,0:T(8,128)(2,1)}, bf16[128,1024]{1,0:T(8,128)(2,1)S(1)}, u32[]{:S(2)}) copy-start(bf16[128,1024]{1,0:T(8,128)(2,1)S(1)} %collective-permute-done.10.refs_12_) | copy-start | bytes 786436
  66.0 7.5 %copy-start.17 = (bf16[64,1024]{1,0:T(8,128)(2,1)S(1)}, bf16[64,1024]{1,0:T(8,128)(2,1)}, u32[]{:S(2)}) copy-start(bf16[64,1024]{1,0:T(8,128)(2,1)} %get-tuple-element.44) | copy-start | bytes 393220
  66.0 11.0 %copy-start.13 = (bf16[256,1024]{1,0:T(8,128)(2,1)S(1)}, bf16[256,1024]{1,0:T(8,128)(2,1)}, u32[]{:S(2)}) copy-start(bf16[256,1024]{1,0:T(8,128)(2,1)} %get-tuple-element.60) | copy-start | bytes 1572868
  66.0 12.3 %copy-start.12 = (f32[16,128]{1,0:T(8,128)S(1)}, f32[16,128]{1,0:T(8,128)}, u32[]{:S(2)}) copy-start(f32[16,128]{1,0:T(8,128)} %get-tuple-element.45) | copy-start | bytes 24580
  66.0 22.2 %copy-start.7 = (bf16[64,1024]{1,0:T(8,128)(2,1)S(1)}, bf16[64,1024]{1,0:T(8,128)(2,1)}, u32[]{:S(2)}) copy-start(bf16[64,1024]{1,0:T(8,128)(2,1)} %get-tuple-element.48) | copy-start | bytes 393220
  66.0 22.2 %copy-start.8 = (bf16[64,1024]{1,0:T(8,128)(2,1)S(1)}, bf16[64,1024]{1,0:T(8,128)(2,1)}, u32[]{:S(2)}) copy-start(bf16[64,1024]{1,0:T(8,128)(2,1)} %get-tuple-element.50) | copy-start | bytes 393220
  66.0 47.6 %copy-start.4 = (bf16[64,1024]{1,0:T(8,128)(2,1)S(1)}, bf16[64,1024]{1,0:T(8,128)(2,1)}, u32[]{:S(2)}) copy-start(bf16[64,1024]{1,0:T(8,128)(2,1)} %get-tuple-element.41) | copy-start | bytes 393220
  66.0 7.4 %collective-permute-start.16 = (f32[16,128]{1,0:T(8,128)}, f32[16,128]{1,0:T(8,128)S(1)}, u32[]{:S(2)}, u32[]{:S(2)}) collective-permute-start(f32[16,128]{1,0:T(8,128)} %get-tuple-element.45), channel_id=1, source_target_pairs={{0,4},{1,5},{2,6},{3,7},{4,0},{5,1},{6,2},{7,3},{8,12},{9,13},{10,... | collective-permute-start | bytes 24584 | tf_op jit(solution)/shard_map/ppermute | solution.py:322
  66.1 7.4 %collective-permute-start.17 = (f32[16,128]{1,0:T(8,128)}, f32[16,128]{1,0:T(8,128)S(1)}, u32[]{:S(2)}, u32[]{:S(2)}) collective-permute-start(f32[16,128]{1,0:T(8,128)} %get-tuple-element.45), channel_id=1, source_target_pairs={{0,8},{1,9},{2,10},{3,11},{4,12},{5,13},{6,14},{7,15},{8,0},{9,1},... | collective-permute-start | bytes 24584 | tf_op jit(solution)/shard_map/ppermute | solution.py:322
  67.6 9.4 %collective-permute-start.18 = (f32[16,128]{1,0:T(8,128)}, f32[16,128]{1,0:T(8,128)S(1)}, u32[]{:S(2)}, u32[]{:S(2)}) collective-permute-start(f32[16,128]{1,0:T(8,128)} %get-tuple-element.45), channel_id=1, source_target_pairs={{0,12},{1,13},{2,14},{3,15},{4,8},{5,9},{6,10},{7,11},{8,4},{9,5},... | collective-permute-start | bytes 24584 | tf_op jit(solution)/shard_map/ppermute | solution.py:322
  69.7 11.8 %collective-permute-start.13 = (bf16[128,1024]{1,0:T(8,128)(2,1)}, bf16[128,1024]{1,0:T(8,128)(2,1)S(1)}, u32[]{:S(2)}, u32[]{:S(2)}) collective-permute-start(bf16[128,1024]{1,0:T(8,128)(2,1)} %get-tuple-element.42), channel_id=1, source_target_pairs={{0,4},{1,5},{2,6},{3,7},{4,8},{5,9},{6,10},{7,11},{8,12},{9,13},{1... | collective-permute-start | bytes 786440 | tf_op jit(solution)/shard_map/ppermute | solution.py:198
  69.7 11.8 %collective-permute-start.14 = (bf16[128,1024]{1,0:T(8,128)(2,1)}, bf16[128,1024]{1,0:T(8,128)(2,1)S(1)}, u32[]{:S(2)}, u32[]{:S(2)}) collective-permute-start(bf16[128,1024]{1,0:T(8,128)(2,1)} %get-tuple-element.43), channel_id=1, source_target_pairs={{0,28},{1,29},{2,30},{3,31},{4,0},{5,1},{6,2},{7,3},{8,4},{9,5},{1... | collective-permute-start | bytes 786440 | tf_op jit(solution)/shard_map/ppermute | solution.py:198
  73.4 8.1 %collective-permute-start.15 = (bf16[64,1024]{1,0:T(8,128)(2,1)S(1)}, bf16[64,1024]{1,0:T(8,128)(2,1)S(1)}, u32[]{:S(2)}, u32[]{:S(2)}) collective-permute-start(bf16[64,1024]{1,0:T(8,128)(2,1)S(1)} %copy-done.17), channel_id=1, source_target_pairs={{0,8},{1,25},{2,10},{3,27},{4,12},{5,29},{6,14},{7,31},{8,16},{9,1... | collective-permute-start | bytes 393224 | tf_op jit(solution)/shard_map/ppermute | solution.py:198
  73.5 40.7 %collective-permute-start.27 = (bf16[256,1024]{1,0:T(8,128)(2,1)}, bf16[256,1024]{1,0:T(8,128)(2,1)S(1)}, u32[]{:S(2)}, u32[]{:S(2)}) collective-permute-start(bf16[256,1024]{1,0:T(8,128)(2,1)} %get-tuple-element.55), channel_id=1, source_target_pairs={{1,2},{2,1},{3,4},{4,3},{5,6},{6,5},{7,8},{8,7},{9,10},{10,9},{11,... | collective-permute-start | bytes 1572872 | tf_op jit(solution)/shard_map/ppermute | solution.py:328
  77.0 40.9 %collective-permute-start.31 = (bf16[256,1024]{1,0:T(8,128)(2,1)S(1)}, bf16[256,1024]{1,0:T(8,128)(2,1)S(1)}, u32[]{:S(2)}, u32[]{:S(2)}) collective-permute-start(bf16[256,1024]{1,0:T(8,128)(2,1)S(1)} %copy-done.13), channel_id=1, source_target_pairs={{3,1},{0,2},{5,3},{2,4},{7,5},{4,6},{9,7},{6,8},{11,9},{8,10},{13,... | collective-permute-start | bytes 1572872 | tf_op jit(solution)/shard_map/ppermute | solution.py:329
  78.3 39.8 %copy-start = (bf16[512,1024]{1,0:T(8,128)(2,1)S(1)}, bf16[512,1024]{1,0:T(8,128)(2,1)}, u32[]{:S(2)}) copy-start(bf16[512,1024]{1,0:T(8,128)(2,1)} %get-tuple-element.39) | copy-start | bytes 3145732
  81.5 6.8 %collective-permute-start.21 = (f32[16,128]{1,0:T(8,128)S(1)}, f32[16,128]{1,0:T(8,128)S(1)}, u32[]{:S(2)}, u32[]{:S(2)}) collective-permute-start(f32[16,128]{1,0:T(8,128)S(1)} %add_add_fusion.2), channel_id=1, source_target_pairs={{0,16},{1,17},{2,18},{3,19},{4,20},{5,21},{6,22},{7,23},{8,24},{9,... | collective-permute-start | bytes 24584 | tf_op jit(solution)/shard_map/ppermute | solution.py:322
  86.9 11.2 %collective-permute-start.22 = (f32[16,128]{1,0:T(8,128)S(1)}, f32[16,128]{1,0:T(8,128)S(1)}, u32[]{:S(2)}, u32[]{:S(2)}) collective-permute-start(f32[16,128]{1,0:T(8,128)S(1)} %add_add_fusion.2), channel_id=1, source_target_pairs={{0,2},{1,3},{2,0},{3,1},{4,6},{5,7},{6,4},{7,5},{8,10},{9,11},{10,... | collective-permute-start | bytes 24584 | tf_op jit(solution)/shard_map/ppermute | solution.py:322
  86.9 18.7 %collective-permute-start.23 = (f32[16,128]{1,0:T(8,128)S(1)}, f32[16,128]{1,0:T(8,128)S(1)}, u32[]{:S(2)}, u32[]{:S(2)}) collective-permute-start(f32[16,128]{1,0:T(8,128)S(1)} %add_add_fusion.2), channel_id=1, source_target_pairs={{0,18},{1,19},{2,16},{3,17},{4,22},{5,23},{6,20},{7,21},{8,26},{9,... | collective-permute-start | bytes 24584 | tf_op jit(solution)/shard_map/ppermute | solution.py:322
  88.3 44.1 %collective-permute-start.12 = (bf16[512,1024]{1,0:T(8,128)(2,1)}, bf16[512,1024]{1,0:T(8,128)(2,1)S(1)}, u32[]{:S(2)}, u32[]{:S(2)}) collective-permute-start(bf16[512,1024]{1,0:T(8,128)(2,1)} %get-tuple-element.40), channel_id=1, source_target_pairs={{0,1},{1,0},{2,3},{3,2},{4,5},{5,4},{6,7},{7,6},{8,9},{9,8},{10,11... | collective-permute-start | bytes 3145736 | tf_op jit(solution)/shard_map/ppermute | solution.py:198
  98.1 14.3 %collective-permute-start.19 = (bf16[64,1024]{1,0:T(8,128)(2,1)S(1)}, bf16[64,1024]{1,0:T(8,128)(2,1)S(1)}, u32[]{:S(2)}, u32[]{:S(2)}) collective-permute-start(bf16[64,1024]{1,0:T(8,128)(2,1)S(1)} %get-tuple-element.79), channel_id=1, source_target_pairs={{0,8},{1,9},{2,10},{3,11},{4,12},{5,13},{6,14},{7,15},{8,16},{9,17... | collective-permute-start | bytes 393224 | tf_op jit(solution)/shard_map/ppermute | solution.py:198
  105.6 8.0 %collective-permute-start.20 = (bf16[64,1024]{1,0:T(8,128)(2,1)S(1)}, bf16[64,1024]{1,0:T(8,128)(2,1)S(1)}, u32[]{:S(2)}, u32[]{:S(2)}) collective-permute-start(bf16[64,1024]{1,0:T(8,128)(2,1)S(1)} %get-tuple-element.78), channel_id=1, source_target_pairs={{0,24},{1,25},{2,26},{3,27},{4,28},{5,29},{6,30},{7,31},{8,0},{9,1... | collective-permute-start | bytes 393224 | tf_op jit(solution)/shard_map/ppermute | solution.py:198
  113.7 7.9 %collective-permute-start.24 = (bf16[2,8,1024]{2,1,0:T(8,128)(2,1)S(1)}, bf16[2,8,1024]{2,1,0:T(8,128)(2,1)S(1)}, u32[]{:S(2)}, u32[]{:S(2)}) collective-permute-start(bf16[2,8,1024]{2,1,0:T(8,128)(2,1)S(1)} %get-tuple-element.77), channel_id=1, source_target_pairs={{0,1},{1,0},{2,3},{3,2},{4,5},{5,4},{6,7},{7,6},{8,9},{9,8},{10,11... | collective-permute-start | bytes 98312 | tf_op jit(solution)/shard_map/ppermute | solution.py:198
  114.2 4.1 %collective-permute-start.28 = (f32[16,128]{1,0:T(8,128)S(1)}, f32[16,128]{1,0:T(8,128)S(1)}, u32[]{:S(2)}, u32[]{:S(2)}) collective-permute-start(f32[16,128]{1,0:T(8,128)S(1)} %add_add_fusion.1), channel_id=1, source_target_pairs={{0,32},{32,0},{64,96},{96,64},{128,160},{160,128},{192,224},{224,1... | collective-permute-start | bytes 24584 | tf_op jit(solution)/shard_map/ppermute | solution.py:322
  115.5 4.1 %collective-permute-start.29 = (f32[16,128]{1,0:T(8,128)S(1)}, f32[16,128]{1,0:T(8,128)S(1)}, u32[]{:S(2)}, u32[]{:S(2)}) collective-permute-start(f32[16,128]{1,0:T(8,128)S(1)} %add_add_fusion.1), channel_id=1, source_target_pairs={{0,64},{32,96},{64,0},{96,32},{128,192},{160,224},{192,128},{224,1... | collective-permute-start | bytes 24584 | tf_op jit(solution)/shard_map/ppermute | solution.py:322
  117.9 3.7 %collective-permute-start.30 = (f32[16,128]{1,0:T(8,128)S(1)}, f32[16,128]{1,0:T(8,128)S(1)}, u32[]{:S(2)}, u32[]{:S(2)}) collective-permute-start(f32[16,128]{1,0:T(8,128)S(1)} %add_add_fusion.1), channel_id=1, source_target_pairs={{0,96},{32,64},{64,32},{96,0},{128,224},{160,192},{192,160},{224,1... | collective-permute-start | bytes 24584 | tf_op jit(solution)/shard_map/ppermute | solution.py:322
  118.3 3.3 %collective-permute-start.25 = (bf16[2,8,1024]{2,1,0:T(8,128)(2,1)S(1)}, bf16[2,8,1024]{2,1,0:T(8,128)(2,1)S(1)}, u32[]{:S(2)}, u32[]{:S(2)}) collective-permute-start(bf16[2,8,1024]{2,1,0:T(8,128)(2,1)S(1)} %get-tuple-element.76), channel_id=1, source_target_pairs={{0,2},{1,3},{2,0},{3,1},{4,6},{5,7},{6,4},{7,5},{8,10},{9,11},{10,... | collective-permute-start | bytes 98312 | tf_op jit(solution)/shard_map/ppermute | solution.py:198
  119.5 3.5 %collective-permute-start.26 = (bf16[2,8,1024]{2,1,0:T(8,128)(2,1)S(1)}, bf16[2,8,1024]{2,1,0:T(8,128)(2,1)S(1)}, u32[]{:S(2)}, u32[]{:S(2)}) collective-permute-start(bf16[2,8,1024]{2,1,0:T(8,128)(2,1)S(1)} %get-tuple-element.75), channel_id=1, source_target_pairs={{0,3},{1,2},{2,1},{3,0},{4,7},{5,6},{6,5},{7,4},{8,11},{9,10},{10,... | collective-permute-start | bytes 98312 | tf_op jit(solution)/shard_map/ppermute | solution.py:198
  123.0 4.5 %collective-permute-start.32 = (f32[16,128]{1,0:T(8,128)S(1)}, f32[16,128]{1,0:T(8,128)S(1)}, u32[]{:S(2)}, u32[]{:S(2)}) collective-permute-start(f32[16,128]{1,0:T(8,128)S(1)} %add_add_fusion), channel_id=1, source_target_pairs={{0,128},{1,129},{2,130},{3,131},{4,132},{5,133},{6,134},{7,135},{8... | collective-permute-start | bytes 24584 | tf_op jit(solution)/shard_map/ppermute | solution.py:354
  125.5 2.4 %collective-permute-start.33 = (f32[16,128]{1,0:T(8,128)S(1)}, f32[16,128]{1,0:T(8,128)S(1)}, u32[]{:S(2)}, u32[]{:S(2)}) collective-permute-start(f32[16,128]{1,0:T(8,128)S(1)} %add_add_fusion), channel_id=1, source_target_pairs={{0,1},{1,0},{2,3},{3,2},{4,5},{5,4},{6,7},{7,6},{8,9},{9,8},{10,11... | collective-permute-start | bytes 24584 | tf_op jit(solution)/shard_map/ppermute | solution.py:198
  127.1 4.6 %collective-permute-start.34 = (f32[16,128]{1,0:T(8,128)S(1)}, f32[16,128]{1,0:T(8,128)S(1)}, u32[]{:S(2)}, u32[]{:S(2)}) collective-permute-start(f32[16,128]{1,0:T(8,128)S(1)} %add_add_fusion), channel_id=1, source_target_pairs={{0,129},{1,128},{2,131},{3,130},{4,133},{5,132},{6,135},{7,134},{8... | collective-permute-start | bytes 24584 | tf_op jit(solution)/shard_map/ppermute | solution.py:356
  (5 other events, 6.6 us)

commit v3 on v2

v3 whole, which is shorter than its diff:
```python
import functools
import math

import jax
import jax.numpy as jnp
from jax import lax
from jax.experimental import pallas as pl
from jax.experimental.pallas import tpu as pltpu
from jax.sharding import PartitionSpec as P

COARSE = 8
MASKED = -1e30
LANES = 128
SLOT = 16
PER_STEP = 2
BF16 = jnp.bfloat16
F32 = jnp.float32
OFFSETS = (0, 2, -2, 4, 1, 3, -1, -3)


def after(x, *done):
    return lax.optimization_barrier((x, *done))[0]


def mm(a, b, contract):
    return lax.dot_general(a, b, (contract, ((), ())), preferred_element_type=F32)


ROW_COL = ((1,), (0,))
ROW_ROW = ((1,), (1,))
COL_COL = ((0,), (0,))


def split_sum(x):
    lane = lax.broadcasted_iota(jnp.int32, x.shape, 1)
    high = x.astype(BF16).astype(F32)
    rest = x - high
    mid = rest.astype(BF16).astype(F32)
    low = rest - mid
    kept = jnp.where(lane < SLOT, high, jnp.where(lane < 2 * SLOT, mid, low))
    return jnp.where(lane < 3 * SLOT, kept, 0.0).astype(BF16)


def whole_sum(x):
    lane = lax.broadcasted_iota(jnp.int32, x.shape, 1)
    total = x + pltpu.roll(x, LANES - SLOT, 1) + pltpu.roll(x, LANES - 2 * SLOT, 1)
    return jnp.where(lane < SLOT, total, 0.0)


def resplit(x):
    total = whole_sum(x)
    return split_sum(total + pltpu.roll(total, SLOT, 1) + pltpu.roll(total, 2 * SLOT, 1))


def wide(x):
    return x.astype(F32)


def merge_kernel(half_ref, up_ref, down_ref, four_ref, up_odd_ref, down_odd_ref, up_out, down_out):
    block = up_ref.shape[0]
    across = wide(four_ref[...])
    upper = half_ref[0] == 0
    for ref, odd, far, out in (
        (up_ref, up_odd_ref, upper, up_out),
        (down_ref, down_odd_ref, jnp.logical_not(upper), down_out),
    ):
        total = wide(ref[...]) + wide(odd[block:]) + jnp.where(far, across, 0.0)
        out[: block - SLOT] = total[: block - SLOT].astype(BF16)
        for h in range(0, total.shape[1], LANES):
            out[block - SLOT :, h : h + LANES] = resplit(total[block - SLOT :, h : h + LANES])


def quad_kernel(here_ref, up_ref, down_ref, up_two_ref, down_two_ref, keep_out, *outs):
    block = here_ref.shape[0]
    total = wide(here_ref[...]) + wide(up_ref[:block]) + wide(down_ref[:block])
    total = total + wide(up_two_ref[...]) + wide(down_two_ref[...])
    part = (block - SLOT) // 2
    pieces = [
        jnp.concatenate(
            [total[j * COARSE : (j + 1) * COARSE], total[part + j * COARSE : part + (j + 1) * COARSE]],
            axis=0,
        )
        for j in range(4)
    ]
    tail = total[block - SLOT :]
    keep_out[: 2 * COARSE] = pieces[0]
    keep_out[2 * COARSE :] = tail
    bias = [resplit(tail[:, h : h + LANES]) for h in range(0, total.shape[1], LANES)]
    bias = jnp.concatenate(bias, axis=1)
    for piece, out in zip(pieces[1:], outs):
        out[: 2 * COARSE] = piece.astype(BF16)
        out[2 * COARSE :] = bias


def finish_kernel(half_ref, keep_ref, core_ref, side_ref, corner_ref, rows_out, bias_out):
    mine = keep_ref[...] + wide(side_ref[...])
    other = wide(core_ref[...]) + wide(corner_ref[...])
    first = half_ref[0] == 0
    low = jnp.where(first, mine, other)
    high = jnp.where(first, other, mine)
    rows_out[...] = jnp.concatenate([low[: 2 * COARSE], high[: 2 * COARSE]], axis=1).astype(BF16)
    for i, x in enumerate((low, high)):
        packed = jnp.zeros((SLOT, LANES), F32)
        for h in range(LANES // SLOT):
            one = whole_sum(x[2 * COARSE :, h * LANES : (h + 1) * LANES])
            packed = packed + (pltpu.roll(one, h * SLOT, 1) if h else one)
        bias_out[i * SLOT : (i + 1) * SLOT] = packed


def small_call(kernel, half, arrays, out_shape):
    smem = [pl.BlockSpec(memory_space=pltpu.SMEM)] if half is not None else []
    args = [half] if half is not None else []
    return pl.pallas_call(
        kernel,
        in_specs=smem + [pl.BlockSpec(memory_space=pltpu.VMEM)] * len(arrays),
        out_specs=[pl.BlockSpec(memory_space=pltpu.VMEM)] * len(out_shape),
        out_shape=out_shape,
        cost_estimate=pl.CostEstimate(flops=10**6, bytes_accessed=10**6, transcendentals=0),
    )(*args, *arrays)


def attention_kernel(inv_scale, half_ref, *refs):
    (q_ref, k_ref, v_ref, g_ref, kv_par, qg_par, kv_own_out, kv_par_out) = refs[:8]
    coarse_refs = refs[8:14]
    row_hot_ref, key_hot_ref, table_ref, keep_ref = refs[14:18]
    own_ref, par_ref, own_out_ref, par_out_ref = refs[18:22]
    coarse_out = refs[22:28]
    rows = q_ref.shape[0]
    part = coarse_refs[0].shape[0] // 2
    places = [(r, a) for r in range(len(coarse_refs)) for a in range(0, coarse_refs[r].shape[0], 2 * part)]
    total = part * len(places)
    keep = keep_ref[...] > 0.0
    row_hot = row_hot_ref[...]
    key_hot = key_hot_ref[...]

    def one_head(head):
        lanes = slice(head * LANES, (head + 1) * LANES)
        q = jnp.concatenate([q_ref[:, lanes], qg_par[:rows, lanes]], axis=0)
        g_all = jnp.concatenate([g_ref[:, lanes], qg_par[rows:, lanes]], axis=0)
        g = jnp.where(keep, g_all.astype(F32), 0.0).astype(BF16)
        k_main = jnp.concatenate([coarse_refs[r][a : a + part, lanes] for r, a in places] + [k_ref[:, lanes], kv_par[:rows, lanes]], axis=0)
        v_main = jnp.concatenate([coarse_refs[r][a + part : a + 2 * part, lanes] for r, a in places] + [v_ref[:, lanes], kv_par[rows:, lanes]], axis=0)
        main = k_main.shape[0]
        hot_main = key_hot[:main]
        hot_own = key_hot[main : main + rows]
        hot_par = key_hot[main + rows :]
        row_bias = mm(row_hot, table_ref[head], ROW_COL).astype(BF16)
        q_ext = jnp.concatenate([q, row_bias], axis=1)
        k_main_ext = jnp.concatenate([k_main, hot_main], axis=1)
        k_own_ext = jnp.concatenate([kv_own_out[:rows, lanes], hot_own], axis=1)
        k_par_ext = jnp.concatenate([kv_par_out[:rows, lanes], hot_par], axis=1)
        v_own = kv_own_out[rows:, lanes]
        v_par = kv_par_out[rows:, lanes]

        def stacked(a, own, par, contract):
            return jnp.concatenate([mm(a[:rows], own, contract), mm(a[rows:], par, contract)], axis=0)

        to_two = inv_scale * math.log2(math.e)
        s_main = mm(q_ext, k_main_ext, ROW_ROW)
        s_out = stacked(q_ext, k_own_ext, k_par_ext, ROW_ROW)
        gp_main = mm(g, v_main, ROW_ROW)
        gp_out = stacked(g, v_own, v_par, ROW_ROW)
        yield
        peak = jnp.maximum(
            jnp.max(s_main, axis=1, keepdims=True), jnp.max(s_out, axis=1, keepdims=True)
        )
        e_main = jnp.exp2((s_main - peak) * to_two)
        e_out = jnp.exp2((s_out - peak) * to_two)
        yield
        norm = 1.0 / (
            jnp.sum(e_main, axis=1, keepdims=True) + jnp.sum(e_out, axis=1, keepdims=True)
        )
        p_main = e_main * norm
        p_out = e_out * norm
        pb_main = p_main.astype(BF16)
        pb_out = p_out.astype(BF16)
        mixed = mm(pb_main, v_main, ROW_COL) + stacked(pb_out, v_own, v_par, ROW_COL)
        yield
        attended = jnp.where(keep, mixed, 0.0).astype(BF16)
        delta = jnp.sum(g.astype(F32) * mixed, axis=1, keepdims=True)
        d_main = p_main * (gp_main - delta)
        d_out = p_out * (gp_out - delta)
        db_main = d_main.astype(BF16)
        db_out = d_out.astype(BF16)
        dl_main = (d_main - db_main.astype(F32)).astype(BF16)
        dl_out = (d_out - db_out.astype(F32)).astype(BF16)
        yield
        q_terms = mm(db_main, k_main_ext, ROW_COL) + stacked(db_out, k_own_ext, k_par_ext, ROW_COL)
        grad_q = (q_terms[:, :LANES] * inv_scale).astype(BF16)
        by_level = q_terms[:, LANES:] + (
            mm(dl_main, hot_main, ROW_COL) + stacked(dl_out, hot_own, hot_par, ROW_COL)
        )
        bias = lax.dot_general(
            row_hot.astype(F32),
            by_level,
            (COL_COL, ((), ())),
            precision=lax.Precision.HIGHEST,
            preferred_element_type=F32,
        )
        bias = split_sum(bias)
        yield
        gk_main = (mm(db_main, q, COL_COL) * inv_scale).astype(BF16)
        gv_main = mm(pb_main, g, COL_COL).astype(BF16)
        gk_own = (mm(db_out[:rows], q[:rows], COL_COL) * inv_scale).astype(BF16)
        gk_par = (mm(db_out[rows:], q[rows:], COL_COL) * inv_scale).astype(BF16)
        gv_own = mm(pb_out[:rows], g[:rows], COL_COL).astype(BF16)
        gv_par = mm(pb_out[rows:], g[rows:], COL_COL).astype(BF16)
        for place, ref in ((0, own_ref), (1, par_ref)):
            here = slice(place * rows, (place + 1) * rows)
            there = slice(total + place * rows, total + (place + 1) * rows)
            ref[0 * rows : 1 * rows, lanes] = attended[here]
            ref[1 * rows : 2 * rows, lanes] = grad_q[here]
            ref[2 * rows : 3 * rows, lanes] = gk_main[there]
            ref[3 * rows : 4 * rows, lanes] = gv_main[there]
        own_out_ref[:rows, lanes] = gk_own
        own_out_ref[rows:, lanes] = gv_own
        par_out_ref[:rows, lanes] = gk_par
        par_out_ref[rows:, lanes] = gv_par
        for j, (r, a) in enumerate(places):
            a = a // (2 * part) * (2 * part + SLOT)
            coarse_out[r][a : a + part, lanes] = gk_main[j * part : (j + 1) * part]
            coarse_out[r][a + part : a + 2 * part, lanes] = gv_main[j * part : (j + 1) * part]
            coarse_out[r][a + 2 * part : a + 2 * part + SLOT, lanes] = bias

    waiting = [one_head(head) for head in range(table_ref.shape[0])]
    running = []
    while waiting or running:
        if waiting and len(running) < 2:
            running.append(waiting.pop(0))
        for work in list(running):
            if next(work, running) is running:
                running.remove(work)


def call_kernel(inv_scale, half, full, pairs, coarse, tables, heads):
    rows, width = full[0].shape
    half_width = width // 2
    steps = heads // 2 // PER_STEP
    lanes = PER_STEP * LANES
    row_hot, key_hot, table, keep = tables

    def mine(h, half_ref):
        return (0, half_ref[0] * steps + h)

    def at(h, half_ref):
        return (0, h)

    def fixed(h, half_ref):
        return (0, 0)

    in_specs = (
        [pl.BlockSpec((rows, lanes), mine)] * 4
        + [pl.BlockSpec((2 * rows, lanes), at)] * 4
        + [pl.BlockSpec((x.shape[0], lanes), at) for x in coarse]
        + [
            pl.BlockSpec(row_hot.shape, fixed),
            pl.BlockSpec(key_hot.shape, fixed),
            pl.BlockSpec((PER_STEP, SLOT, LANES), lambda h, half_ref: (half_ref[0] * steps + h, 0, 0)),
            pl.BlockSpec(keep.shape, fixed),
        ]
    )
    blocks = [x.shape[0] // coarse[0].shape[0] for x in coarse]
    out_rows = [4 * rows] * 2 + [2 * rows] * 2 + [n * (coarse[0].shape[0] + SLOT) for n in blocks]
    out_shape = [jax.ShapeDtypeStruct((r, half_width), BF16) for r in out_rows]
    out_specs = [pl.BlockSpec((r, lanes), at) for r in out_rows]
    return pl.pallas_call(
        functools.partial(attention_kernel, inv_scale),
        grid_spec=pltpu.PrefetchScalarGridSpec(
            num_scalar_prefetch=1, grid=(steps,), in_specs=in_specs, out_specs=out_specs
        ),
        out_shape=out_shape,
        compiler_params=pltpu.CompilerParams(
            dimension_semantics=("arbitrary",), vmem_limit_bytes=60 * 1024 * 1024
        ),
        cost_estimate=pl.CostEstimate(
            flops=12 * 2 * rows * 640 * half_width,
            bytes_accessed=10 * 1024 * 1024,
            transcendentals=heads * rows * 640,
        ),
    )(half, *full, *pairs, *coarse, row_hot, key_hot, table, keep)


def shards(queries, keys, values, grad_out, valid, scale_ids, scale_bias):
    q, k, v, g = queries[0], keys[0], values[0], grad_out[0]
    rows, width = q.shape
    half_width = width // 2
    heads, levels = scale_bias.shape[:2]
    tiles = lax.axis_size("tile")
    depth = tiles // 4
    images = lax.axis_size("batch")
    tile = lax.axis_index("tile")
    core = tile % 2
    inv_scale = 1.0 / math.sqrt(width // heads)
    half = core.reshape(1)

    def send(x, target):
        return lax.ppermute(x, "tile", [(i, target(i)) for i in range(tiles)])

    def to_core(x):
        return send(x, lambda i: i ^ 1)

    def to_side(x):
        return send(x, lambda i: i ^ 2)

    def to_corner(x):
        return send(x, lambda i: i ^ 3)

    def to_depth(x, distance):
        return send(x, lambda i: (i + 4 * distance) % tiles)

    edge = [(i, (i + 1 if i % 2 else i - 1) % tiles) for i in range(tiles)]
    jump = [(i, (i + 2 if i % 2 else i - 2) % tiles) for i in range(tiles)]

    def cut(x, which):
        return lax.dynamic_slice_in_dim(x, which * half_width, half_width, 1)

    def small(which):
        start, size = (0, which * half_width), (COARSE, half_width)
        return jnp.stack([lax.dynamic_slice(k, start, size), lax.dynamic_slice(v, start, size)])

    small_mine, small_other = small(core), small(1 - core)
    first = [small_mine, to_core(small_other), to_side(small_mine), to_corner(small_other)]
    kv_other = jnp.concatenate([cut(k, 1 - core), cut(v, 1 - core)], axis=0)
    kv_mine = jnp.concatenate([cut(k, core), cut(v, core)], axis=0)
    qg_other = jnp.concatenate([cut(q, 1 - core), cut(g, 1 - core)], axis=0)
    first[1], first[3], kv_other = lax.optimization_barrier((first[1], first[3], kv_other))
    kv_own_out = lax.ppermute(kv_other, "tile", edge)
    group = jnp.concatenate(first, axis=1).reshape(-1, half_width)
    kv_mine, qg_other, group = lax.optimization_barrier((kv_mine, qg_other, group))
    kv_par_out = lax.ppermute(kv_mine, "tile", jump)
    kv_par = to_core(kv_other)
    qg_par = to_core(qg_other)
    up_two = to_depth(group, -2)
    down_two = to_depth(group, 2)
    up_odd = to_depth(jnp.concatenate([group, up_two], axis=0), -1)
    down_odd = to_depth(jnp.concatenate([group, down_two], axis=0), 1)
    far = jnp.where(core == 0, up_two, down_two)
    far, kv_own_out = lax.optimization_barrier((far, kv_own_out))
    four = send(far, lambda i: (i + (8 if i % 2 else -8)) % tiles)
    coarse = [group, up_two, down_two, four, up_odd, down_odd]

    valid_grid = valid[0].reshape(tiles, rows)
    scale_grid = scale_ids.reshape(tiles, rows)
    level_grid = jnp.where(valid_grid > 0, scale_grid, levels)
    inner = jnp.arange(rows, dtype=jnp.int32)
    fine_grid = jnp.where(inner[None, :] >= COARSE, level_grid, levels)
    near_grid = jnp.pad(fine_grid, ((1, 1), (0, 0)), constant_values=levels)
    partner = tile ^ 1
    outward = 2 * core - 1

    def line(grid, index):
        return lax.dynamic_index_in_dim(grid, index, 0, keepdims=False)

    z_here = tile // 4
    spots = jnp.stack([((z_here + d) % depth) * 4 + (j ^ (tile % 4)) for d in OFFSETS for j in range(4)])
    pick = (spots[:, None] == jnp.arange(tiles, dtype=jnp.int32)[None, :]).astype(F32)
    coarse_level = jnp.dot(
        pick, level_grid[:, :COARSE].astype(F32), precision=lax.Precision.HIGHEST
    ).astype(jnp.int32)
    key_level = jnp.concatenate(
        [
            coarse_level.reshape(-1),
            line(near_grid, tile + 1),
            line(near_grid, partner + 1),
            line(near_grid, tile + 1 + outward),
            line(near_grid, partner + 1 - outward),
        ]
    )
    column = jnp.arange(LANES, dtype=jnp.int32)
    key_hot = (
        (key_level[:, None] == (column % SLOT)[None, :]) & (column < 3 * SLOT)[None, :]
    ).astype(BF16)
    row_level = jnp.concatenate([line(scale_grid, tile), line(scale_grid, partner)])
    row_hot = (row_level[:, None] == jnp.arange(SLOT, dtype=jnp.int32)[None, :]).astype(BF16)
    keep = jnp.concatenate([line(valid_grid, tile), line(valid_grid, partner)]).astype(F32)[:, None]

    level_ids = jnp.arange(levels, dtype=jnp.int32)
    scaled = jnp.where(
        (level_ids[None, :] <= level_ids[:, None])[None], scale_bias / inv_scale, MASKED
    )
    scaled = jnp.pad(
        scaled,
        ((0, 0), (0, SLOT - levels), (0, SLOT - levels)),
        constant_values=MASKED,
    )
    parts = []
    rest = scaled
    for _ in range(3):
        piece = lax.reduce_precision(rest, 8, 7)
        parts.append(piece)
        rest = rest - piece
    table = jnp.pad(
        jnp.concatenate(parts, axis=2), ((0, 0), (0, 0), (0, LANES - 3 * SLOT))
    ).astype(BF16)

    results = call_kernel(
        inv_scale,
        half,
        (q, k, v, g),
        (kv_par, qg_par, kv_own_out, kv_par_out),
        coarse,
        (row_hot, key_hot, table, keep),
        heads,
    )
    own, par, own_out, par_out = results[:4]
    here, up_two, down_two, four, up_odd, down_odd = results[4:10]

    def joined(mine, other_half):
        return jnp.where(
            core == 0,
            jnp.concatenate([mine, other_half], axis=-1),
            jnp.concatenate([other_half, mine], axis=-1),
        )

    every = images * tiles

    def flipped(x, mask):
        return lax.ppermute(x, ("batch", "tile"), [(i, i ^ mask) for i in range(every)])

    block, columns = here.shape

    def like(count, dtype):
        return jax.ShapeDtypeStruct((count, columns), dtype)

    def beside(pairs):
        return [p for p in pairs if p[0] // 4 == p[1] // 4], [p for p in pairs if p[0] // 4 != p[1] // 4]

    edge_y, edge_z = beside(edge)
    jump_y, jump_z = beside([(b, a) for a, b in jump])
    jump_y, jump_z = jump_y + [(i, i ^ 1) for i, _ in jump_z], jump_z + [(i, i ^ 1) for i, _ in jump_y]
    middle = (tile % 4 == 1) | (tile % 4 == 2)
    other_y = lax.ppermute(own_out, "tile", edge_y)
    mine_y = lax.ppermute(par_out, "tile", jump_y)
    other = to_core(par)
    up_odd = to_depth(up_odd, 1)
    down_odd = to_depth(down_odd, -1)
    four = send(four, lambda i: (i + (-8 if i % 2 else 8)) % tiles)
    up_odd, down_odd, four, own_out, par_out, other_y = lax.optimization_barrier(
        (up_odd, down_odd, four, own_out, par_out, other_y)
    )
    up_two, down_two = small_call(
        merge_kernel, half, (up_two, down_two, four, up_odd, down_odd), [like(block, BF16)] * 2
    )
    own_out, par_out, up_two, down_two = lax.optimization_barrier((own_out, par_out, up_two, down_two))
    other_z = lax.ppermute(own_out, "tile", edge_z)
    mine_z = lax.ppermute(par_out, "tile", jump_z)
    up_two = to_depth(up_two, 2)
    down_two = to_depth(down_two, -2)
    up_two, down_two, mine_y, other = lax.optimization_barrier((up_two, down_two, mine_y, other))
    kept, *quad = small_call(
        quad_kernel,
        None,
        (here, up_odd, down_odd, up_two, down_two),
        [like(2 * COARSE + SLOT, F32)] + [like(2 * COARSE + SLOT, BF16)] * 3,
    )
    quad = [to_core(quad[0]), to_side(quad[1]), to_corner(quad[2])]
    attended = joined(own[:rows], other[:rows])
    grad_q = joined(own[rows : 2 * rows], other[rows : 2 * rows])
    *quad, other_z = lax.optimization_barrier((*quad, other_z))
    fine_other = wide(other[2 * rows :]) + wide(other_y) + wide(other_z)
    coarse_rows, bias = small_call(
        finish_kernel,
        half,
        (kept, *quad),
        [
            jax.ShapeDtypeStruct((2 * COARSE, width), BF16),
            jax.ShapeDtypeStruct((2 * SLOT, LANES), F32),
        ],
    )
    bias = sum([flipped(bias, m * tiles) for m in (1, 2, 3)], bias)
    bias, mine_z, attended, grad_q = lax.optimization_barrier((bias, mine_z, attended, grad_q))
    bias = bias + flipped(bias, 4 * tiles)
    fine_mine = wide(own[2 * rows :]) + wide(jnp.where(middle, mine_y, mine_z))
    fine = joined(fine_mine, fine_other).astype(BF16)
    grad_bias = (
        bias.reshape(2, SLOT, heads // 2, SLOT)
        .transpose(0, 2, 1, 3)
        .reshape(heads, SLOT, SLOT)[:, :levels, :levels]
    )

    coarse_rows = coarse_rows.reshape(2, COARSE, width)
    fine = fine.reshape(2, rows, width)
    grads = jnp.concatenate([coarse_rows, fine[:, COARSE:]], axis=1)
    return (attended[None], grad_q[None], grads[0][None], grads[1][None], grad_bias)


def solution(mesh):
    block = P("batch", "tile", None)
    return jax.shard_map(
        shards,
        mesh=mesh,
        in_specs=(block, block, block, block, P("batch", None), P(), P()),
        out_specs=(block, block, block, block, P()),
        check_vma=False,
    )
```

time: 136 us -> 120 us (0.88); the launches traced: 136 us -> 118 us
  starting transfers between devices: 61.4 us -> 44.7 us
  waiting for transfers between devices: 42.2 us -> 38.3 us
    ppermute x13 -> x8, waiting for transfers between devices: 12.6 us -> 2.07 us  [the longest x4 2.06 us: flipped(): lax.ppermute(x, ('batch', 'tile'), [(i, i ^ mask) for i in range(every)])]
    ppermute x20 -> x19, waiting for transfers between devices: 18.8 us -> 25.2 us  [send(): return lax.ppermute(x, 'tile', [(i, target(i)) for i in range(tiles)])]
    pallas_call x0 -> x3, Pallas kernels: none -> 6.3 us  [small_call(): pl.pallas_call(kernel, in_specs=smem + [pl.BlockSpec(memory_space=pltpu.V...]
    ppermute x13 -> x8, starting transfers between devices: 21.8 us -> 15.7 us  [the longest x4 5.89 us: flipped(): lax.ppermute(x, ('batch', 'tile'), [(i, i ^ mask) for i in range(every)])]
    ppermute x20 -> x19, starting transfers between devices: 32.2 us -> 26.1 us  [send(): return lax.ppermute(x, 'tile', [(i, target(i)) for i in range(tiles)])]
    pallas_call x1, Pallas kernels: 17.5 us -> 12.1 us  [call_kernel(): pl.pallas_call(functools.partial(attention_kernel, inv_scale), grid_spec=...]
    ppermute x1, starting transfers between devices: 3.34 us -> 0.79 us  [shards(): kv_par_out = lax.ppermute(kv_mine, 'tile', jump)]
    unnamed x40 -> x46, local copies, waits for them, and re-layouts: 0.79 us -> 3.22 us
  transfers between devices with their start and end apart: 35 -> 29, of which waited for: 12 -> 12; matrix products, arithmetic and copies ran while one was open for 6% -> 9% of each run, Pallas kernels for 0% -> 5%
where the time goes in v3:
time: 120 us; the launch traced here: 118 us
  starting transfers between devices  44.7 us (37%)
  waiting for transfers between devices  38.3 us (32%)
  Pallas kernels  18.4 us (15%)
  other arithmetic  7.64 us (6%)
  local copies, waits for them, and re-layouts  7.35 us (6%)
    ppermute x19, starting transfers between devices, send(): return lax.ppermute(x, 'tile', [(i, target(i)) for i in range(tiles)])  26.1 us
    ppermute x19, waiting for transfers between devices, send(): return lax.ppermute(x, 'tile', [(i, target(i)) for i in range(tiles)])  25.2 us
    pallas_call x1, Pallas kernels, call_kernel(): pl.pallas_call(functools.partial(attention_kernel, inv_scale), grid_spec=...  12.1 us
    ppermute x1, waiting for transfers between devices, shards(): kv_own_out = lax.ppermute(kv_other, 'tile', edge)  11.1 us
    pallas_call x3, Pallas kernels, small_call(): pl.pallas_call(kernel, in_specs=smem + [pl.BlockSpec(memory_space=pltpu.V...  6.3 us
    ppermute x4, starting transfers between devices, flipped(): lax.ppermute(x, ('batch', 'tile'), [(i, i ^ mask) for i in range(every)])  5.89 us
    ppermute x1, starting transfers between devices, shards(): other_y = lax.ppermute(own_out, 'tile', edge_y)  5.34 us
    unnamed x46, local copies, waits for them, and re-layouts  3.22 us
  transfers between devices with their start and end apart: 29, of which 12 were waited for; matrix products, arithmetic and copies ran while one was open for 9% of the time, Pallas kernels for 5%

profile of v3, /device:TPU:1, one launch (start us, length us, event | category | flops | bytes accessed | tf_op | source)
XLA Modules:
  0.0 117.7 jit_solution(7028463992207829835)
XLA Ops:
  0.7 0.8 constant_dynamic-slice_fusion.4
  1.4 2.8 %collective-permute-start.1 = (bf16[2,8,1024]{2,1,0:T(8,128)(2,1)S(1)}, bf16[2,8,1024]{2,1,0:T(8,128)(2,1)S(1)}, u32[]{:S(2)}, u32[]{:S(2)}) collective-permute-start(bf16[2,8,1024]{2,1,0:T(8,128)(2,1)S(1)} %pad_maximum_fusion.9), channel_id=1, source_target_pairs={{0,3},{1,2},{2,1},{3,0},{4,7},{5,6},{6,5},{7,4},{8,11},{9,10},{10,... | collective-permute-start | bytes 98312 | tf_op jit(solution)/shard_map/ppermute | solution.py:297
  4.2 0.7 collective-permute-start
  4.9 1.3 %collective-permute-start.3 = (bf16[2,8,1024]{2,1,0:T(8,128)(2,1)S(1)}, bf16[2,8,1024]{2,1,0:T(8,128)(2,1)S(1)}, u32[]{:S(2)}, u32[]{:S(2)}) collective-permute-start(bf16[2,8,1024]{2,1,0:T(8,128)(2,1)S(1)} %pad_maximum_fusion.10), channel_id=1, source_target_pairs={{0,2},{1,3},{2,0},{3,1},{4,6},{5,7},{6,4},{7,5},{8,10},{9,11},{10,... | collective-permute-start | bytes 98312 | tf_op jit(solution)/shard_map/ppermute | solution.py:297
  6.3 1.4 %dynamic-slice_bitcast_fusion.2 = (bf16[128,1024]{1,0:T(8,128)(2,1)S(1)}, bf16[128,1024]{1,0:T(8,128)(2,1)S(1)}, bf16[128,1024]{1,0:T(8,128)(2,1)S(1)}, bf16[128,1024]{1,0:T(8,128)(2,1)S(1)}) fusion(bf16[1,128,2048]{2,1,0:T(8,128)(2,1)} %param.9, s32[]{:T(128)S(6)} %select_n.258, s32[]{:T(128)S(6)} %select_n.257, bf16[1,128,2048]{2,1,0:T(8,128)(2,1)} %param.8), kind=kLoop, calls=%fused_computation.21 | loop fusion | bytes 2097160 | tf_op jit(solution)/shard_map/dynamic_slice | solution.py:315
  8.7 0.9 and_convert_fusion.refs_15_
  9.6 1.4 %collective-permute-start.6 = (bf16[64,1024]{1,0:T(8,128)(2,1)S(1)}, bf16[64,1024]{1,0:T(8,128)(2,1)S(1)}, u32[]{:S(2)}, u32[]{:S(2)}) collective-permute-start(bf16[64,1024]{1,0:T(8,128)(2,1)S(1)} %bitcast.84), channel_id=1, source_target_pairs={{0,8},{1,9},{2,10},{3,11},{4,12},{5,13},{6,14},{7,15},{8,16},{9,17... | collective-permute-start | bytes 393224 | tf_op jit(solution)/shard_map/ppermute | solution.py:297
  11.0 3.1 %collective-permute-start.5 = (bf16[64,1024]{1,0:T(8,128)(2,1)S(1)}, bf16[64,1024]{1,0:T(8,128)(2,1)S(1)}, u32[]{:S(2)}, u32[]{:S(2)}) collective-permute-start(bf16[64,1024]{1,0:T(8,128)(2,1)S(1)} %bitcast.85), channel_id=1, source_target_pairs={{0,24},{1,25},{2,26},{3,27},{4,28},{5,29},{6,30},{7,31},{8,0},{9,1... | collective-permute-start | bytes 393224 | tf_op jit(solution)/shard_map/ppermute | solution.py:297
  14.1 2.1 %collective-permute-start.7 = (bf16[256,1024]{1,0:T(8,128)(2,1)S(1)}, bf16[256,1024]{1,0:T(8,128)(2,1)S(1)}, u32[]{:S(2)}, u32[]{:S(2)}) collective-permute-start(bf16[256,1024]{1,0:T(8,128)(2,1)S(1)} %pad_maximum_fusion.3), channel_id=1, source_target_pairs={{0,31},{1,2},{2,1},{3,4},{4,3},{5,6},{6,5},{7,8},{8,7},{9,10},{10,... | collective-permute-start | bytes 1572872 | tf_op jit(solution)/shard_map/ppermute | solution.py:327
  16.2 0.7 fusion.9.refs_14_
  17.0 1.2 collective-permute-start.2
  18.2 0.8 collective-permute-start.8
  19.0 2.4 %collective-permute-done.5.refs_9_ = bf16[64,1024]{1,0:T(8,128)(2,1)S(1)} collective-permute-done((bf16[64,1024]{1,0:T(8,128)(2,1)S(1)}, bf16[64,1024]{1,0:T(8,128)(2,1)S(1)}, u32[]{:S(2)}, u32[]{:S(2)}) %collective-permute-start.5) | collective-permute-done | bytes 131104 | tf_op jit(solution)/shard_map/ppermute | solution.py:297
  21.5 0.9 collective-permute-start.11
  22.5 11.1 %collective-permute-done.7.refs_6_ = bf16[256,1024]{1,0:T(8,128)(2,1)S(1)} collective-permute-done((bf16[256,1024]{1,0:T(8,128)(2,1)S(1)}, bf16[256,1024]{1,0:T(8,128)(2,1)S(1)}, u32[]{:S(2)}, u32[]{:S(2)}) %collective-permute-start.7) | collective-permute-done | bytes 524320 | tf_op jit(solution)/shard_map/ppermute | solution.py:327
  33.6 2.1 %collective-permute-start.10 = (bf16[128,1024]{1,0:T(8,128)(2,1)S(1)}, bf16[128,1024]{1,0:T(8,128)(2,1)}, u32[]{:S(2)}, u32[]{:S(2)}) collective-permute-start(bf16[128,1024]{1,0:T(8,128)(2,1)S(1)} %get-tuple-element.121), channel_id=1, source_target_pairs={{0,28},{1,29},{2,30},{3,31},{4,0},{5,1},{6,2},{7,3},{8,4},{9,5},{1... | collective-permute-start | bytes 786440 | tf_op jit(solution)/shard_map/ppermute | solution.py:297
  35.9 0.8 copy.27.refs_17_
  36.7 0.7 fusion.11.refs_16_
  37.4 3.8 %collective-permute-done.10.refs_12_ = bf16[128,1024]{1,0:T(8,128)(2,1)} collective-permute-done((bf16[128,1024]{1,0:T(8,128)(2,1)S(1)}, bf16[128,1024]{1,0:T(8,128)(2,1)}, u32[]{:S(2)}, u32[]{:S(2)}) %collective-permute-start.10) | collective-permute-done | bytes 262176 | tf_op jit(solution)/shard_map/ppermute | solution.py:297
  41.2 1.3 %collective-permute-done.9.refs_11_ = bf16[64,1024]{1,0:T(8,128)(2,1)S(1)} collective-permute-done((bf16[64,1024]{1,0:T(8,128)(2,1)S(1)}, bf16[64,1024]{1,0:T(8,128)(2,1)S(1)}, u32[]{:S(2)}, u32[]{:S(2)}) %collective-permute-start.9) | collective-permute-done | bytes 131104 | tf_op jit(solution)/shard_map/ppermute | solution.py:297
  43.1 12.1 %shard_map.110 = (bf16[512,1024]{1,0:T(8,128)(2,1)}, bf16[512,1024]{1,0:T(8,128)(2,1)}, bf16[256,1024]{1,0:T(8,128)(2,1)}, bf16[256,1024]{1,0:T(8,128)(2,1)}, bf...) custom-call(s32[1]{0:T(128)} %bitcast.half_ref, ...), custom_call_target="tpu_custom_call" | custom-call | flops 2013265920 | bytes 10485760 | tf_op jit(solution)/shard_map/pallas_call | solution.py:266
  55.5 5.3 %collective-permute-start.15 = (bf16[256,1024]{1,0:T(8,128)(2,1)}, bf16[256,1024]{1,0:T(8,128)(2,1)}, u32[]{:S(2)}, u32[]{:S(2)}) collective-permute-start(bf16[256,1024]{1,0:T(8,128)(2,1)} %get-tuple-element.85), channel_id=1, source_target_pairs={{1,2},{2,1},{5,6},{6,5},{9,10},{10,9},{13,14},{14,13},{17,18},{18,... | collective-permute-start | bytes 1572872 | tf_op jit(solution)/shard_map/ppermute | solution.py:432
  60.9 3.7 %collective-permute-start.14 = (bf16[80,1024]{1,0:T(8,128)(2,1)}, bf16[80,1024]{1,0:T(8,128)(2,1)S(1)}, u32[]{:S(2)}, u32[]{:S(2)}) collective-permute-start(bf16[80,1024]{1,0:T(8,128)(2,1)} %get-tuple-element.64), channel_id=1, source_target_pairs={{0,8},{1,25},{2,10},{3,27},{4,12},{5,29},{6,14},{7,31},{8,16},{9,1... | collective-permute-start | bytes 491528 | tf_op jit(solution)/shard_map/ppermute | solution.py:297
  64.6 2.7 %collective-permute-start.13 = (bf16[160,1024]{1,0:T(8,128)(2,1)}, bf16[160,1024]{1,0:T(8,128)(2,1)S(1)}, u32[]{:S(2)}, u32[]{:S(2)}) collective-permute-start(bf16[160,1024]{1,0:T(8,128)(2,1)} %get-tuple-element.63), channel_id=1, source_target_pairs={{0,28},{1,29},{2,30},{3,31},{4,0},{5,1},{6,2},{7,3},{8,4},{9,5},{1... | collective-permute-start | bytes 983048 | tf_op jit(solution)/shard_map/ppermute | solution.py:297
  67.3 2.8 %collective-permute-done.14.four_ref = bf16[80,1024]{1,0:T(8,128)(2,1)S(1)} collective-permute-done((bf16[80,1024]{1,0:T(8,128)(2,1)}, bf16[80,1024]{1,0:T(8,128)(2,1)S(1)}, u32[]{:S(2)}, u32[]{:S(2)}) %collective-permute-start.14) | collective-permute-done | bytes 163872 | tf_op jit(solution)/shard_map/ppermute | solution.py:297
  70.1 1.8 %collective-permute-done.12.up_odd_ref.up_ref = bf16[160,1024]{1,0:T(8,128)(2,1)S(1)} collective-permute-done((bf16[160,1024]{1,0:T(8,128)(2,1)}, bf16[160,1024]{1,0:T(8,128)(2,1)S(1)}, u32[]{:S(2)}, u32[]{:S(2)}) %collective-permute-start.12) | collective-permute-done | bytes 327712 | tf_op jit(solution)/shard_map/ppermute | solution.py:297
  71.9 2.6 %collective-permute-done.13.down_odd_ref.down_ref = bf16[160,1024]{1,0:T(8,128)(2,1)S(1)} collective-permute-done((bf16[160,1024]{1,0:T(8,128)(2,1)}, bf16[160,1024]{1,0:T(8,128)(2,1)S(1)}, u32[]{:S(2)}, u32[]{:S(2)}) %collective-permute-start.13) | collective-permute-done | bytes 327712 | tf_op jit(solution)/shard_map/ppermute | solution.py:297
  74.6 0.7 copy-done.1
  75.3 2.4 %shard_map.111 = (bf16[80,1024]{1,0:T(8,128)(2,1)}, bf16[80,1024]{1,0:T(8,128)(2,1)}) custom-call(s32[1]{0:T(128)} %bitcast.half_ref, bf16[80,1024]{1,0:T(8,128)(2,1)} %get-tuple-element.71.up_ref, bf16[80,1024]{1,0:T(8,128)(2,1)} %get-tuple-element.72.down_ref, bf16[80,1024]{1,0:T(8,128)(2,1)} %copy-done.8, bf16[160,1024]{1,0:T(8,128)(2,1)} %copy-done, ...), custom_call_target="tpu_custom_call" | custom-call | flops 1000000 | bytes 1000000 | tf_op jit(solution)/shard_map/pallas_call | solution.py:113
  77.7 1.0 collective-permute-start.16
  78.7 2.6 %collective-permute-start.17 = (bf16[80,1024]{1,0:T(8,128)(2,1)}, bf16[80,1024]{1,0:T(8,128)(2,1)S(1)}, u32[]{:S(2)}, u32[]{:S(2)}) collective-permute-start(bf16[80,1024]{1,0:T(8,128)(2,1)} %get-tuple-element.77), channel_id=1, source_target_pairs={{0,24},{1,25},{2,26},{3,27},{4,28},{5,29},{6,30},{7,31},{8,0},{9,1... | collective-permute-start | bytes 491528 | tf_op jit(solution)/shard_map/ppermute | solution.py:297
  81.3 1.5 %collective-permute-start.23 = (bf16[256,1024]{1,0:T(8,128)(2,1)}, bf16[256,1024]{1,0:T(8,128)(2,1)}, u32[]{:S(2)}, u32[]{:S(2)}) collective-permute-start(bf16[256,1024]{1,0:T(8,128)(2,1)} %get-tuple-element.85), channel_id=1, source_target_pairs={{0,31},{3,4},{4,3},{7,8},{8,7},{11,12},{12,11},{15,16},{16,15},{19... | collective-permute-start | bytes 1572872 | tf_op jit(solution)/shard_map/ppermute | solution.py:445
  82.8 3.0 %collective-permute-start.27 = (bf16[256,1024]{1,0:T(8,128)(2,1)}, bf16[256,1024]{1,0:T(8,128)(2,1)}, u32[]{:S(2)}, u32[]{:S(2)}) collective-permute-start(bf16[256,1024]{1,0:T(8,128)(2,1)} %get-tuple-element.90), channel_id=1, source_target_pairs={{30,0},{5,3},{2,4},{9,7},{6,8},{13,11},{10,12},{17,15},{14,16},{21... | collective-permute-start | bytes 1572872 | tf_op jit(solution)/shard_map/ppermute | solution.py:446
  85.8 2.7 %collective-permute-done.16.up_two_ref = bf16[80,1024]{1,0:T(8,128)(2,1)S(1)} collective-permute-done((bf16[80,1024]{1,0:T(8,128)(2,1)}, bf16[80,1024]{1,0:T(8,128)(2,1)S(1)}, u32[]{:S(2)}, u32[]{:S(2)}) %collective-permute-start.16) | collective-permute-done | bytes 163872 | tf_op jit(solution)/shard_map/ppermute | solution.py:297
  88.5 1.2 collective-permute-done.17.down_two_ref
  89.6 0.7 copy-done.7
  90.3 2.2 %shard_map.112 = (f32[32,1024]{1,0:T(8,128)}, bf16[32,1024]{1,0:T(8,128)(2,1)}, bf16[32,1024]{1,0:T(8,128)(2,1)}, bf16[32,1024]{1,0:T(8,128)(2,1)}) custom-call(bf16[80,1024]{1,0:T(8,128)(2,1)} %get-tuple-element.61.here_ref, bf16[160,1024]{1,0:T(8,128)(2,1)} %copy-done, bf16[160,1024]{1,0:T(8,128)(2,1)} %copy-done.1, bf16[80,1024]{1,0:T(8,128)(2,1)} %copy-done.6, ...), custom_call_target="tpu_custom_call" | custom-call | flops 1000000 | bytes 1000000 | tf_op jit(solution)/shard_map/pallas_call | solution.py:113
  92.6 1.8 %collective-permute-start.21 = (bf16[32,1024]{1,0:T(8,128)(2,1)}, bf16[32,1024]{1,0:T(8,128)(2,1)S(1)}, u32[]{:S(2)}, u32[]{:S(2)}) collective-permute-start(bf16[32,1024]{1,0:T(8,128)(2,1)} %get-tuple-element.83), channel_id=1, source_target_pairs={{0,2},{1,3},{2,0},{3,1},{4,6},{5,7},{6,4},{7,5},{8,10},{9,11},{10,... | collective-permute-start | bytes 196616 | tf_op jit(solution)/shard_map/ppermute | solution.py:297
  94.6 0.9 maximum_select_fusion.1
  95.6 0.9 maximum_select_fusion
  96.5 5.1 %collective-permute-done.21.side_ref = bf16[32,1024]{1,0:T(8,128)(2,1)S(1)} collective-permute-done((bf16[32,1024]{1,0:T(8,128)(2,1)}, bf16[32,1024]{1,0:T(8,128)(2,1)S(1)}, u32[]{:S(2)}, u32[]{:S(2)}) %collective-permute-start.21) | collective-permute-done | bytes 65568 | tf_op jit(solution)/shard_map/ppermute | solution.py:297
  101.5 1.4 %collective-permute-done.22.corner_ref = bf16[32,1024]{1,0:T(8,128)(2,1)S(1)} collective-permute-done((bf16[32,1024]{1,0:T(8,128)(2,1)}, bf16[32,1024]{1,0:T(8,128)(2,1)S(1)}, u32[]{:S(2)}, u32[]{:S(2)}) %collective-permute-start.22) | collective-permute-done | bytes 65568 | tf_op jit(solution)/shard_map/ppermute | solution.py:297
  103.6 1.8 %shard_map.113 = (bf16[16,2048]{1,0:T(8,128)(2,1)}, f32[32,128]{1,0:T(8,128)}) custom-call(s32[1]{0:T(128)} %bitcast.half_ref, f32[32,1024]{1,0:T(8,128)} %get-tuple-element.81.keep_ref, bf16[32,1024]{1,0:T(8,128)(2,1)} %copy-done.13, bf16[32,1024]{1,0:T(8,128)(2,1)} %copy-done.14, bf16[32,1024]{1,0:T(8,128)(2,1)} %copy-done.15), custom_call_target="tpu_custom_call" | custom-call | flops 1000000 | bytes 1000000 | tf_op jit(solution)/shard_map/pallas_call | solution.py:113
  105.4 2.5 %collective-permute-start.26 = (f32[32,128]{1,0:T(8,128)}, f32[32,128]{1,0:T(8,128)S(1)}, u32[]{:S(2)}, u32[]{:S(2)}) collective-permute-start(f32[32,128]{1,0:T(8,128)} %get-tuple-element.89), channel_id=1, source_target_pairs={{0,96},{1,97},{2,98},{3,99},{4,100},{5,101},{6,102},{7,103},{8,104... | collective-permute-start | bytes 49160 | tf_op jit(solution)/shard_map/ppermute | solution.py:418
  108.6 1.5 %convert_add_fusion = bf16[256,1024]{1,0:T(8,128)(2,1)S(1)} fusion(bf16[256,1024]{1,0:T(8,128)(2,1)} %collective-permute-done.23, bf16[256,1024]{1,0:T(8,128)(2,1)} %collective-permute-done.15, bf16[512,1024]{1,0:T(8,128)(2,1)S(1)} %collective-permute-done.19), kind=kLoop, calls=%fused_computation.7 | loop fusion | flops 1572864 | bytes 2097152 | tf_op jit(solution)/shard_map/add | solution.py:460
  110.1 2.0 %collective-permute-done.25 = f32[32,128]{1,0:T(8,128)S(1)} collective-permute-done((f32[32,128]{1,0:T(8,128)}, f32[32,128]{1,0:T(8,128)S(1)}, u32[]{:S(2)}, u32[]{:S(2)}) %collective-permute-start.25) | collective-permute-done | bytes 16416 | tf_op jit(solution)/shard_map/ppermute | solution.py:418
  112.2 2.6 %collective-permute-start.28 = (f32[32,128]{1,0:T(8,128)S(1)}, f32[32,128]{1,0:T(8,128)S(1)}, u32[]{:S(2)}, u32[]{:S(2)}) collective-permute-start(f32[32,128]{1,0:T(8,128)S(1)} %add_add_fusion), channel_id=1, source_target_pairs={{0,128},{1,129},{2,130},{3,131},{4,132},{5,133},{6,134},{7,135},{8... | collective-permute-start | bytes 49160 | tf_op jit(solution)/shard_map/ppermute | solution.py:418
  115.9 1.0 pad_maximum_fusion.2
  (104 shorter events, 6.0 us)
Async XLA Ops:
  1.4 8.1 %collective-permute-start.1 = (bf16[2,8,1024]{2,1,0:T(8,128)(2,1)S(1)}, bf16[2,8,1024]{2,1,0:T(8,128)(2,1)S(1)}, u32[]{:S(2)}, u32[]{:S(2)}) collective-permute-start(bf16[2,8,1024]{2,1,0:T(8,128)(2,1)S(1)} %pad_maximum_fusion.9), channel_id=1, source_target_pairs={{0,3},{1,2},{2,1},{3,0},{4,7},{5,6},{6,5},{7,4},{8,11},{9,10},{10,... | collective-permute-start | bytes 98312 | tf_op jit(solution)/shard_map/ppermute | solution.py:297
  4.2 5.3 %collective-permute-start = (bf16[2,8,1024]{2,1,0:T(8,128)(2,1)S(1)}, bf16[2,8,1024]{2,1,0:T(8,128)(2,1)S(1)}, u32[]{:S(2)}, u32[]{:S(2)}) collective-permute-start(bf16[2,8,1024]{2,1,0:T(8,128)(2,1)S(1)} %pad_maximum_fusion.9), channel_id=1, source_target_pairs={{0,1},{1,0},{2,3},{3,2},{4,5},{5,4},{6,7},{7,6},{8,9},{9,8},{10,11... | collective-permute-start | bytes 98312 | tf_op jit(solution)/shard_map/ppermute | solution.py:297
  4.9 4.7 %collective-permute-start.3 = (bf16[2,8,1024]{2,1,0:T(8,128)(2,1)S(1)}, bf16[2,8,1024]{2,1,0:T(8,128)(2,1)S(1)}, u32[]{:S(2)}, u32[]{:S(2)}) collective-permute-start(bf16[2,8,1024]{2,1,0:T(8,128)(2,1)S(1)} %pad_maximum_fusion.10), channel_id=1, source_target_pairs={{0,2},{1,3},{2,0},{3,1},{4,6},{5,7},{6,4},{7,5},{8,10},{9,11},{10,... | collective-permute-start | bytes 98312 | tf_op jit(solution)/shard_map/ppermute | solution.py:297
  6.3 1.4 %copy-start.16 = (s32[4096]{0:T(1024)S(1)}, s32[4096]{0:T(1024)}, u32[]{:S(2)}) copy-start(s32[4096]{0:T(1024)} %param.12) | copy-start | bytes 49156
  6.3 1.4 %copy-start.17 = (s32[1,4096]{1,0:T(1,128)S(1)}, s32[1,4096]{1,0:T(1,128)}, u32[]{:S(2)}) copy-start(s32[1,4096]{1,0:T(1,128)} %param.11) | copy-start | bytes 49156
  6.3 2.1 %copy-start.11 = (f32[16,13,13]{2,0,1:T(8,128)S(1)}, f32[16,13,13]{2,0,1:T(8,128)}, u32[]{:S(2)}) copy-start(f32[16,13,13]{2,0,1:T(8,128)} %param.13) | copy-start | bytes 32452
  6.3 2.1 %copy-start.9 = (bf16[1,128,2048]{2,1,0:T(8,128)(2,1)S(1)}, bf16[1,128,2048]{2,1,0:T(8,128)(2,1)}, u32[]{:S(2)}) copy-start(bf16[1,128,2048]{2,1,0:T(8,128)(2,1)} %param.7) | copy-start | bytes 1572868
  6.3 2.1 %copy-start.10 = (bf16[1,128,2048]{2,1,0:T(8,128)(2,1)S(1)}, bf16[1,128,2048]{2,1,0:T(8,128)(2,1)}, u32[]{:S(2)}) copy-start(bf16[1,128,2048]{2,1,0:T(8,128)(2,1)} %param.10) | copy-start | bytes 1572868
  9.6 27.9 %copy-start.3 = (bf16[2,32,1024]{2,1,0:T(8,128)(2,1)}, bf16[2,32,1024]{2,1,0:T(8,128)(2,1)S(1)}, u32[]{:S(2)}) copy-start(bf16[2,32,1024]{2,1,0:T(8,128)(2,1)S(1)} %pad_maximum_fusion.8) | copy-start | bytes 393220
  9.6 8.7 %collective-permute-start.6 = (bf16[64,1024]{1,0:T(8,128)(2,1)S(1)}, bf16[64,1024]{1,0:T(8,128)(2,1)S(1)}, u32[]{:S(2)}, u32[]{:S(2)}) collective-permute-start(bf16[64,1024]{1,0:T(8,128)(2,1)S(1)} %bitcast.84), channel_id=1, source_target_pairs={{0,8},{1,9},{2,10},{3,11},{4,12},{5,13},{6,14},{7,15},{8,16},{9,17... | collective-permute-start | bytes 393224 | tf_op jit(solution)/shard_map/ppermute | solution.py:297
  11.0 10.5 %collective-permute-start.5 = (bf16[64,1024]{1,0:T(8,128)(2,1)S(1)}, bf16[64,1024]{1,0:T(8,128)(2,1)S(1)}, u32[]{:S(2)}, u32[]{:S(2)}) collective-permute-start(bf16[64,1024]{1,0:T(8,128)(2,1)S(1)} %bitcast.85), channel_id=1, source_target_pairs={{0,24},{1,25},{2,26},{3,27},{4,28},{5,29},{6,30},{7,31},{8,0},{9,1... | collective-permute-start | bytes 393224 | tf_op jit(solution)/shard_map/ppermute | solution.py:297
  14.1 19.5 %collective-permute-start.7 = (bf16[256,1024]{1,0:T(8,128)(2,1)S(1)}, bf16[256,1024]{1,0:T(8,128)(2,1)S(1)}, u32[]{:S(2)}, u32[]{:S(2)}) collective-permute-start(bf16[256,1024]{1,0:T(8,128)(2,1)S(1)} %pad_maximum_fusion.3), channel_id=1, source_target_pairs={{0,31},{1,2},{2,1},{3,4},{4,3},{5,6},{6,5},{7,8},{8,7},{9,10},{10,... | collective-permute-start | bytes 1572872 | tf_op jit(solution)/shard_map/ppermute | solution.py:327
  17.0 24.2 %collective-permute-start.2 = (bf16[256,1024]{1,0:T(8,128)(2,1)S(1)}, bf16[256,1024]{1,0:T(8,128)(2,1)}, u32[]{:S(2)}, u32[]{:S(2)}) collective-permute-start(bf16[256,1024]{1,0:T(8,128)(2,1)S(1)} %pad_maximum_fusion.3), channel_id=1, source_target_pairs={{0,1},{1,0},{2,3},{3,2},{4,5},{5,4},{6,7},{7,6},{8,9},{9,8},{10,11... | collective-permute-start | bytes 1572872 | tf_op jit(solution)/shard_map/ppermute | solution.py:297
  18.1 23.1 %collective-permute-start.4 = (bf16[256,1024]{1,0:T(8,128)(2,1)S(1)}, bf16[256,1024]{1,0:T(8,128)(2,1)}, u32[]{:S(2)}, u32[]{:S(2)}) collective-permute-start(bf16[256,1024]{1,0:T(8,128)(2,1)S(1)} %pad_maximum_fusion.5), channel_id=1, source_target_pairs={{0,1},{1,0},{2,3},{3,2},{4,5},{5,4},{6,7},{7,6},{8,9},{9,8},{10,11... | collective-permute-start | bytes 1572872 | tf_op jit(solution)/shard_map/ppermute | solution.py:297
  18.2 24.3 %copy-start.4 = (bf16[64,1024]{1,0:T(8,128)(2,1)}, bf16[64,1024]{1,0:T(8,128)(2,1)S(1)}, u32[]{:S(2)}) copy-start(bf16[64,1024]{1,0:T(8,128)(2,1)S(1)} %collective-permute-done.6.refs_10_) | copy-start | bytes 393220
  18.2 23.0 %collective-permute-start.8 = (bf16[256,1024]{1,0:T(8,128)(2,1)S(1)}, bf16[256,1024]{1,0:T(8,128)(2,1)}, u32[]{:S(2)}, u32[]{:S(2)}) collective-permute-start(bf16[256,1024]{1,0:T(8,128)(2,1)S(1)} %pad_maximum_fusion.4), channel_id=1, source_target_pairs={{0,30},{1,3},{2,0},{3,5},{4,2},{5,7},{6,4},{7,9},{8,6},{9,11},{10,... | collective-permute-start | bytes 1572872 | tf_op jit(solution)/shard_map/ppermute | solution.py:330
  21.5 21.0 %copy-start.5 = (bf16[64,1024]{1,0:T(8,128)(2,1)}, bf16[64,1024]{1,0:T(8,128)(2,1)S(1)}, u32[]{:S(2)}) copy-start(bf16[64,1024]{1,0:T(8,128)(2,1)S(1)} %collective-permute-done.5.refs_9_) | copy-start | bytes 393220
  21.5 14.2 %collective-permute-start.11 = (bf16[128,1024]{1,0:T(8,128)(2,1)S(1)}, bf16[128,1024]{1,0:T(8,128)(2,1)}, u32[]{:S(2)}, u32[]{:S(2)}) collective-permute-start(bf16[128,1024]{1,0:T(8,128)(2,1)S(1)} %get-tuple-element.120), channel_id=1, source_target_pairs={{0,4},{1,5},{2,6},{3,7},{4,8},{5,9},{6,10},{7,11},{8,12},{9,13},{1... | collective-permute-start | bytes 786440 | tf_op jit(solution)/shard_map/ppermute | solution.py:297
  33.6 9.0 %copy-start.19 = (bf16[256,1024]{1,0:T(8,128)(2,1)}, bf16[256,1024]{1,0:T(8,128)(2,1)S(1)}, u32[]{:S(2)}) copy-start(bf16[256,1024]{1,0:T(8,128)(2,1)S(1)} %collective-permute-done.7.refs_6_) | copy-start | bytes 1572868
  33.6 7.6 %collective-permute-start.10 = (bf16[128,1024]{1,0:T(8,128)(2,1)S(1)}, bf16[128,1024]{1,0:T(8,128)(2,1)}, u32[]{:S(2)}, u32[]{:S(2)}) collective-permute-start(bf16[128,1024]{1,0:T(8,128)(2,1)S(1)} %get-tuple-element.121), channel_id=1, source_target_pairs={{0,28},{1,29},{2,30},{3,31},{4,0},{5,1},{6,2},{7,3},{8,4},{9,5},{1... | collective-permute-start | bytes 786440 | tf_op jit(solution)/shard_map/ppermute | solution.py:297
  35.7 6.8 %collective-permute-start.9 = (bf16[64,1024]{1,0:T(8,128)(2,1)S(1)}, bf16[64,1024]{1,0:T(8,128)(2,1)S(1)}, u32[]{:S(2)}, u32[]{:S(2)}) collective-permute-start(bf16[64,1024]{1,0:T(8,128)(2,1)S(1)} %broadcast_select_fusion), channel_id=1, source_target_pairs={{0,24},{1,9},{2,26},{3,11},{4,28},{5,13},{6,30},{7,15},{8,0},{9,17... | collective-permute-start | bytes 393224 | tf_op jit(solution)/shard_map/ppermute | solution.py:297
  55.3 26.0 %copy-start.2 = (bf16[512,1024]{1,0:T(8,128)(2,1)S(1)}, bf16[512,1024]{1,0:T(8,128)(2,1)}, u32[]{:S(2)}) copy-start(bf16[512,1024]{1,0:T(8,128)(2,1)} %get-tuple-element.91) | copy-start | bytes 3145732
  55.3 34.4 %collective-permute-start.19 = (bf16[512,1024]{1,0:T(8,128)(2,1)}, bf16[512,1024]{1,0:T(8,128)(2,1)S(1)}, u32[]{:S(2)}, u32[]{:S(2)}) collective-permute-start(bf16[512,1024]{1,0:T(8,128)(2,1)} %get-tuple-element.78), channel_id=1, source_target_pairs={{0,1},{1,0},{2,3},{3,2},{4,5},{5,4},{6,7},{7,6},{8,9},{9,8},{10,11... | collective-permute-start | bytes 3145736 | tf_op jit(solution)/shard_map/ppermute | solution.py:297
  55.5 19.0 %collective-permute-start.15 = (bf16[256,1024]{1,0:T(8,128)(2,1)}, bf16[256,1024]{1,0:T(8,128)(2,1)}, u32[]{:S(2)}, u32[]{:S(2)}) collective-permute-start(bf16[256,1024]{1,0:T(8,128)(2,1)} %get-tuple-element.85), channel_id=1, source_target_pairs={{1,2},{2,1},{5,6},{6,5},{9,10},{10,9},{13,14},{14,13},{17,18},{18,... | collective-permute-start | bytes 1572872 | tf_op jit(solution)/shard_map/ppermute | solution.py:432
  60.9 9.2 %collective-permute-start.14 = (bf16[80,1024]{1,0:T(8,128)(2,1)}, bf16[80,1024]{1,0:T(8,128)(2,1)S(1)}, u32[]{:S(2)}, u32[]{:S(2)}) collective-permute-start(bf16[80,1024]{1,0:T(8,128)(2,1)} %get-tuple-element.64), channel_id=1, source_target_pairs={{0,8},{1,25},{2,10},{3,27},{4,12},{5,29},{6,14},{7,31},{8,16},{9,1... | collective-permute-start | bytes 491528 | tf_op jit(solution)/shard_map/ppermute | solution.py:297
  64.6 7.3 %collective-permute-start.12 = (bf16[160,1024]{1,0:T(8,128)(2,1)}, bf16[160,1024]{1,0:T(8,128)(2,1)S(1)}, u32[]{:S(2)}, u32[]{:S(2)}) collective-permute-start(bf16[160,1024]{1,0:T(8,128)(2,1)} %get-tuple-element.62), channel_id=1, source_target_pairs={{0,4},{1,5},{2,6},{3,7},{4,8},{5,9},{6,10},{7,11},{8,12},{9,13},{1... | collective-permute-start | bytes 983048 | tf_op jit(solution)/shard_map/ppermute | solution.py:297
  64.6 10.0 %collective-permute-start.13 = (bf16[160,1024]{1,0:T(8,128)(2,1)}, bf16[160,1024]{1,0:T(8,128)(2,1)S(1)}, u32[]{:S(2)}, u32[]{:S(2)}) collective-permute-start(bf16[160,1024]{1,0:T(8,128)(2,1)} %get-tuple-element.63), channel_id=1, source_target_pairs={{0,28},{1,29},{2,30},{3,31},{4,0},{5,1},{6,2},{7,3},{8,4},{9,5},{1... | collective-permute-start | bytes 983048 | tf_op jit(solution)/shard_map/ppermute | solution.py:297
  70.1 4.5 %copy-start.8 = (bf16[80,1024]{1,0:T(8,128)(2,1)}, bf16[80,1024]{1,0:T(8,128)(2,1)S(1)}, u32[]{:S(2)}) copy-start(bf16[80,1024]{1,0:T(8,128)(2,1)S(1)} %collective-permute-done.14.four_ref) | copy-start | bytes 491524
  70.1 12.7 %collective-permute-start.18 = (bf16[256,1024]{1,0:T(8,128)(2,1)}, bf16[256,1024]{1,0:T(8,128)(2,1)S(1)}, u32[]{:S(2)}, u32[]{:S(2)}) collective-permute-start(bf16[256,1024]{1,0:T(8,128)(2,1)} %get-tuple-element.90), channel_id=1, source_target_pairs={{3,1},{0,2},{7,5},{4,6},{11,9},{8,10},{15,13},{12,14},{19,17},{16,... | collective-permute-start | bytes 1572872 | tf_op jit(solution)/shard_map/ppermute | solution.py:433
  71.9 2.7 %copy-start = (bf16[160,1024]{1,0:T(8,128)(2,1)}, bf16[160,1024]{1,0:T(8,128)(2,1)S(1)}, u32[]{:S(2)}) copy-start(bf16[160,1024]{1,0:T(8,128)(2,1)S(1)} %collective-permute-done.12.up_odd_ref.up_ref) | copy-start | bytes 983044
  74.6 0.7 copy-start.1
  77.7 10.8 %collective-permute-start.16 = (bf16[80,1024]{1,0:T(8,128)(2,1)}, bf16[80,1024]{1,0:T(8,128)(2,1)S(1)}, u32[]{:S(2)}, u32[]{:S(2)}) collective-permute-start(bf16[80,1024]{1,0:T(8,128)(2,1)} %get-tuple-element.76), channel_id=1, source_target_pairs={{0,8},{1,9},{2,10},{3,11},{4,12},{5,13},{6,14},{7,15},{8,16},{9,17... | collective-permute-start | bytes 491528 | tf_op jit(solution)/shard_map/ppermute | solution.py:297
  78.7 10.9 %collective-permute-start.17 = (bf16[80,1024]{1,0:T(8,128)(2,1)}, bf16[80,1024]{1,0:T(8,128)(2,1)S(1)}, u32[]{:S(2)}, u32[]{:S(2)}) collective-permute-start(bf16[80,1024]{1,0:T(8,128)(2,1)} %get-tuple-element.77), channel_id=1, source_target_pairs={{0,24},{1,25},{2,26},{3,27},{4,28},{5,29},{6,30},{7,31},{8,0},{9,1... | collective-permute-start | bytes 491528 | tf_op jit(solution)/shard_map/ppermute | solution.py:297
  81.3 15.2 %collective-permute-start.23 = (bf16[256,1024]{1,0:T(8,128)(2,1)}, bf16[256,1024]{1,0:T(8,128)(2,1)}, u32[]{:S(2)}, u32[]{:S(2)}) collective-permute-start(bf16[256,1024]{1,0:T(8,128)(2,1)} %get-tuple-element.85), channel_id=1, source_target_pairs={{0,31},{3,4},{4,3},{7,8},{8,7},{11,12},{12,11},{15,16},{16,15},{19... | collective-permute-start | bytes 1572872 | tf_op jit(solution)/shard_map/ppermute | solution.py:445
  82.8 29.4 %collective-permute-start.27 = (bf16[256,1024]{1,0:T(8,128)(2,1)}, bf16[256,1024]{1,0:T(8,128)(2,1)}, u32[]{:S(2)}, u32[]{:S(2)}) collective-permute-start(bf16[256,1024]{1,0:T(8,128)(2,1)} %get-tuple-element.90), channel_id=1, source_target_pairs={{30,0},{5,3},{2,4},{9,7},{6,8},{13,11},{10,12},{17,15},{14,16},{21... | collective-permute-start | bytes 1572872 | tf_op jit(solution)/shard_map/ppermute | solution.py:446
  88.5 1.8 %copy-start.6 = (bf16[80,1024]{1,0:T(8,128)(2,1)}, bf16[80,1024]{1,0:T(8,128)(2,1)S(1)}, u32[]{:S(2)}) copy-start(bf16[80,1024]{1,0:T(8,128)(2,1)S(1)} %collective-permute-done.16.up_two_ref) | copy-start | bytes 491524
  89.6 0.7 copy-start.7
  92.5 4.0 %collective-permute-start.20 = (bf16[32,1024]{1,0:T(8,128)(2,1)}, bf16[32,1024]{1,0:T(8,128)(2,1)S(1)}, u32[]{:S(2)}, u32[]{:S(2)}) collective-permute-start(bf16[32,1024]{1,0:T(8,128)(2,1)} %get-tuple-element.82), channel_id=1, source_target_pairs={{0,1},{1,0},{2,3},{3,2},{4,5},{5,4},{6,7},{7,6},{8,9},{9,8},{10,11... | collective-permute-start | bytes 196616 | tf_op jit(solution)/shard_map/ppermute | solution.py:297
  92.6 9.0 %collective-permute-start.21 = (bf16[32,1024]{1,0:T(8,128)(2,1)}, bf16[32,1024]{1,0:T(8,128)(2,1)S(1)}, u32[]{:S(2)}, u32[]{:S(2)}) collective-permute-start(bf16[32,1024]{1,0:T(8,128)(2,1)} %get-tuple-element.83), channel_id=1, source_target_pairs={{0,2},{1,3},{2,0},{3,1},{4,6},{5,7},{6,4},{7,5},{8,10},{9,11},{10,... | collective-permute-start | bytes 196616 | tf_op jit(solution)/shard_map/ppermute | solution.py:297
  94.3 8.6 %collective-permute-start.22 = (bf16[32,1024]{1,0:T(8,128)(2,1)}, bf16[32,1024]{1,0:T(8,128)(2,1)S(1)}, u32[]{:S(2)}, u32[]{:S(2)}) collective-permute-start(bf16[32,1024]{1,0:T(8,128)(2,1)} %get-tuple-element.84), channel_id=1, source_target_pairs={{0,3},{1,2},{2,1},{3,0},{4,7},{5,6},{6,5},{7,4},{8,11},{9,10},{10,... | collective-permute-start | bytes 196616 | tf_op jit(solution)/shard_map/ppermute | solution.py:297
  96.5 6.5 %copy-start.13 = (bf16[32,1024]{1,0:T(8,128)(2,1)}, bf16[32,1024]{1,0:T(8,128)(2,1)S(1)}, u32[]{:S(2)}) copy-start(bf16[32,1024]{1,0:T(8,128)(2,1)S(1)} %collective-permute-done.20.core_ref) | copy-start | bytes 196612
  101.5 1.4 %copy-start.14 = (bf16[32,1024]{1,0:T(8,128)(2,1)}, bf16[32,1024]{1,0:T(8,128)(2,1)S(1)}, u32[]{:S(2)}) copy-start(bf16[32,1024]{1,0:T(8,128)(2,1)S(1)} %collective-permute-done.21.side_ref) | copy-start | bytes 196612
  105.4 6.8 %copy-start.18 = (f32[32,128]{1,0:T(8,128)S(1)}, f32[32,128]{1,0:T(8,128)}, u32[]{:S(2)}) copy-start(f32[32,128]{1,0:T(8,128)} %get-tuple-element.89) | copy-start | bytes 49156
  105.4 4.7 %collective-permute-start.26 = (f32[32,128]{1,0:T(8,128)}, f32[32,128]{1,0:T(8,128)S(1)}, u32[]{:S(2)}, u32[]{:S(2)}) collective-permute-start(f32[32,128]{1,0:T(8,128)} %get-tuple-element.89), channel_id=1, source_target_pairs={{0,96},{1,97},{2,98},{3,99},{4,100},{5,101},{6,102},{7,103},{8,104... | collective-permute-start | bytes 49160 | tf_op jit(solution)/shard_map/ppermute | solution.py:418
  107.8 4.3 %collective-permute-start.25 = (f32[32,128]{1,0:T(8,128)}, f32[32,128]{1,0:T(8,128)S(1)}, u32[]{:S(2)}, u32[]{:S(2)}) collective-permute-start(f32[32,128]{1,0:T(8,128)} %get-tuple-element.89), channel_id=1, source_target_pairs={{0,64},{1,65},{2,66},{3,67},{4,68},{5,69},{6,70},{7,71},{8,72},{9,... | collective-permute-start | bytes 49160 | tf_op jit(solution)/shard_map/ppermute | solution.py:418
  108.4 3.8 %collective-permute-start.24 = (f32[32,128]{1,0:T(8,128)}, f32[32,128]{1,0:T(8,128)S(1)}, u32[]{:S(2)}, u32[]{:S(2)}) collective-permute-start(f32[32,128]{1,0:T(8,128)} %get-tuple-element.89), channel_id=1, source_target_pairs={{0,32},{1,33},{2,34},{3,35},{4,36},{5,37},{6,38},{7,39},{8,40},{9,... | collective-permute-start | bytes 49160 | tf_op jit(solution)/shard_map/ppermute | solution.py:418
  112.2 4.8 %collective-permute-start.28 = (f32[32,128]{1,0:T(8,128)S(1)}, f32[32,128]{1,0:T(8,128)S(1)}, u32[]{:S(2)}, u32[]{:S(2)}) collective-permute-start(f32[32,128]{1,0:T(8,128)S(1)} %add_add_fusion), channel_id=1, source_target_pairs={{0,128},{1,129},{2,130},{3,131},{4,132},{5,133},{6,134},{7,135},{8... | collective-permute-start | bytes 49160 | tf_op jit(solution)/shard_map/ppermute | solution.py:418
  115.1 0.8 copy-start.12
  (2 other events, 1.3 us)

commit v4 on v3

--- a/solution.py
+++ b/solution.py
@@ -64,7 +64,7 @@
         (up_ref, up_odd_ref, upper, up_out),
         (down_ref, down_odd_ref, jnp.logical_not(upper), down_out),
     ):
-        total = wide(ref[...]) + wide(odd[block:]) + jnp.where(far, across, 0.0)
+        total = wide(ref[...]) + wide(odd[block - SLOT :]) + jnp.where(far, across, 0.0)
         out[: block - SLOT] = total[: block - SLOT].astype(BF16)
         for h in range(0, total.shape[1], LANES):
             out[block - SLOT :, h : h + LANES] = resplit(total[block - SLOT :, h : h + LANES])
@@ -72,7 +72,10 @@
 
 def quad_kernel(here_ref, up_ref, down_ref, up_two_ref, down_two_ref, keep_out, *outs):
     block = here_ref.shape[0]
-    total = wide(here_ref[...]) + wide(up_ref[:block]) + wide(down_ref[:block])
+    both = slice(0, block - SLOT), slice(2 * (block - SLOT), 2 * (block - SLOT) + SLOT)
+    up = jnp.concatenate([wide(up_ref[rows]) for rows in both], axis=0)
+    down = jnp.concatenate([wide(down_ref[rows]) for rows in both], axis=0)
+    total = wide(here_ref[...]) + up + down
     total = total + wide(up_two_ref[...]) + wide(down_two_ref[...])
     part = (block - SLOT) // 2
     pieces = [
@@ -190,14 +193,7 @@
         by_level = q_terms[:, LANES:] + (
             mm(dl_main, hot_main, ROW_COL) + stacked(dl_out, hot_own, hot_par, ROW_COL)
         )
-        bias = lax.dot_general(
-            row_hot.astype(F32),
-            by_level,
-            (COL_COL, ((), ())),
-            precision=lax.Precision.HIGHEST,
-            preferred_element_type=F32,
-        )
-        bias = split_sum(bias)
+        bias = resplit(mm(row_hot, split_sum(by_level), COL_COL))
         yield
         gk_main = (mm(db_main, q, COL_COL) * inv_scale).astype(BF16)
         gv_main = mm(pb_main, g, COL_COL).astype(BF16)
@@ -216,11 +212,11 @@
         own_out_ref[rows:, lanes] = gv_own
         par_out_ref[:rows, lanes] = gk_par
         par_out_ref[rows:, lanes] = gv_par
+        for ref in coarse_out:
+            ref[ref.shape[0] - SLOT :, lanes] = bias
         for j, (r, a) in enumerate(places):
-            a = a // (2 * part) * (2 * part + SLOT)
             coarse_out[r][a : a + part, lanes] = gk_main[j * part : (j + 1) * part]
             coarse_out[r][a + part : a + 2 * part, lanes] = gv_main[j * part : (j + 1) * part]
-            coarse_out[r][a + 2 * part : a + 2 * part + SLOT, lanes] = bias
 
     waiting = [one_head(head) for head in range(table_ref.shape[0])]
     running = []
@@ -259,8 +255,7 @@
             pl.BlockSpec(keep.shape, fixed),
         ]
     )
-    blocks = [x.shape[0] // coarse[0].shape[0] for x in coarse]
-    out_rows = [4 * rows] * 2 + [2 * rows] * 2 + [n * (coarse[0].shape[0] + SLOT) for n in blocks]
+    out_rows = [4 * rows] * 2 + [2 * rows] * 2 + [x.shape[0] + SLOT for x in coarse]
     out_shape = [jax.ShapeDtypeStruct((r, half_width), BF16) for r in out_rows]
     out_specs = [pl.BlockSpec((r, lanes), at) for r in out_rows]
     return pl.pallas_call(

time: 120 us -> 119 us (level)
  no operation moved by 1% of the time
where the time goes in v4:
time: 119 us; the launch traced here: 117 us
  starting transfers between devices  45 us (38%)
  waiting for transfers between devices  37.4 us (31%)
  Pallas kernels  18.1 us (15%)
  other arithmetic  7.64 us (6%)
  local copies, waits for them, and re-layouts  7.33 us (6%)
    ppermute x19, starting transfers between devices, send(): return lax.ppermute(x, 'tile', [(i, target(i)) for i in range(tiles)])  26.1 us
    ppermute x19, waiting for transfers between devices, send(): return lax.ppermute(x, 'tile', [(i, target(i)) for i in range(tiles)])  24.2 us
    pallas_call x1, Pallas kernels, call_kernel(): pl.pallas_call(functools.partial(attention_kernel, inv_scale), grid_spec=...  11.8 us
    ppermute x1, waiting for transfers between devices, shards(): kv_own_out = lax.ppermute(kv_other, 'tile', edge)  11.1 us
    pallas_call x3, Pallas kernels, small_call(): pl.pallas_call(kernel, in_specs=smem + [pl.BlockSpec(memory_space=pltpu.V...  6.26 us
    ppermute x4, starting transfers between devices, flipped(): lax.ppermute(x, ('batch', 'tile'), [(i, i ^ mask) for i in range(every)])  5.87 us
    ppermute x1, starting transfers between devices, shards(): other_y = lax.ppermute(own_out, 'tile', edge_y)  5.34 us
    ppermute x1, starting transfers between devices, shards(): mine_z = lax.ppermute(par_out, 'tile', jump_z)  3.26 us
  transfers between devices with their start and end apart: 29, of which 12 were waited for; matrix products, arithmetic and copies ran while one was open for 9% of the time, Pallas kernels for 5%

profile of v4, /device:TPU:1, one launch (start us, length us, event | category | flops | bytes accessed | tf_op | source)
XLA Modules:
  0.0 116.7 jit_solution(5317974329788749517)
XLA Ops:
  0.7 0.8 constant_dynamic-slice_fusion.4
  1.4 2.8 %collective-permute-start.1 = (bf16[2,8,1024]{2,1,0:T(8,128)(2,1)S(1)}, bf16[2,8,1024]{2,1,0:T(8,128)(2,1)S(1)}, u32[]{:S(2)}, u32[]{:S(2)}) collective-permute-start(bf16[2,8,1024]{2,1,0:T(8,128)(2,1)S(1)} %pad_maximum_fusion.9), channel_id=1, source_target_pairs={{0,3},{1,2},{2,1},{3,0},{4,7},{5,6},{6,5},{7,4},{8,11},{9,10},{10,... | collective-permute-start | bytes 98312 | tf_op jit(solution)/shard_map/ppermute | solution.py:292
  4.2 0.7 collective-permute-start
  4.9 1.3 %collective-permute-start.3 = (bf16[2,8,1024]{2,1,0:T(8,128)(2,1)S(1)}, bf16[2,8,1024]{2,1,0:T(8,128)(2,1)S(1)}, u32[]{:S(2)}, u32[]{:S(2)}) collective-permute-start(bf16[2,8,1024]{2,1,0:T(8,128)(2,1)S(1)} %pad_maximum_fusion.10), channel_id=1, source_target_pairs={{0,2},{1,3},{2,0},{3,1},{4,6},{5,7},{6,4},{7,5},{8,10},{9,11},{10,... | collective-permute-start | bytes 98312 | tf_op jit(solution)/shard_map/ppermute | solution.py:292
  6.3 1.4 %dynamic-slice_bitcast_fusion.2 = (bf16[128,1024]{1,0:T(8,128)(2,1)S(1)}, bf16[128,1024]{1,0:T(8,128)(2,1)S(1)}, bf16[128,1024]{1,0:T(8,128)(2,1)S(1)}, bf16[128,1024]{1,0:T(8,128)(2,1)S(1)}) fusion(bf16[1,128,2048]{2,1,0:T(8,128)(2,1)} %param.9, s32[]{:T(128)S(6)} %select_n.258, s32[]{:T(128)S(6)} %select_n.257, bf16[1,128,2048]{2,1,0:T(8,128)(2,1)} %param.8), kind=kLoop, calls=%fused_computation.21 | loop fusion | bytes 2097160 | tf_op jit(solution)/shard_map/dynamic_slice | solution.py:310
  8.7 0.9 and_convert_fusion.refs_15_
  9.6 1.4 %collective-permute-start.6 = (bf16[64,1024]{1,0:T(8,128)(2,1)S(1)}, bf16[64,1024]{1,0:T(8,128)(2,1)S(1)}, u32[]{:S(2)}, u32[]{:S(2)}) collective-permute-start(bf16[64,1024]{1,0:T(8,128)(2,1)S(1)} %bitcast.84), channel_id=1, source_target_pairs={{0,8},{1,9},{2,10},{3,11},{4,12},{5,13},{6,14},{7,15},{8,16},{9,17... | collective-permute-start | bytes 393224 | tf_op jit(solution)/shard_map/ppermute | solution.py:292
  11.0 3.1 %collective-permute-start.5 = (bf16[64,1024]{1,0:T(8,128)(2,1)S(1)}, bf16[64,1024]{1,0:T(8,128)(2,1)S(1)}, u32[]{:S(2)}, u32[]{:S(2)}) collective-permute-start(bf16[64,1024]{1,0:T(8,128)(2,1)S(1)} %bitcast.85), channel_id=1, source_target_pairs={{0,24},{1,25},{2,26},{3,27},{4,28},{5,29},{6,30},{7,31},{8,0},{9,1... | collective-permute-start | bytes 393224 | tf_op jit(solution)/shard_map/ppermute | solution.py:292
  14.1 2.1 %collective-permute-start.7 = (bf16[256,1024]{1,0:T(8,128)(2,1)S(1)}, bf16[256,1024]{1,0:T(8,128)(2,1)S(1)}, u32[]{:S(2)}, u32[]{:S(2)}) collective-permute-start(bf16[256,1024]{1,0:T(8,128)(2,1)S(1)} %pad_maximum_fusion.3), channel_id=1, source_target_pairs={{0,31},{1,2},{2,1},{3,4},{4,3},{5,6},{6,5},{7,8},{8,7},{9,10},{10,... | collective-permute-start | bytes 1572872 | tf_op jit(solution)/shard_map/ppermute | solution.py:322
  16.2 0.7 fusion.9.refs_14_
  17.0 1.2 collective-permute-start.2
  18.2 0.8 collective-permute-start.8
  19.0 2.4 %collective-permute-done.5.refs_9_ = bf16[64,1024]{1,0:T(8,128)(2,1)S(1)} collective-permute-done((bf16[64,1024]{1,0:T(8,128)(2,1)S(1)}, bf16[64,1024]{1,0:T(8,128)(2,1)S(1)}, u32[]{:S(2)}, u32[]{:S(2)}) %collective-permute-start.5) | collective-permute-done | bytes 131104 | tf_op jit(solution)/shard_map/ppermute | solution.py:292
  21.5 0.9 collective-permute-start.11
  22.5 11.1 %collective-permute-done.7.refs_6_ = bf16[256,1024]{1,0:T(8,128)(2,1)S(1)} collective-permute-done((bf16[256,1024]{1,0:T(8,128)(2,1)S(1)}, bf16[256,1024]{1,0:T(8,128)(2,1)S(1)}, u32[]{:S(2)}, u32[]{:S(2)}) %collective-permute-start.7) | collective-permute-done | bytes 524320 | tf_op jit(solution)/shard_map/ppermute | solution.py:322
  33.6 2.1 %collective-permute-start.10 = (bf16[128,1024]{1,0:T(8,128)(2,1)S(1)}, bf16[128,1024]{1,0:T(8,128)(2,1)}, u32[]{:S(2)}, u32[]{:S(2)}) collective-permute-start(bf16[128,1024]{1,0:T(8,128)(2,1)S(1)} %get-tuple-element.121), channel_id=1, source_target_pairs={{0,28},{1,29},{2,30},{3,31},{4,0},{5,1},{6,2},{7,3},{8,4},{9,5},{1... | collective-permute-start | bytes 786440 | tf_op jit(solution)/shard_map/ppermute | solution.py:292
  35.9 0.8 copy.27.refs_17_
  36.7 0.7 fusion.11.refs_16_
  37.4 3.8 %collective-permute-done.10.refs_12_ = bf16[128,1024]{1,0:T(8,128)(2,1)} collective-permute-done((bf16[128,1024]{1,0:T(8,128)(2,1)S(1)}, bf16[128,1024]{1,0:T(8,128)(2,1)}, u32[]{:S(2)}, u32[]{:S(2)}) %collective-permute-start.10) | collective-permute-done | bytes 262176 | tf_op jit(solution)/shard_map/ppermute | solution.py:292
  41.2 1.3 %collective-permute-done.9.refs_11_ = bf16[64,1024]{1,0:T(8,128)(2,1)S(1)} collective-permute-done((bf16[64,1024]{1,0:T(8,128)(2,1)S(1)}, bf16[64,1024]{1,0:T(8,128)(2,1)S(1)}, u32[]{:S(2)}, u32[]{:S(2)}) %collective-permute-start.9) | collective-permute-done | bytes 131104 | tf_op jit(solution)/shard_map/ppermute | solution.py:292
  43.1 11.8 %shard_map.110 = (bf16[512,1024]{1,0:T(8,128)(2,1)}, bf16[512,1024]{1,0:T(8,128)(2,1)}, bf16[256,1024]{1,0:T(8,128)(2,1)}, bf16[256,1024]{1,0:T(8,128)(2,1)}, bf...) custom-call(s32[1]{0:T(128)} %bitcast.half_ref, ...), custom_call_target="tpu_custom_call" | custom-call | flops 2013265920 | bytes 10485760 | tf_op jit(solution)/shard_map/pallas_call | solution.py:261
  55.3 5.3 %collective-permute-start.15 = (bf16[256,1024]{1,0:T(8,128)(2,1)}, bf16[256,1024]{1,0:T(8,128)(2,1)}, u32[]{:S(2)}, u32[]{:S(2)}) collective-permute-start(bf16[256,1024]{1,0:T(8,128)(2,1)} %get-tuple-element.85), channel_id=1, source_target_pairs={{1,2},{2,1},{5,6},{6,5},{9,10},{10,9},{13,14},{14,13},{17,18},{18,... | collective-permute-start | bytes 1572872 | tf_op jit(solution)/shard_map/ppermute | solution.py:427
  60.6 3.7 %collective-permute-start.14 = (bf16[80,1024]{1,0:T(8,128)(2,1)}, bf16[80,1024]{1,0:T(8,128)(2,1)S(1)}, u32[]{:S(2)}, u32[]{:S(2)}) collective-permute-start(bf16[80,1024]{1,0:T(8,128)(2,1)} %get-tuple-element.64), channel_id=1, source_target_pairs={{0,8},{1,25},{2,10},{3,27},{4,12},{5,29},{6,14},{7,31},{8,16},{9,1... | collective-permute-start | bytes 491528 | tf_op jit(solution)/shard_map/ppermute | solution.py:292
  64.3 2.7 %collective-permute-start.13 = (bf16[144,1024]{1,0:T(8,128)(2,1)}, bf16[144,1024]{1,0:T(8,128)(2,1)S(1)}, u32[]{:S(2)}, u32[]{:S(2)}) collective-permute-start(bf16[144,1024]{1,0:T(8,128)(2,1)} %get-tuple-element.63), channel_id=1, source_target_pairs={{0,28},{1,29},{2,30},{3,31},{4,0},{5,1},{6,2},{7,3},{8,4},{9,5},{1... | collective-permute-start | bytes 884744 | tf_op jit(solution)/shard_map/ppermute | solution.py:292
  67.0 2.8 %collective-permute-done.14.four_ref = bf16[80,1024]{1,0:T(8,128)(2,1)S(1)} collective-permute-done((bf16[80,1024]{1,0:T(8,128)(2,1)}, bf16[80,1024]{1,0:T(8,128)(2,1)S(1)}, u32[]{:S(2)}, u32[]{:S(2)}) %collective-permute-start.14) | collective-permute-done | bytes 163872 | tf_op jit(solution)/shard_map/ppermute | solution.py:292
  69.8 1.5 %collective-permute-done.12.up_odd_ref.up_ref = bf16[144,1024]{1,0:T(8,128)(2,1)S(1)} collective-permute-done((bf16[144,1024]{1,0:T(8,128)(2,1)}, bf16[144,1024]{1,0:T(8,128)(2,1)S(1)}, u32[]{:S(2)}, u32[]{:S(2)}) %collective-permute-start.12) | collective-permute-done | bytes 294944 | tf_op jit(solution)/shard_map/ppermute | solution.py:292
  71.3 2.3 %collective-permute-done.13.down_odd_ref.down_ref = bf16[144,1024]{1,0:T(8,128)(2,1)S(1)} collective-permute-done((bf16[144,1024]{1,0:T(8,128)(2,1)}, bf16[144,1024]{1,0:T(8,128)(2,1)S(1)}, u32[]{:S(2)}, u32[]{:S(2)}) %collective-permute-start.13) | collective-permute-done | bytes 294944 | tf_op jit(solution)/shard_map/ppermute | solution.py:292
  73.6 0.7 copy-done.1
  74.3 2.3 %shard_map.111 = (bf16[80,1024]{1,0:T(8,128)(2,1)}, bf16[80,1024]{1,0:T(8,128)(2,1)}) custom-call(s32[1]{0:T(128)} %bitcast.half_ref, bf16[80,1024]{1,0:T(8,128)(2,1)} %get-tuple-element.71.up_ref, bf16[80,1024]{1,0:T(8,128)(2,1)} %get-tuple-element.72.down_ref, bf16[80,1024]{1,0:T(8,128)(2,1)} %copy-done.6, bf16[144,1024]{1,0:T(8,128)(2,1)} %copy-done, ...), custom_call_target="tpu_custom_call" | custom-call | flops 1000000 | bytes 1000000 | tf_op jit(solution)/shard_map/pallas_call | solution.py:116
  76.7 1.0 collective-permute-start.16
  77.7 2.5 %collective-permute-start.17 = (bf16[80,1024]{1,0:T(8,128)(2,1)}, bf16[80,1024]{1,0:T(8,128)(2,1)S(1)}, u32[]{:S(2)}, u32[]{:S(2)}) collective-permute-start(bf16[80,1024]{1,0:T(8,128)(2,1)} %get-tuple-element.77), channel_id=1, source_target_pairs={{0,24},{1,25},{2,26},{3,27},{4,28},{5,29},{6,30},{7,31},{8,0},{9,1... | collective-permute-start | bytes 491528 | tf_op jit(solution)/shard_map/ppermute | solution.py:292
  80.3 1.5 %collective-permute-start.23 = (bf16[256,1024]{1,0:T(8,128)(2,1)}, bf16[256,1024]{1,0:T(8,128)(2,1)}, u32[]{:S(2)}, u32[]{:S(2)}) collective-permute-start(bf16[256,1024]{1,0:T(8,128)(2,1)} %get-tuple-element.85), channel_id=1, source_target_pairs={{0,31},{3,4},{4,3},{7,8},{8,7},{11,12},{12,11},{15,16},{16,15},{19... | collective-permute-start | bytes 1572872 | tf_op jit(solution)/shard_map/ppermute | solution.py:440
  81.8 3.3 %collective-permute-start.27 = (bf16[256,1024]{1,0:T(8,128)(2,1)}, bf16[256,1024]{1,0:T(8,128)(2,1)}, u32[]{:S(2)}, u32[]{:S(2)}) collective-permute-start(bf16[256,1024]{1,0:T(8,128)(2,1)} %get-tuple-element.90), channel_id=1, source_target_pairs={{30,0},{5,3},{2,4},{9,7},{6,8},{13,11},{10,12},{17,15},{14,16},{21... | collective-permute-start | bytes 1572872 | tf_op jit(solution)/shard_map/ppermute | solution.py:441
  85.0 1.5 %collective-permute-done.16.up_two_ref = bf16[80,1024]{1,0:T(8,128)(2,1)S(1)} collective-permute-done((bf16[80,1024]{1,0:T(8,128)(2,1)}, bf16[80,1024]{1,0:T(8,128)(2,1)S(1)}, u32[]{:S(2)}, u32[]{:S(2)}) %collective-permute-start.16) | collective-permute-done | bytes 163872 | tf_op jit(solution)/shard_map/ppermute | solution.py:292
  86.5 2.1 %collective-permute-done.17.down_two_ref = bf16[80,1024]{1,0:T(8,128)(2,1)S(1)} collective-permute-done((bf16[80,1024]{1,0:T(8,128)(2,1)}, bf16[80,1024]{1,0:T(8,128)(2,1)S(1)}, u32[]{:S(2)}, u32[]{:S(2)}) %collective-permute-start.17) | collective-permute-done | bytes 163872 | tf_op jit(solution)/shard_map/ppermute | solution.py:292
  89.3 2.1 %shard_map.112 = (f32[32,1024]{1,0:T(8,128)}, bf16[32,1024]{1,0:T(8,128)(2,1)}, bf16[32,1024]{1,0:T(8,128)(2,1)}, bf16[32,1024]{1,0:T(8,128)(2,1)}) custom-call(bf16[80,1024]{1,0:T(8,128)(2,1)} %get-tuple-element.61.here_ref, bf16[144,1024]{1,0:T(8,128)(2,1)} %copy-done, bf16[144,1024]{1,0:T(8,128)(2,1)} %copy-done.1, bf16[80,1024]{1,0:T(8,128)(2,1)} %copy-done.7, ...), custom_call_target="tpu_custom_call" | custom-call | flops 1000000 | bytes 1000000 | tf_op jit(solution)/shard_map/pallas_call | solution.py:116
  91.6 1.7 %collective-permute-start.21 = (bf16[32,1024]{1,0:T(8,128)(2,1)}, bf16[32,1024]{1,0:T(8,128)(2,1)S(1)}, u32[]{:S(2)}, u32[]{:S(2)}) collective-permute-start(bf16[32,1024]{1,0:T(8,128)(2,1)} %get-tuple-element.83), channel_id=1, source_target_pairs={{0,2},{1,3},{2,0},{3,1},{4,6},{5,7},{6,4},{7,5},{8,10},{9,11},{10,... | collective-permute-start | bytes 196616 | tf_op jit(solution)/shard_map/ppermute | solution.py:292
  93.6 0.9 maximum_select_fusion.1
  94.5 0.9 maximum_select_fusion
  95.5 5.1 %collective-permute-done.21.side_ref = bf16[32,1024]{1,0:T(8,128)(2,1)S(1)} collective-permute-done((bf16[32,1024]{1,0:T(8,128)(2,1)}, bf16[32,1024]{1,0:T(8,128)(2,1)S(1)}, u32[]{:S(2)}, u32[]{:S(2)}) %collective-permute-start.21) | collective-permute-done | bytes 65568 | tf_op jit(solution)/shard_map/ppermute | solution.py:292
  100.5 1.4 %collective-permute-done.22.corner_ref = bf16[32,1024]{1,0:T(8,128)(2,1)S(1)} collective-permute-done((bf16[32,1024]{1,0:T(8,128)(2,1)}, bf16[32,1024]{1,0:T(8,128)(2,1)S(1)}, u32[]{:S(2)}, u32[]{:S(2)}) %collective-permute-start.22) | collective-permute-done | bytes 65568 | tf_op jit(solution)/shard_map/ppermute | solution.py:292
  102.6 1.8 %shard_map.113 = (bf16[16,2048]{1,0:T(8,128)(2,1)}, f32[32,128]{1,0:T(8,128)}) custom-call(s32[1]{0:T(128)} %bitcast.half_ref, f32[32,1024]{1,0:T(8,128)} %get-tuple-element.81.keep_ref, bf16[32,1024]{1,0:T(8,128)(2,1)} %copy-done.13, bf16[32,1024]{1,0:T(8,128)(2,1)} %copy-done.14, bf16[32,1024]{1,0:T(8,128)(2,1)} %copy-done.15), custom_call_target="tpu_custom_call" | custom-call | flops 1000000 | bytes 1000000 | tf_op jit(solution)/shard_map/pallas_call | solution.py:116
  104.4 2.5 %collective-permute-start.26 = (f32[32,128]{1,0:T(8,128)}, f32[32,128]{1,0:T(8,128)S(1)}, u32[]{:S(2)}, u32[]{:S(2)}) collective-permute-start(f32[32,128]{1,0:T(8,128)} %get-tuple-element.89), channel_id=1, source_target_pairs={{0,96},{1,97},{2,98},{3,99},{4,100},{5,101},{6,102},{7,103},{8,104... | collective-permute-start | bytes 49160 | tf_op jit(solution)/shard_map/ppermute | solution.py:413
  107.6 1.5 %convert_add_fusion = bf16[256,1024]{1,0:T(8,128)(2,1)S(1)} fusion(bf16[256,1024]{1,0:T(8,128)(2,1)} %collective-permute-done.23, bf16[256,1024]{1,0:T(8,128)(2,1)} %collective-permute-done.15, bf16[512,1024]{1,0:T(8,128)(2,1)S(1)} %collective-permute-done.19), kind=kLoop, calls=%fused_computation.7 | loop fusion | flops 1572864 | bytes 2097152 | tf_op jit(solution)/shard_map/add | solution.py:455
  109.1 2.0 %collective-permute-done.25 = f32[32,128]{1,0:T(8,128)S(1)} collective-permute-done((f32[32,128]{1,0:T(8,128)}, f32[32,128]{1,0:T(8,128)S(1)}, u32[]{:S(2)}, u32[]{:S(2)}) %collective-permute-start.25) | collective-permute-done | bytes 16416 | tf_op jit(solution)/shard_map/ppermute | solution.py:413
  111.2 2.6 %collective-permute-start.28 = (f32[32,128]{1,0:T(8,128)S(1)}, f32[32,128]{1,0:T(8,128)S(1)}, u32[]{:S(2)}, u32[]{:S(2)}) collective-permute-start(f32[32,128]{1,0:T(8,128)S(1)} %add_add_fusion), channel_id=1, source_target_pairs={{0,128},{1,129},{2,130},{3,131},{4,132},{5,133},{6,134},{7,135},{8... | collective-permute-start | bytes 49160 | tf_op jit(solution)/shard_map/ppermute | solution.py:413
  114.9 1.0 pad_maximum_fusion.2
  116.1 0.7 slice.47
  (104 shorter events, 6.1 us)
Async XLA Ops:
  1.4 8.1 %collective-permute-start.1 = (bf16[2,8,1024]{2,1,0:T(8,128)(2,1)S(1)}, bf16[2,8,1024]{2,1,0:T(8,128)(2,1)S(1)}, u32[]{:S(2)}, u32[]{:S(2)}) collective-permute-start(bf16[2,8,1024]{2,1,0:T(8,128)(2,1)S(1)} %pad_maximum_fusion.9), channel_id=1, source_target_pairs={{0,3},{1,2},{2,1},{3,0},{4,7},{5,6},{6,5},{7,4},{8,11},{9,10},{10,... | collective-permute-start | bytes 98312 | tf_op jit(solution)/shard_map/ppermute | solution.py:292
  4.2 5.3 %collective-permute-start = (bf16[2,8,1024]{2,1,0:T(8,128)(2,1)S(1)}, bf16[2,8,1024]{2,1,0:T(8,128)(2,1)S(1)}, u32[]{:S(2)}, u32[]{:S(2)}) collective-permute-start(bf16[2,8,1024]{2,1,0:T(8,128)(2,1)S(1)} %pad_maximum_fusion.9), channel_id=1, source_target_pairs={{0,1},{1,0},{2,3},{3,2},{4,5},{5,4},{6,7},{7,6},{8,9},{9,8},{10,11... | collective-permute-start | bytes 98312 | tf_op jit(solution)/shard_map/ppermute | solution.py:292
  4.9 4.7 %collective-permute-start.3 = (bf16[2,8,1024]{2,1,0:T(8,128)(2,1)S(1)}, bf16[2,8,1024]{2,1,0:T(8,128)(2,1)S(1)}, u32[]{:S(2)}, u32[]{:S(2)}) collective-permute-start(bf16[2,8,1024]{2,1,0:T(8,128)(2,1)S(1)} %pad_maximum_fusion.10), channel_id=1, source_target_pairs={{0,2},{1,3},{2,0},{3,1},{4,6},{5,7},{6,4},{7,5},{8,10},{9,11},{10,... | collective-permute-start | bytes 98312 | tf_op jit(solution)/shard_map/ppermute | solution.py:292
  6.3 1.4 %copy-start.16 = (s32[4096]{0:T(1024)S(1)}, s32[4096]{0:T(1024)}, u32[]{:S(2)}) copy-start(s32[4096]{0:T(1024)} %param.12) | copy-start | bytes 49156
  6.3 1.4 %copy-start.17 = (s32[1,4096]{1,0:T(1,128)S(1)}, s32[1,4096]{1,0:T(1,128)}, u32[]{:S(2)}) copy-start(s32[1,4096]{1,0:T(1,128)} %param.11) | copy-start | bytes 49156
  6.3 2.1 %copy-start.11 = (f32[16,13,13]{2,0,1:T(8,128)S(1)}, f32[16,13,13]{2,0,1:T(8,128)}, u32[]{:S(2)}) copy-start(f32[16,13,13]{2,0,1:T(8,128)} %param.13) | copy-start | bytes 32452
  6.3 2.1 %copy-start.9 = (bf16[1,128,2048]{2,1,0:T(8,128)(2,1)S(1)}, bf16[1,128,2048]{2,1,0:T(8,128)(2,1)}, u32[]{:S(2)}) copy-start(bf16[1,128,2048]{2,1,0:T(8,128)(2,1)} %param.7) | copy-start | bytes 1572868
  6.3 2.1 %copy-start.10 = (bf16[1,128,2048]{2,1,0:T(8,128)(2,1)S(1)}, bf16[1,128,2048]{2,1,0:T(8,128)(2,1)}, u32[]{:S(2)}) copy-start(bf16[1,128,2048]{2,1,0:T(8,128)(2,1)} %param.10) | copy-start | bytes 1572868
  9.6 27.9 %copy-start.3 = (bf16[2,32,1024]{2,1,0:T(8,128)(2,1)}, bf16[2,32,1024]{2,1,0:T(8,128)(2,1)S(1)}, u32[]{:S(2)}) copy-start(bf16[2,32,1024]{2,1,0:T(8,128)(2,1)S(1)} %pad_maximum_fusion.8) | copy-start | bytes 393220
  9.6 8.7 %collective-permute-start.6 = (bf16[64,1024]{1,0:T(8,128)(2,1)S(1)}, bf16[64,1024]{1,0:T(8,128)(2,1)S(1)}, u32[]{:S(2)}, u32[]{:S(2)}) collective-permute-start(bf16[64,1024]{1,0:T(8,128)(2,1)S(1)} %bitcast.84), channel_id=1, source_target_pairs={{0,8},{1,9},{2,10},{3,11},{4,12},{5,13},{6,14},{7,15},{8,16},{9,17... | collective-permute-start | bytes 393224 | tf_op jit(solution)/shard_map/ppermute | solution.py:292
  11.0 10.5 %collective-permute-start.5 = (bf16[64,1024]{1,0:T(8,128)(2,1)S(1)}, bf16[64,1024]{1,0:T(8,128)(2,1)S(1)}, u32[]{:S(2)}, u32[]{:S(2)}) collective-permute-start(bf16[64,1024]{1,0:T(8,128)(2,1)S(1)} %bitcast.85), channel_id=1, source_target_pairs={{0,24},{1,25},{2,26},{3,27},{4,28},{5,29},{6,30},{7,31},{8,0},{9,1... | collective-permute-start | bytes 393224 | tf_op jit(solution)/shard_map/ppermute | solution.py:292
  14.1 19.5 %collective-permute-start.7 = (bf16[256,1024]{1,0:T(8,128)(2,1)S(1)}, bf16[256,1024]{1,0:T(8,128)(2,1)S(1)}, u32[]{:S(2)}, u32[]{:S(2)}) collective-permute-start(bf16[256,1024]{1,0:T(8,128)(2,1)S(1)} %pad_maximum_fusion.3), channel_id=1, source_target_pairs={{0,31},{1,2},{2,1},{3,4},{4,3},{5,6},{6,5},{7,8},{8,7},{9,10},{10,... | collective-permute-start | bytes 1572872 | tf_op jit(solution)/shard_map/ppermute | solution.py:322
  17.0 24.2 %collective-permute-start.2 = (bf16[256,1024]{1,0:T(8,128)(2,1)S(1)}, bf16[256,1024]{1,0:T(8,128)(2,1)}, u32[]{:S(2)}, u32[]{:S(2)}) collective-permute-start(bf16[256,1024]{1,0:T(8,128)(2,1)S(1)} %pad_maximum_fusion.3), channel_id=1, source_target_pairs={{0,1},{1,0},{2,3},{3,2},{4,5},{5,4},{6,7},{7,6},{8,9},{9,8},{10,11... | collective-permute-start | bytes 1572872 | tf_op jit(solution)/shard_map/ppermute | solution.py:292
  18.1 23.1 %collective-permute-start.4 = (bf16[256,1024]{1,0:T(8,128)(2,1)S(1)}, bf16[256,1024]{1,0:T(8,128)(2,1)}, u32[]{:S(2)}, u32[]{:S(2)}) collective-permute-start(bf16[256,1024]{1,0:T(8,128)(2,1)S(1)} %pad_maximum_fusion.5), channel_id=1, source_target_pairs={{0,1},{1,0},{2,3},{3,2},{4,5},{5,4},{6,7},{7,6},{8,9},{9,8},{10,11... | collective-permute-start | bytes 1572872 | tf_op jit(solution)/shard_map/ppermute | solution.py:292
  18.2 24.3 %copy-start.4 = (bf16[64,1024]{1,0:T(8,128)(2,1)}, bf16[64,1024]{1,0:T(8,128)(2,1)S(1)}, u32[]{:S(2)}) copy-start(bf16[64,1024]{1,0:T(8,128)(2,1)S(1)} %collective-permute-done.6.refs_10_) | copy-start | bytes 393220
  18.2 23.0 %collective-permute-start.8 = (bf16[256,1024]{1,0:T(8,128)(2,1)S(1)}, bf16[256,1024]{1,0:T(8,128)(2,1)}, u32[]{:S(2)}, u32[]{:S(2)}) collective-permute-start(bf16[256,1024]{1,0:T(8,128)(2,1)S(1)} %pad_maximum_fusion.4), channel_id=1, source_target_pairs={{0,30},{1,3},{2,0},{3,5},{4,2},{5,7},{6,4},{7,9},{8,6},{9,11},{10,... | collective-permute-start | bytes 1572872 | tf_op jit(solution)/shard_map/ppermute | solution.py:325
  21.5 21.0 %copy-start.5 = (bf16[64,1024]{1,0:T(8,128)(2,1)}, bf16[64,1024]{1,0:T(8,128)(2,1)S(1)}, u32[]{:S(2)}) copy-start(bf16[64,1024]{1,0:T(8,128)(2,1)S(1)} %collective-permute-done.5.refs_9_) | copy-start | bytes 393220
  21.5 14.2 %collective-permute-start.11 = (bf16[128,1024]{1,0:T(8,128)(2,1)S(1)}, bf16[128,1024]{1,0:T(8,128)(2,1)}, u32[]{:S(2)}, u32[]{:S(2)}) collective-permute-start(bf16[128,1024]{1,0:T(8,128)(2,1)S(1)} %get-tuple-element.120), channel_id=1, source_target_pairs={{0,4},{1,5},{2,6},{3,7},{4,8},{5,9},{6,10},{7,11},{8,12},{9,13},{1... | collective-permute-start | bytes 786440 | tf_op jit(solution)/shard_map/ppermute | solution.py:292
  33.6 9.0 %copy-start.19 = (bf16[256,1024]{1,0:T(8,128)(2,1)}, bf16[256,1024]{1,0:T(8,128)(2,1)S(1)}, u32[]{:S(2)}) copy-start(bf16[256,1024]{1,0:T(8,128)(2,1)S(1)} %collective-permute-done.7.refs_6_) | copy-start | bytes 1572868
  33.6 7.6 %collective-permute-start.10 = (bf16[128,1024]{1,0:T(8,128)(2,1)S(1)}, bf16[128,1024]{1,0:T(8,128)(2,1)}, u32[]{:S(2)}, u32[]{:S(2)}) collective-permute-start(bf16[128,1024]{1,0:T(8,128)(2,1)S(1)} %get-tuple-element.121), channel_id=1, source_target_pairs={{0,28},{1,29},{2,30},{3,31},{4,0},{5,1},{6,2},{7,3},{8,4},{9,5},{1... | collective-permute-start | bytes 786440 | tf_op jit(solution)/shard_map/ppermute | solution.py:292
  35.7 6.8 %collective-permute-start.9 = (bf16[64,1024]{1,0:T(8,128)(2,1)S(1)}, bf16[64,1024]{1,0:T(8,128)(2,1)S(1)}, u32[]{:S(2)}, u32[]{:S(2)}) collective-permute-start(bf16[64,1024]{1,0:T(8,128)(2,1)S(1)} %broadcast_select_fusion), channel_id=1, source_target_pairs={{0,24},{1,9},{2,26},{3,11},{4,28},{5,13},{6,30},{7,15},{8,0},{9,17... | collective-permute-start | bytes 393224 | tf_op jit(solution)/shard_map/ppermute | solution.py:292
  55.0 25.3 %copy-start.2 = (bf16[512,1024]{1,0:T(8,128)(2,1)S(1)}, bf16[512,1024]{1,0:T(8,128)(2,1)}, u32[]{:S(2)}) copy-start(bf16[512,1024]{1,0:T(8,128)(2,1)} %get-tuple-element.91) | copy-start | bytes 3145732
  55.0 33.7 %collective-permute-start.19 = (bf16[512,1024]{1,0:T(8,128)(2,1)}, bf16[512,1024]{1,0:T(8,128)(2,1)S(1)}, u32[]{:S(2)}, u32[]{:S(2)}) collective-permute-start(bf16[512,1024]{1,0:T(8,128)(2,1)} %get-tuple-element.78), channel_id=1, source_target_pairs={{0,1},{1,0},{2,3},{3,2},{4,5},{5,4},{6,7},{7,6},{8,9},{9,8},{10,11... | collective-permute-start | bytes 3145736 | tf_op jit(solution)/shard_map/ppermute | solution.py:292
  55.3 18.3 %collective-permute-start.15 = (bf16[256,1024]{1,0:T(8,128)(2,1)}, bf16[256,1024]{1,0:T(8,128)(2,1)}, u32[]{:S(2)}, u32[]{:S(2)}) collective-permute-start(bf16[256,1024]{1,0:T(8,128)(2,1)} %get-tuple-element.85), channel_id=1, source_target_pairs={{1,2},{2,1},{5,6},{6,5},{9,10},{10,9},{13,14},{14,13},{17,18},{18,... | collective-permute-start | bytes 1572872 | tf_op jit(solution)/shard_map/ppermute | solution.py:427
  60.6 9.2 %collective-permute-start.14 = (bf16[80,1024]{1,0:T(8,128)(2,1)}, bf16[80,1024]{1,0:T(8,128)(2,1)S(1)}, u32[]{:S(2)}, u32[]{:S(2)}) collective-permute-start(bf16[80,1024]{1,0:T(8,128)(2,1)} %get-tuple-element.64), channel_id=1, source_target_pairs={{0,8},{1,25},{2,10},{3,27},{4,12},{5,29},{6,14},{7,31},{8,16},{9,1... | collective-permute-start | bytes 491528 | tf_op jit(solution)/shard_map/ppermute | solution.py:292
  64.3 7.0 %collective-permute-start.12 = (bf16[144,1024]{1,0:T(8,128)(2,1)}, bf16[144,1024]{1,0:T(8,128)(2,1)S(1)}, u32[]{:S(2)}, u32[]{:S(2)}) collective-permute-start(bf16[144,1024]{1,0:T(8,128)(2,1)} %get-tuple-element.62), channel_id=1, source_target_pairs={{0,4},{1,5},{2,6},{3,7},{4,8},{5,9},{6,10},{7,11},{8,12},{9,13},{1... | collective-permute-start | bytes 884744 | tf_op jit(solution)/shard_map/ppermute | solution.py:292
  64.3 9.3 %collective-permute-start.13 = (bf16[144,1024]{1,0:T(8,128)(2,1)}, bf16[144,1024]{1,0:T(8,128)(2,1)S(1)}, u32[]{:S(2)}, u32[]{:S(2)}) collective-permute-start(bf16[144,1024]{1,0:T(8,128)(2,1)} %get-tuple-element.63), channel_id=1, source_target_pairs={{0,28},{1,29},{2,30},{3,31},{4,0},{5,1},{6,2},{7,3},{8,4},{9,5},{1... | collective-permute-start | bytes 884744 | tf_op jit(solution)/shard_map/ppermute | solution.py:292
  69.8 3.8 %copy-start.6 = (bf16[80,1024]{1,0:T(8,128)(2,1)}, bf16[80,1024]{1,0:T(8,128)(2,1)S(1)}, u32[]{:S(2)}) copy-start(bf16[80,1024]{1,0:T(8,128)(2,1)S(1)} %collective-permute-done.14.four_ref) | copy-start | bytes 491524
  69.8 11.9 %collective-permute-start.18 = (bf16[256,1024]{1,0:T(8,128)(2,1)}, bf16[256,1024]{1,0:T(8,128)(2,1)S(1)}, u32[]{:S(2)}, u32[]{:S(2)}) collective-permute-start(bf16[256,1024]{1,0:T(8,128)(2,1)} %get-tuple-element.90), channel_id=1, source_target_pairs={{3,1},{0,2},{7,5},{4,6},{11,9},{8,10},{15,13},{12,14},{19,17},{16,... | collective-permute-start | bytes 1572872 | tf_op jit(solution)/shard_map/ppermute | solution.py:428
  71.3 2.3 %copy-start = (bf16[144,1024]{1,0:T(8,128)(2,1)}, bf16[144,1024]{1,0:T(8,128)(2,1)S(1)}, u32[]{:S(2)}) copy-start(bf16[144,1024]{1,0:T(8,128)(2,1)S(1)} %collective-permute-done.12.up_odd_ref.up_ref) | copy-start | bytes 884740
  73.6 0.7 copy-start.1
  76.7 9.9 %collective-permute-start.16 = (bf16[80,1024]{1,0:T(8,128)(2,1)}, bf16[80,1024]{1,0:T(8,128)(2,1)S(1)}, u32[]{:S(2)}, u32[]{:S(2)}) collective-permute-start(bf16[80,1024]{1,0:T(8,128)(2,1)} %get-tuple-element.76), channel_id=1, source_target_pairs={{0,8},{1,9},{2,10},{3,11},{4,12},{5,13},{6,14},{7,15},{8,16},{9,17... | collective-permute-start | bytes 491528 | tf_op jit(solution)/shard_map/ppermute | solution.py:292
  77.7 11.0 %collective-permute-start.17 = (bf16[80,1024]{1,0:T(8,128)(2,1)}, bf16[80,1024]{1,0:T(8,128)(2,1)S(1)}, u32[]{:S(2)}, u32[]{:S(2)}) collective-permute-start(bf16[80,1024]{1,0:T(8,128)(2,1)} %get-tuple-element.77), channel_id=1, source_target_pairs={{0,24},{1,25},{2,26},{3,27},{4,28},{5,29},{6,30},{7,31},{8,0},{9,1... | collective-permute-start | bytes 491528 | tf_op jit(solution)/shard_map/ppermute | solution.py:292
  80.3 15.2 %collective-permute-start.23 = (bf16[256,1024]{1,0:T(8,128)(2,1)}, bf16[256,1024]{1,0:T(8,128)(2,1)}, u32[]{:S(2)}, u32[]{:S(2)}) collective-permute-start(bf16[256,1024]{1,0:T(8,128)(2,1)} %get-tuple-element.85), channel_id=1, source_target_pairs={{0,31},{3,4},{4,3},{7,8},{8,7},{11,12},{12,11},{15,16},{16,15},{19... | collective-permute-start | bytes 1572872 | tf_op jit(solution)/shard_map/ppermute | solution.py:440
  81.8 29.4 %collective-permute-start.27 = (bf16[256,1024]{1,0:T(8,128)(2,1)}, bf16[256,1024]{1,0:T(8,128)(2,1)}, u32[]{:S(2)}, u32[]{:S(2)}) collective-permute-start(bf16[256,1024]{1,0:T(8,128)(2,1)} %get-tuple-element.90), channel_id=1, source_target_pairs={{30,0},{5,3},{2,4},{9,7},{6,8},{13,11},{10,12},{17,15},{14,16},{21... | collective-permute-start | bytes 1572872 | tf_op jit(solution)/shard_map/ppermute | solution.py:441
  86.5 2.1 %copy-start.7 = (bf16[80,1024]{1,0:T(8,128)(2,1)}, bf16[80,1024]{1,0:T(8,128)(2,1)S(1)}, u32[]{:S(2)}) copy-start(bf16[80,1024]{1,0:T(8,128)(2,1)S(1)} %collective-permute-done.16.up_two_ref) | copy-start | bytes 491524
  88.7 0.7 copy-start.8
  91.4 4.0 %collective-permute-start.20 = (bf16[32,1024]{1,0:T(8,128)(2,1)}, bf16[32,1024]{1,0:T(8,128)(2,1)S(1)}, u32[]{:S(2)}, u32[]{:S(2)}) collective-permute-start(bf16[32,1024]{1,0:T(8,128)(2,1)} %get-tuple-element.82), channel_id=1, source_target_pairs={{0,1},{1,0},{2,3},{3,2},{4,5},{5,4},{6,7},{7,6},{8,9},{9,8},{10,11... | collective-permute-start | bytes 196616 | tf_op jit(solution)/shard_map/ppermute | solution.py:292
  91.6 8.9 %collective-permute-start.21 = (bf16[32,1024]{1,0:T(8,128)(2,1)}, bf16[32,1024]{1,0:T(8,128)(2,1)S(1)}, u32[]{:S(2)}, u32[]{:S(2)}) collective-permute-start(bf16[32,1024]{1,0:T(8,128)(2,1)} %get-tuple-element.83), channel_id=1, source_target_pairs={{0,2},{1,3},{2,0},{3,1},{4,6},{5,7},{6,4},{7,5},{8,10},{9,11},{10,... | collective-permute-start | bytes 196616 | tf_op jit(solution)/shard_map/ppermute | solution.py:292
  93.3 8.7 %collective-permute-start.22 = (bf16[32,1024]{1,0:T(8,128)(2,1)}, bf16[32,1024]{1,0:T(8,128)(2,1)S(1)}, u32[]{:S(2)}, u32[]{:S(2)}) collective-permute-start(bf16[32,1024]{1,0:T(8,128)(2,1)} %get-tuple-element.84), channel_id=1, source_target_pairs={{0,3},{1,2},{2,1},{3,0},{4,7},{5,6},{6,5},{7,4},{8,11},{9,10},{10,... | collective-permute-start | bytes 196616 | tf_op jit(solution)/shard_map/ppermute | solution.py:292
  95.5 6.5 %copy-start.13 = (bf16[32,1024]{1,0:T(8,128)(2,1)}, bf16[32,1024]{1,0:T(8,128)(2,1)S(1)}, u32[]{:S(2)}) copy-start(bf16[32,1024]{1,0:T(8,128)(2,1)S(1)} %collective-permute-done.20.core_ref) | copy-start | bytes 196612
  100.5 1.4 %copy-start.14 = (bf16[32,1024]{1,0:T(8,128)(2,1)}, bf16[32,1024]{1,0:T(8,128)(2,1)S(1)}, u32[]{:S(2)}) copy-start(bf16[32,1024]{1,0:T(8,128)(2,1)S(1)} %collective-permute-done.21.side_ref) | copy-start | bytes 196612
  104.3 6.8 %copy-start.18 = (f32[32,128]{1,0:T(8,128)S(1)}, f32[32,128]{1,0:T(8,128)}, u32[]{:S(2)}) copy-start(f32[32,128]{1,0:T(8,128)} %get-tuple-element.89) | copy-start | bytes 49156
  104.4 4.7 %collective-permute-start.26 = (f32[32,128]{1,0:T(8,128)}, f32[32,128]{1,0:T(8,128)S(1)}, u32[]{:S(2)}, u32[]{:S(2)}) collective-permute-start(f32[32,128]{1,0:T(8,128)} %get-tuple-element.89), channel_id=1, source_target_pairs={{0,96},{1,97},{2,98},{3,99},{4,100},{5,101},{6,102},{7,103},{8,104... | collective-permute-start | bytes 49160 | tf_op jit(solution)/shard_map/ppermute | solution.py:413
  106.8 4.3 %collective-permute-start.25 = (f32[32,128]{1,0:T(8,128)}, f32[32,128]{1,0:T(8,128)S(1)}, u32[]{:S(2)}, u32[]{:S(2)}) collective-permute-start(f32[32,128]{1,0:T(8,128)} %get-tuple-element.89), channel_id=1, source_target_pairs={{0,64},{1,65},{2,66},{3,67},{4,68},{5,69},{6,70},{7,71},{8,72},{9,... | collective-permute-start | bytes 49160 | tf_op jit(solution)/shard_map/ppermute | solution.py:413
  107.4 3.8 %collective-permute-start.24 = (f32[32,128]{1,0:T(8,128)}, f32[32,128]{1,0:T(8,128)S(1)}, u32[]{:S(2)}, u32[]{:S(2)}) collective-permute-start(f32[32,128]{1,0:T(8,128)} %get-tuple-element.89), channel_id=1, source_target_pairs={{0,32},{1,33},{2,34},{3,35},{4,36},{5,37},{6,38},{7,39},{8,40},{9,... | collective-permute-start | bytes 49160 | tf_op jit(solution)/shard_map/ppermute | solution.py:413
  111.2 4.8 %collective-permute-start.28 = (f32[32,128]{1,0:T(8,128)S(1)}, f32[32,128]{1,0:T(8,128)S(1)}, u32[]{:S(2)}, u32[]{:S(2)}) collective-permute-start(f32[32,128]{1,0:T(8,128)S(1)} %add_add_fusion), channel_id=1, source_target_pairs={{0,128},{1,129},{2,130},{3,131},{4,132},{5,133},{6,134},{7,135},{8... | collective-permute-start | bytes 49160 | tf_op jit(solution)/shard_map/ppermute | solution.py:413
  114.1 0.8 copy-start.12
  (2 other events, 1.3 us)

commit v5 on v4

--- a/solution.py
+++ b/solution.py
@@ -421,6 +421,7 @@
         return [p for p in pairs if p[0] // 4 == p[1] // 4], [p for p in pairs if p[0] // 4 != p[1] // 4]
 
     edge_y, edge_z = beside(edge)
+    edge_y = edge_y + [(i, i ^ 3) for i, _ in edge_z]
     jump_y, jump_z = beside([(b, a) for a, b in jump])
     jump_y, jump_z = jump_y + [(i, i ^ 1) for i, _ in jump_z], jump_z + [(i, i ^ 1) for i, _ in jump_y]
     middle = (tile % 4 == 1) | (tile % 4 == 2)
@@ -452,7 +453,7 @@
     attended = joined(own[:rows], other[:rows])
     grad_q = joined(own[rows : 2 * rows], other[rows : 2 * rows])
     *quad, other_z = lax.optimization_barrier((*quad, other_z))
-    fine_other = wide(other[2 * rows :]) + wide(other_y) + wide(other_z)
+    fine_other = wide(other[2 * rows :]) + wide(jnp.where(middle, other_y, other_z))
     coarse_rows, bias = small_call(
         finish_kernel,
         half,

time: 119 us -> 117 us (0.983); the launches traced: 117 us -> 116 us
  waiting for transfers between devices: 37.4 us -> 33.6 us
  starting transfers between devices: 45 us -> 48.4 us
    ppermute x1, starting transfers between devices: 0.01 us -> 4.09 us  [shards(): mine_y = lax.ppermute(par_out, 'tile', jump_y)]
    ppermute x19, waiting for transfers between devices: 24.2 us -> 20.3 us  [send(): return lax.ppermute(x, 'tile', [(i, target(i)) for i in range(tiles)])]
    ppermute x1, starting transfers between devices: 5.34 us -> 3.39 us  [shards(): other_y = lax.ppermute(own_out, 'tile', edge_y)]
  transfers between devices with their start and end apart: 29 -> 29, of which waited for: 12 -> 10; matrix products, arithmetic and copies ran while one was open for 9% -> 9% of each run, Pallas kernels for 5% -> 5%
where the time goes in v5:
time: 117 us; the launch traced here: 116 us
  starting transfers between devices  48.4 us (41%)
  waiting for transfers between devices  33.6 us (29%)
  Pallas kernels  18.1 us (15%)
  other arithmetic  7.48 us (6%)
  local copies, waits for them, and re-layouts  7.47 us (6%)
    ppermute x19, starting transfers between devices, send(): return lax.ppermute(x, 'tile', [(i, target(i)) for i in range(tiles)])  26.3 us
    ppermute x19, waiting for transfers between devices, send(): return lax.ppermute(x, 'tile', [(i, target(i)) for i in range(tiles)])  20.3 us
    pallas_call x1, Pallas kernels, call_kernel(): pl.pallas_call(functools.partial(attention_kernel, inv_scale), grid_spec=...  11.8 us
    ppermute x1, waiting for transfers between devices, shards(): kv_own_out = lax.ppermute(kv_other, 'tile', edge)  11.1 us
    pallas_call x3, Pallas kernels, small_call(): pl.pallas_call(kernel, in_specs=smem + [pl.BlockSpec(memory_space=pltpu.V...  6.26 us
    ppermute x4, starting transfers between devices, flipped(): lax.ppermute(x, ('batch', 'tile'), [(i, i ^ mask) for i in range(every)])  5.94 us
    ppermute x1, starting transfers between devices, shards(): mine_z = lax.ppermute(par_out, 'tile', jump_z)  4.26 us
    ppermute x1, starting transfers between devices, shards(): mine_y = lax.ppermute(par_out, 'tile', jump_y)  4.09 us
  transfers between devices with their start and end apart: 29, of which 10 were waited for; matrix products, arithmetic and copies ran while one was open for 9% of the time, Pallas kernels for 5%

profile of v5, /device:TPU:1, one launch (start us, length us, event | category | flops | bytes accessed | tf_op | source)
XLA Modules:
  0.0 116.3 jit_solution(8270717667633466760)
XLA Ops:
  0.7 0.8 constant_dynamic-slice_fusion.4
  1.4 2.8 %collective-permute-start.1 = (bf16[2,8,1024]{2,1,0:T(8,128)(2,1)S(1)}, bf16[2,8,1024]{2,1,0:T(8,128)(2,1)S(1)}, u32[]{:S(2)}, u32[]{:S(2)}) collective-permute-start(bf16[2,8,1024]{2,1,0:T(8,128)(2,1)S(1)} %pad_maximum_fusion.9), channel_id=1, source_target_pairs={{0,3},{1,2},{2,1},{3,0},{4,7},{5,6},{6,5},{7,4},{8,11},{9,10},{10,... | collective-permute-start | bytes 98312 | tf_op jit(solution)/shard_map/ppermute | solution.py:292
  4.2 0.7 collective-permute-start
  4.9 1.3 %collective-permute-start.3 = (bf16[2,8,1024]{2,1,0:T(8,128)(2,1)S(1)}, bf16[2,8,1024]{2,1,0:T(8,128)(2,1)S(1)}, u32[]{:S(2)}, u32[]{:S(2)}) collective-permute-start(bf16[2,8,1024]{2,1,0:T(8,128)(2,1)S(1)} %pad_maximum_fusion.10), channel_id=1, source_target_pairs={{0,2},{1,3},{2,0},{3,1},{4,6},{5,7},{6,4},{7,5},{8,10},{9,11},{10,... | collective-permute-start | bytes 98312 | tf_op jit(solution)/shard_map/ppermute | solution.py:292
  6.3 1.4 %dynamic-slice_bitcast_fusion.2 = (bf16[128,1024]{1,0:T(8,128)(2,1)S(1)}, bf16[128,1024]{1,0:T(8,128)(2,1)S(1)}, bf16[128,1024]{1,0:T(8,128)(2,1)S(1)}, bf16[128,1024]{1,0:T(8,128)(2,1)S(1)}) fusion(bf16[1,128,2048]{2,1,0:T(8,128)(2,1)} %param.9, s32[]{:T(128)S(6)} %select_n.262, s32[]{:T(128)S(6)} %select_n.261, bf16[1,128,2048]{2,1,0:T(8,128)(2,1)} %param.8), kind=kLoop, calls=%fused_computation.21 | loop fusion | bytes 2097160 | tf_op jit(solution)/shard_map/dynamic_slice | solution.py:310
  8.7 0.9 and_convert_fusion.refs_15_
  9.6 1.4 %collective-permute-start.6 = (bf16[64,1024]{1,0:T(8,128)(2,1)S(1)}, bf16[64,1024]{1,0:T(8,128)(2,1)S(1)}, u32[]{:S(2)}, u32[]{:S(2)}) collective-permute-start(bf16[64,1024]{1,0:T(8,128)(2,1)S(1)} %bitcast.84), channel_id=1, source_target_pairs={{0,8},{1,9},{2,10},{3,11},{4,12},{5,13},{6,14},{7,15},{8,16},{9,17... | collective-permute-start | bytes 393224 | tf_op jit(solution)/shard_map/ppermute | solution.py:292
  11.0 3.1 %collective-permute-start.5 = (bf16[64,1024]{1,0:T(8,128)(2,1)S(1)}, bf16[64,1024]{1,0:T(8,128)(2,1)S(1)}, u32[]{:S(2)}, u32[]{:S(2)}) collective-permute-start(bf16[64,1024]{1,0:T(8,128)(2,1)S(1)} %bitcast.85), channel_id=1, source_target_pairs={{0,24},{1,25},{2,26},{3,27},{4,28},{5,29},{6,30},{7,31},{8,0},{9,1... | collective-permute-start | bytes 393224 | tf_op jit(solution)/shard_map/ppermute | solution.py:292
  14.1 2.1 %collective-permute-start.7 = (bf16[256,1024]{1,0:T(8,128)(2,1)S(1)}, bf16[256,1024]{1,0:T(8,128)(2,1)S(1)}, u32[]{:S(2)}, u32[]{:S(2)}) collective-permute-start(bf16[256,1024]{1,0:T(8,128)(2,1)S(1)} %pad_maximum_fusion.3), channel_id=1, source_target_pairs={{0,31},{1,2},{2,1},{3,4},{4,3},{5,6},{6,5},{7,8},{8,7},{9,10},{10,... | collective-permute-start | bytes 1572872 | tf_op jit(solution)/shard_map/ppermute | solution.py:322
  16.2 0.7 fusion.9.refs_14_
  17.0 1.2 %collective-permute-start.2 = (bf16[256,1024]{1,0:T(8,128)(2,1)S(1)}, bf16[256,1024]{1,0:T(8,128)(2,1)}, u32[]{:S(2)}, u32[]{:S(2)}) collective-permute-start(bf16[256,1024]{1,0:T(8,128)(2,1)S(1)} %pad_maximum_fusion.3), channel_id=1, source_target_pairs={{0,1},{1,0},{2,3},{3,2},{4,5},{5,4},{6,7},{7,6},{8,9},{9,8},{10,11... | collective-permute-start | bytes 1572872 | tf_op jit(solution)/shard_map/ppermute | solution.py:292
  18.2 0.8 collective-permute-start.8
  19.0 2.4 %collective-permute-done.5.refs_9_ = bf16[64,1024]{1,0:T(8,128)(2,1)S(1)} collective-permute-done((bf16[64,1024]{1,0:T(8,128)(2,1)S(1)}, bf16[64,1024]{1,0:T(8,128)(2,1)S(1)}, u32[]{:S(2)}, u32[]{:S(2)}) %collective-permute-start.5) | collective-permute-done | bytes 131104 | tf_op jit(solution)/shard_map/ppermute | solution.py:292
  21.5 0.9 collective-permute-start.11
  22.5 11.1 %collective-permute-done.7.refs_6_ = bf16[256,1024]{1,0:T(8,128)(2,1)S(1)} collective-permute-done((bf16[256,1024]{1,0:T(8,128)(2,1)S(1)}, bf16[256,1024]{1,0:T(8,128)(2,1)S(1)}, u32[]{:S(2)}, u32[]{:S(2)}) %collective-permute-start.7) | collective-permute-done | bytes 524320 | tf_op jit(solution)/shard_map/ppermute | solution.py:322
  33.6 2.1 %collective-permute-start.10 = (bf16[128,1024]{1,0:T(8,128)(2,1)S(1)}, bf16[128,1024]{1,0:T(8,128)(2,1)}, u32[]{:S(2)}, u32[]{:S(2)}) collective-permute-start(bf16[128,1024]{1,0:T(8,128)(2,1)S(1)} %get-tuple-element.121), channel_id=1, source_target_pairs={{0,28},{1,29},{2,30},{3,31},{4,0},{5,1},{6,2},{7,3},{8,4},{9,5},{1... | collective-permute-start | bytes 786440 | tf_op jit(solution)/shard_map/ppermute | solution.py:292
  35.9 0.8 copy.27.refs_17_
  36.7 0.7 fusion.11.refs_16_
  37.4 3.8 %collective-permute-done.10.refs_12_ = bf16[128,1024]{1,0:T(8,128)(2,1)} collective-permute-done((bf16[128,1024]{1,0:T(8,128)(2,1)S(1)}, bf16[128,1024]{1,0:T(8,128)(2,1)}, u32[]{:S(2)}, u32[]{:S(2)}) %collective-permute-start.10) | collective-permute-done | bytes 262176 | tf_op jit(solution)/shard_map/ppermute | solution.py:292
  41.2 1.3 %collective-permute-done.9.refs_11_ = bf16[64,1024]{1,0:T(8,128)(2,1)S(1)} collective-permute-done((bf16[64,1024]{1,0:T(8,128)(2,1)S(1)}, bf16[64,1024]{1,0:T(8,128)(2,1)S(1)}, u32[]{:S(2)}, u32[]{:S(2)}) %collective-permute-start.9) | collective-permute-done | bytes 131104 | tf_op jit(solution)/shard_map/ppermute | solution.py:292
  43.1 11.8 %shard_map.110 = (bf16[512,1024]{1,0:T(8,128)(2,1)}, bf16[512,1024]{1,0:T(8,128)(2,1)}, bf16[256,1024]{1,0:T(8,128)(2,1)}, bf16[256,1024]{1,0:T(8,128)(2,1)}, bf...) custom-call(s32[1]{0:T(128)} %bitcast.half_ref, ...), custom_call_target="tpu_custom_call" | custom-call | flops 2013265920 | bytes 10485760 | tf_op jit(solution)/shard_map/pallas_call | solution.py:261
  55.3 3.4 %collective-permute-start.15 = (bf16[256,1024]{1,0:T(8,128)(2,1)}, bf16[256,1024]{1,0:T(8,128)(2,1)}, u32[]{:S(2)}, u32[]{:S(2)}) collective-permute-start(bf16[256,1024]{1,0:T(8,128)(2,1)} %get-tuple-element.85), channel_id=1, source_target_pairs={{1,2},{2,1},{5,6},{6,5},{9,10},{10,9},{13,14},{14,13},{17,18},{18,... | collective-permute-start | bytes 1572872 | tf_op jit(solution)/shard_map/ppermute | solution.py:428
  58.6 3.6 %collective-permute-start.14 = (bf16[80,1024]{1,0:T(8,128)(2,1)}, bf16[80,1024]{1,0:T(8,128)(2,1)S(1)}, u32[]{:S(2)}, u32[]{:S(2)}) collective-permute-start(bf16[80,1024]{1,0:T(8,128)(2,1)} %get-tuple-element.64), channel_id=1, source_target_pairs={{0,8},{1,25},{2,10},{3,27},{4,12},{5,29},{6,14},{7,31},{8,16},{9,1... | collective-permute-start | bytes 491528 | tf_op jit(solution)/shard_map/ppermute | solution.py:292
  62.3 2.7 %collective-permute-start.13 = (bf16[144,1024]{1,0:T(8,128)(2,1)}, bf16[144,1024]{1,0:T(8,128)(2,1)S(1)}, u32[]{:S(2)}, u32[]{:S(2)}) collective-permute-start(bf16[144,1024]{1,0:T(8,128)(2,1)} %get-tuple-element.63), channel_id=1, source_target_pairs={{0,28},{1,29},{2,30},{3,31},{4,0},{5,1},{6,2},{7,3},{8,4},{9,5},{1... | collective-permute-start | bytes 884744 | tf_op jit(solution)/shard_map/ppermute | solution.py:292
  65.0 1.1 collective-permute-done.14.four_ref
  66.1 4.1 %collective-permute-start.18 = (bf16[256,1024]{1,0:T(8,128)(2,1)}, bf16[256,1024]{1,0:T(8,128)(2,1)S(1)}, u32[]{:S(2)}, u32[]{:S(2)}) collective-permute-start(bf16[256,1024]{1,0:T(8,128)(2,1)} %get-tuple-element.90), channel_id=1, source_target_pairs={{3,1},{0,2},{7,5},{4,6},{11,9},{8,10},{15,13},{12,14},{19,17},{16,... | collective-permute-start | bytes 1572872 | tf_op jit(solution)/shard_map/ppermute | solution.py:429
  70.2 2.7 %collective-permute-done.12.up_odd_ref.up_ref = bf16[144,1024]{1,0:T(8,128)(2,1)S(1)} collective-permute-done((bf16[144,1024]{1,0:T(8,128)(2,1)}, bf16[144,1024]{1,0:T(8,128)(2,1)S(1)}, u32[]{:S(2)}, u32[]{:S(2)}) %collective-permute-start.12) | collective-permute-done | bytes 294944 | tf_op jit(solution)/shard_map/ppermute | solution.py:292
  72.9 0.7 copy-done
  73.7 2.3 %shard_map.111 = (bf16[80,1024]{1,0:T(8,128)(2,1)}, bf16[80,1024]{1,0:T(8,128)(2,1)}) custom-call(s32[1]{0:T(128)} %bitcast.half_ref, bf16[80,1024]{1,0:T(8,128)(2,1)} %get-tuple-element.71.up_ref, bf16[80,1024]{1,0:T(8,128)(2,1)} %get-tuple-element.72.down_ref, bf16[80,1024]{1,0:T(8,128)(2,1)} %copy-done.6, bf16[144,1024]{1,0:T(8,128)(2,1)} %copy-done, ...), custom_call_target="tpu_custom_call" | custom-call | flops 1000000 | bytes 1000000 | tf_op jit(solution)/shard_map/pallas_call | solution.py:116
  76.0 3.6 %collective-permute-start.17 = (bf16[80,1024]{1,0:T(8,128)(2,1)}, bf16[80,1024]{1,0:T(8,128)(2,1)S(1)}, u32[]{:S(2)}, u32[]{:S(2)}) collective-permute-start(bf16[80,1024]{1,0:T(8,128)(2,1)} %get-tuple-element.77), channel_id=1, source_target_pairs={{0,24},{1,25},{2,26},{3,27},{4,28},{5,29},{6,30},{7,31},{8,0},{9,1... | collective-permute-start | bytes 491528 | tf_op jit(solution)/shard_map/ppermute | solution.py:292
  79.7 1.5 %collective-permute-start.23 = (bf16[256,1024]{1,0:T(8,128)(2,1)}, bf16[256,1024]{1,0:T(8,128)(2,1)}, u32[]{:S(2)}, u32[]{:S(2)}) collective-permute-start(bf16[256,1024]{1,0:T(8,128)(2,1)} %get-tuple-element.85), channel_id=1, source_target_pairs={{0,31},{3,4},{4,3},{7,8},{8,7},{11,12},{12,11},{15,16},{16,15},{19... | collective-permute-start | bytes 1572872 | tf_op jit(solution)/shard_map/ppermute | solution.py:441
  81.1 4.3 %collective-permute-start.27 = (bf16[256,1024]{1,0:T(8,128)(2,1)}, bf16[256,1024]{1,0:T(8,128)(2,1)}, u32[]{:S(2)}, u32[]{:S(2)}) collective-permute-start(bf16[256,1024]{1,0:T(8,128)(2,1)} %get-tuple-element.90), channel_id=1, source_target_pairs={{30,0},{5,3},{2,4},{9,7},{6,8},{13,11},{10,12},{17,15},{14,16},{21... | collective-permute-start | bytes 1572872 | tf_op jit(solution)/shard_map/ppermute | solution.py:442
  85.4 2.0 %collective-permute-done.16.up_two_ref = bf16[80,1024]{1,0:T(8,128)(2,1)S(1)} collective-permute-done((bf16[80,1024]{1,0:T(8,128)(2,1)}, bf16[80,1024]{1,0:T(8,128)(2,1)S(1)}, u32[]{:S(2)}, u32[]{:S(2)}) %collective-permute-start.16) | collective-permute-done | bytes 163872 | tf_op jit(solution)/shard_map/ppermute | solution.py:292
  87.4 0.7 copy-done.7
  88.1 2.1 %shard_map.112 = (f32[32,1024]{1,0:T(8,128)}, bf16[32,1024]{1,0:T(8,128)(2,1)}, bf16[32,1024]{1,0:T(8,128)(2,1)}, bf16[32,1024]{1,0:T(8,128)(2,1)}) custom-call(bf16[80,1024]{1,0:T(8,128)(2,1)} %get-tuple-element.61.here_ref, bf16[144,1024]{1,0:T(8,128)(2,1)} %copy-done, bf16[144,1024]{1,0:T(8,128)(2,1)} %copy-done.1, bf16[80,1024]{1,0:T(8,128)(2,1)} %copy-done.7, ...), custom_call_target="tpu_custom_call" | custom-call | flops 1000000 | bytes 1000000 | tf_op jit(solution)/shard_map/pallas_call | solution.py:116
  90.2 0.7 collective-permute-start.20
  91.4 1.2 %collective-permute-start.22 = (bf16[32,1024]{1,0:T(8,128)(2,1)}, bf16[32,1024]{1,0:T(8,128)(2,1)S(1)}, u32[]{:S(2)}, u32[]{:S(2)}) collective-permute-start(bf16[32,1024]{1,0:T(8,128)(2,1)} %get-tuple-element.84), channel_id=1, source_target_pairs={{0,3},{1,2},{2,1},{3,0},{4,7},{5,6},{6,5},{7,4},{8,11},{9,10},{10,... | collective-permute-start | bytes 196616 | tf_op jit(solution)/shard_map/ppermute | solution.py:292
  92.7 0.9 maximum_select_fusion.1
  93.6 0.9 maximum_select_fusion
  94.5 5.6 %collective-permute-done.21.side_ref = bf16[32,1024]{1,0:T(8,128)(2,1)S(1)} collective-permute-done((bf16[32,1024]{1,0:T(8,128)(2,1)}, bf16[32,1024]{1,0:T(8,128)(2,1)S(1)}, u32[]{:S(2)}, u32[]{:S(2)}) %collective-permute-start.21) | collective-permute-done | bytes 65568 | tf_op jit(solution)/shard_map/ppermute | solution.py:292
  100.1 1.4 %collective-permute-done.22.corner_ref = bf16[32,1024]{1,0:T(8,128)(2,1)S(1)} collective-permute-done((bf16[32,1024]{1,0:T(8,128)(2,1)}, bf16[32,1024]{1,0:T(8,128)(2,1)S(1)}, u32[]{:S(2)}, u32[]{:S(2)}) %collective-permute-start.22) | collective-permute-done | bytes 65568 | tf_op jit(solution)/shard_map/ppermute | solution.py:292
  102.1 1.8 %shard_map.113 = (bf16[16,2048]{1,0:T(8,128)(2,1)}, f32[32,128]{1,0:T(8,128)}) custom-call(s32[1]{0:T(128)} %bitcast.half_ref, f32[32,1024]{1,0:T(8,128)} %get-tuple-element.81.keep_ref, bf16[32,1024]{1,0:T(8,128)(2,1)} %copy-done.13, bf16[32,1024]{1,0:T(8,128)(2,1)} %copy-done.14, bf16[32,1024]{1,0:T(8,128)(2,1)} %copy-done.15), custom_call_target="tpu_custom_call" | custom-call | flops 1000000 | bytes 1000000 | tf_op jit(solution)/shard_map/pallas_call | solution.py:116
  103.9 2.5 %collective-permute-start.26 = (f32[32,128]{1,0:T(8,128)}, f32[32,128]{1,0:T(8,128)S(1)}, u32[]{:S(2)}, u32[]{:S(2)}) collective-permute-start(f32[32,128]{1,0:T(8,128)} %get-tuple-element.89), channel_id=1, source_target_pairs={{0,96},{1,97},{2,98},{3,99},{4,100},{5,101},{6,102},{7,103},{8,104... | collective-permute-start | bytes 49160 | tf_op jit(solution)/shard_map/ppermute | solution.py:413
  107.1 1.3 %convert_add_fusion = bf16[256,1024]{1,0:T(8,128)(2,1)S(1)} fusion(bf16[256,1024]{1,0:T(8,128)(2,1)} %collective-permute-done.15, bf16[256,1024]{1,0:T(8,128)(2,1)} %collective-permute-done.23, bf16[512,1024]{1,0:T(8,128)(2,1)S(1)} %collective-permute-done.19, pred[]{:T(512)S(6)} %or.3), kind=kLoop, calls=%fused_computation.7 | loop fusion | flops 1310720 | bytes 2097153 | tf_op jit(solution)/shard_map/add | solution.py:456
  108.5 2.2 %collective-permute-done.25 = f32[32,128]{1,0:T(8,128)S(1)} collective-permute-done((f32[32,128]{1,0:T(8,128)}, f32[32,128]{1,0:T(8,128)S(1)}, u32[]{:S(2)}, u32[]{:S(2)}) %collective-permute-start.25) | collective-permute-done | bytes 16416 | tf_op jit(solution)/shard_map/ppermute | solution.py:413
  110.7 2.7 %collective-permute-start.28 = (f32[32,128]{1,0:T(8,128)S(1)}, f32[32,128]{1,0:T(8,128)S(1)}, u32[]{:S(2)}, u32[]{:S(2)}) collective-permute-start(f32[32,128]{1,0:T(8,128)S(1)} %add_add_fusion), channel_id=1, source_target_pairs={{0,128},{1,129},{2,130},{3,131},{4,132},{5,133},{6,134},{7,135},{8... | collective-permute-start | bytes 49160 | tf_op jit(solution)/shard_map/ppermute | solution.py:413
  114.5 1.0 pad_maximum_fusion.2
  115.7 0.7 slice.47
  (104 shorter events, 5.6 us)
Async XLA Ops:
  1.4 8.1 %collective-permute-start.1 = (bf16[2,8,1024]{2,1,0:T(8,128)(2,1)S(1)}, bf16[2,8,1024]{2,1,0:T(8,128)(2,1)S(1)}, u32[]{:S(2)}, u32[]{:S(2)}) collective-permute-start(bf16[2,8,1024]{2,1,0:T(8,128)(2,1)S(1)} %pad_maximum_fusion.9), channel_id=1, source_target_pairs={{0,3},{1,2},{2,1},{3,0},{4,7},{5,6},{6,5},{7,4},{8,11},{9,10},{10,... | collective-permute-start | bytes 98312 | tf_op jit(solution)/shard_map/ppermute | solution.py:292
  4.2 5.3 %collective-permute-start = (bf16[2,8,1024]{2,1,0:T(8,128)(2,1)S(1)}, bf16[2,8,1024]{2,1,0:T(8,128)(2,1)S(1)}, u32[]{:S(2)}, u32[]{:S(2)}) collective-permute-start(bf16[2,8,1024]{2,1,0:T(8,128)(2,1)S(1)} %pad_maximum_fusion.9), channel_id=1, source_target_pairs={{0,1},{1,0},{2,3},{3,2},{4,5},{5,4},{6,7},{7,6},{8,9},{9,8},{10,11... | collective-permute-start | bytes 98312 | tf_op jit(solution)/shard_map/ppermute | solution.py:292
  4.9 4.7 %collective-permute-start.3 = (bf16[2,8,1024]{2,1,0:T(8,128)(2,1)S(1)}, bf16[2,8,1024]{2,1,0:T(8,128)(2,1)S(1)}, u32[]{:S(2)}, u32[]{:S(2)}) collective-permute-start(bf16[2,8,1024]{2,1,0:T(8,128)(2,1)S(1)} %pad_maximum_fusion.10), channel_id=1, source_target_pairs={{0,2},{1,3},{2,0},{3,1},{4,6},{5,7},{6,4},{7,5},{8,10},{9,11},{10,... | collective-permute-start | bytes 98312 | tf_op jit(solution)/shard_map/ppermute | solution.py:292
  6.3 1.4 %copy-start.16 = (s32[4096]{0:T(1024)S(1)}, s32[4096]{0:T(1024)}, u32[]{:S(2)}) copy-start(s32[4096]{0:T(1024)} %param.12) | copy-start | bytes 49156
  6.3 1.4 %copy-start.17 = (s32[1,4096]{1,0:T(1,128)S(1)}, s32[1,4096]{1,0:T(1,128)}, u32[]{:S(2)}) copy-start(s32[1,4096]{1,0:T(1,128)} %param.11) | copy-start | bytes 49156
  6.3 2.1 %copy-start.11 = (f32[16,13,13]{2,0,1:T(8,128)S(1)}, f32[16,13,13]{2,0,1:T(8,128)}, u32[]{:S(2)}) copy-start(f32[16,13,13]{2,0,1:T(8,128)} %param.13) | copy-start | bytes 32452
  6.3 2.1 %copy-start.9 = (bf16[1,128,2048]{2,1,0:T(8,128)(2,1)S(1)}, bf16[1,128,2048]{2,1,0:T(8,128)(2,1)}, u32[]{:S(2)}) copy-start(bf16[1,128,2048]{2,1,0:T(8,128)(2,1)} %param.7) | copy-start | bytes 1572868
  6.3 2.1 %copy-start.10 = (bf16[1,128,2048]{2,1,0:T(8,128)(2,1)S(1)}, bf16[1,128,2048]{2,1,0:T(8,128)(2,1)}, u32[]{:S(2)}) copy-start(bf16[1,128,2048]{2,1,0:T(8,128)(2,1)} %param.10) | copy-start | bytes 1572868
  9.6 27.9 %copy-start.3 = (bf16[2,32,1024]{2,1,0:T(8,128)(2,1)}, bf16[2,32,1024]{2,1,0:T(8,128)(2,1)S(1)}, u32[]{:S(2)}) copy-start(bf16[2,32,1024]{2,1,0:T(8,128)(2,1)S(1)} %pad_maximum_fusion.8) | copy-start | bytes 393220
  9.6 8.7 %collective-permute-start.6 = (bf16[64,1024]{1,0:T(8,128)(2,1)S(1)}, bf16[64,1024]{1,0:T(8,128)(2,1)S(1)}, u32[]{:S(2)}, u32[]{:S(2)}) collective-permute-start(bf16[64,1024]{1,0:T(8,128)(2,1)S(1)} %bitcast.84), channel_id=1, source_target_pairs={{0,8},{1,9},{2,10},{3,11},{4,12},{5,13},{6,14},{7,15},{8,16},{9,17... | collective-permute-start | bytes 393224 | tf_op jit(solution)/shard_map/ppermute | solution.py:292
  11.0 10.5 %collective-permute-start.5 = (bf16[64,1024]{1,0:T(8,128)(2,1)S(1)}, bf16[64,1024]{1,0:T(8,128)(2,1)S(1)}, u32[]{:S(2)}, u32[]{:S(2)}) collective-permute-start(bf16[64,1024]{1,0:T(8,128)(2,1)S(1)} %bitcast.85), channel_id=1, source_target_pairs={{0,24},{1,25},{2,26},{3,27},{4,28},{5,29},{6,30},{7,31},{8,0},{9,1... | collective-permute-start | bytes 393224 | tf_op jit(solution)/shard_map/ppermute | solution.py:292
  14.1 19.5 %collective-permute-start.7 = (bf16[256,1024]{1,0:T(8,128)(2,1)S(1)}, bf16[256,1024]{1,0:T(8,128)(2,1)S(1)}, u32[]{:S(2)}, u32[]{:S(2)}) collective-permute-start(bf16[256,1024]{1,0:T(8,128)(2,1)S(1)} %pad_maximum_fusion.3), channel_id=1, source_target_pairs={{0,31},{1,2},{2,1},{3,4},{4,3},{5,6},{6,5},{7,8},{8,7},{9,10},{10,... | collective-permute-start | bytes 1572872 | tf_op jit(solution)/shard_map/ppermute | solution.py:322
  17.0 24.2 %collective-permute-start.2 = (bf16[256,1024]{1,0:T(8,128)(2,1)S(1)}, bf16[256,1024]{1,0:T(8,128)(2,1)}, u32[]{:S(2)}, u32[]{:S(2)}) collective-permute-start(bf16[256,1024]{1,0:T(8,128)(2,1)S(1)} %pad_maximum_fusion.3), channel_id=1, source_target_pairs={{0,1},{1,0},{2,3},{3,2},{4,5},{5,4},{6,7},{7,6},{8,9},{9,8},{10,11... | collective-permute-start | bytes 1572872 | tf_op jit(solution)/shard_map/ppermute | solution.py:292
  18.1 23.1 %collective-permute-start.4 = (bf16[256,1024]{1,0:T(8,128)(2,1)S(1)}, bf16[256,1024]{1,0:T(8,128)(2,1)}, u32[]{:S(2)}, u32[]{:S(2)}) collective-permute-start(bf16[256,1024]{1,0:T(8,128)(2,1)S(1)} %pad_maximum_fusion.5), channel_id=1, source_target_pairs={{0,1},{1,0},{2,3},{3,2},{4,5},{5,4},{6,7},{7,6},{8,9},{9,8},{10,11... | collective-permute-start | bytes 1572872 | tf_op jit(solution)/shard_map/ppermute | solution.py:292
  18.2 24.3 %copy-start.4 = (bf16[64,1024]{1,0:T(8,128)(2,1)}, bf16[64,1024]{1,0:T(8,128)(2,1)S(1)}, u32[]{:S(2)}) copy-start(bf16[64,1024]{1,0:T(8,128)(2,1)S(1)} %collective-permute-done.6.refs_10_) | copy-start | bytes 393220
  18.2 23.0 %collective-permute-start.8 = (bf16[256,1024]{1,0:T(8,128)(2,1)S(1)}, bf16[256,1024]{1,0:T(8,128)(2,1)}, u32[]{:S(2)}, u32[]{:S(2)}) collective-permute-start(bf16[256,1024]{1,0:T(8,128)(2,1)S(1)} %pad_maximum_fusion.4), channel_id=1, source_target_pairs={{0,30},{1,3},{2,0},{3,5},{4,2},{5,7},{6,4},{7,9},{8,6},{9,11},{10,... | collective-permute-start | bytes 1572872 | tf_op jit(solution)/shard_map/ppermute | solution.py:325
  21.5 21.0 %copy-start.5 = (bf16[64,1024]{1,0:T(8,128)(2,1)}, bf16[64,1024]{1,0:T(8,128)(2,1)S(1)}, u32[]{:S(2)}) copy-start(bf16[64,1024]{1,0:T(8,128)(2,1)S(1)} %collective-permute-done.5.refs_9_) | copy-start | bytes 393220
  21.5 14.2 %collective-permute-start.11 = (bf16[128,1024]{1,0:T(8,128)(2,1)S(1)}, bf16[128,1024]{1,0:T(8,128)(2,1)}, u32[]{:S(2)}, u32[]{:S(2)}) collective-permute-start(bf16[128,1024]{1,0:T(8,128)(2,1)S(1)} %get-tuple-element.120), channel_id=1, source_target_pairs={{0,4},{1,5},{2,6},{3,7},{4,8},{5,9},{6,10},{7,11},{8,12},{9,13},{1... | collective-permute-start | bytes 786440 | tf_op jit(solution)/shard_map/ppermute | solution.py:292
  33.6 9.0 %copy-start.19 = (bf16[256,1024]{1,0:T(8,128)(2,1)}, bf16[256,1024]{1,0:T(8,128)(2,1)S(1)}, u32[]{:S(2)}) copy-start(bf16[256,1024]{1,0:T(8,128)(2,1)S(1)} %collective-permute-done.7.refs_6_) | copy-start | bytes 1572868
  33.6 7.6 %collective-permute-start.10 = (bf16[128,1024]{1,0:T(8,128)(2,1)S(1)}, bf16[128,1024]{1,0:T(8,128)(2,1)}, u32[]{:S(2)}, u32[]{:S(2)}) collective-permute-start(bf16[128,1024]{1,0:T(8,128)(2,1)S(1)} %get-tuple-element.121), channel_id=1, source_target_pairs={{0,28},{1,29},{2,30},{3,31},{4,0},{5,1},{6,2},{7,3},{8,4},{9,5},{1... | collective-permute-start | bytes 786440 | tf_op jit(solution)/shard_map/ppermute | solution.py:292
  35.7 6.8 %collective-permute-start.9 = (bf16[64,1024]{1,0:T(8,128)(2,1)S(1)}, bf16[64,1024]{1,0:T(8,128)(2,1)S(1)}, u32[]{:S(2)}, u32[]{:S(2)}) collective-permute-start(bf16[64,1024]{1,0:T(8,128)(2,1)S(1)} %broadcast_select_fusion), channel_id=1, source_target_pairs={{0,24},{1,9},{2,26},{3,11},{4,28},{5,13},{6,30},{7,15},{8,0},{9,17... | collective-permute-start | bytes 393224 | tf_op jit(solution)/shard_map/ppermute | solution.py:292
  55.0 24.7 %copy-start.2 = (bf16[512,1024]{1,0:T(8,128)(2,1)S(1)}, bf16[512,1024]{1,0:T(8,128)(2,1)}, u32[]{:S(2)}) copy-start(bf16[512,1024]{1,0:T(8,128)(2,1)} %get-tuple-element.91) | copy-start | bytes 3145732
  55.0 32.4 %collective-permute-start.19 = (bf16[512,1024]{1,0:T(8,128)(2,1)}, bf16[512,1024]{1,0:T(8,128)(2,1)S(1)}, u32[]{:S(2)}, u32[]{:S(2)}) collective-permute-start(bf16[512,1024]{1,0:T(8,128)(2,1)} %get-tuple-element.78), channel_id=1, source_target_pairs={{0,1},{1,0},{2,3},{3,2},{4,5},{5,4},{6,7},{7,6},{8,9},{9,8},{10,11... | collective-permute-start | bytes 3145736 | tf_op jit(solution)/shard_map/ppermute | solution.py:292
  55.3 17.6 %collective-permute-start.15 = (bf16[256,1024]{1,0:T(8,128)(2,1)}, bf16[256,1024]{1,0:T(8,128)(2,1)}, u32[]{:S(2)}, u32[]{:S(2)}) collective-permute-start(bf16[256,1024]{1,0:T(8,128)(2,1)} %get-tuple-element.85), channel_id=1, source_target_pairs={{1,2},{2,1},{5,6},{6,5},{9,10},{10,9},{13,14},{14,13},{17,18},{18,... | collective-permute-start | bytes 1572872 | tf_op jit(solution)/shard_map/ppermute | solution.py:428
  58.6 7.4 %collective-permute-start.14 = (bf16[80,1024]{1,0:T(8,128)(2,1)}, bf16[80,1024]{1,0:T(8,128)(2,1)S(1)}, u32[]{:S(2)}, u32[]{:S(2)}) collective-permute-start(bf16[80,1024]{1,0:T(8,128)(2,1)} %get-tuple-element.64), channel_id=1, source_target_pairs={{0,8},{1,25},{2,10},{3,27},{4,12},{5,29},{6,14},{7,31},{8,16},{9,1... | collective-permute-start | bytes 491528 | tf_op jit(solution)/shard_map/ppermute | solution.py:292
  62.3 10.6 %collective-permute-start.12 = (bf16[144,1024]{1,0:T(8,128)(2,1)}, bf16[144,1024]{1,0:T(8,128)(2,1)S(1)}, u32[]{:S(2)}, u32[]{:S(2)}) collective-permute-start(bf16[144,1024]{1,0:T(8,128)(2,1)} %get-tuple-element.62), channel_id=1, source_target_pairs={{0,4},{1,5},{2,6},{3,7},{4,8},{5,9},{6,10},{7,11},{8,12},{9,13},{1... | collective-permute-start | bytes 884744 | tf_op jit(solution)/shard_map/ppermute | solution.py:292
  62.3 10.6 %collective-permute-start.13 = (bf16[144,1024]{1,0:T(8,128)(2,1)}, bf16[144,1024]{1,0:T(8,128)(2,1)S(1)}, u32[]{:S(2)}, u32[]{:S(2)}) collective-permute-start(bf16[144,1024]{1,0:T(8,128)(2,1)} %get-tuple-element.63), channel_id=1, source_target_pairs={{0,28},{1,29},{2,30},{3,31},{4,0},{5,1},{6,2},{7,3},{8,4},{9,5},{1... | collective-permute-start | bytes 884744 | tf_op jit(solution)/shard_map/ppermute | solution.py:292
  66.1 6.8 %copy-start.6 = (bf16[80,1024]{1,0:T(8,128)(2,1)}, bf16[80,1024]{1,0:T(8,128)(2,1)S(1)}, u32[]{:S(2)}) copy-start(bf16[80,1024]{1,0:T(8,128)(2,1)S(1)} %collective-permute-done.14.four_ref) | copy-start | bytes 491524
  66.1 15.1 %collective-permute-start.18 = (bf16[256,1024]{1,0:T(8,128)(2,1)}, bf16[256,1024]{1,0:T(8,128)(2,1)S(1)}, u32[]{:S(2)}, u32[]{:S(2)}) collective-permute-start(bf16[256,1024]{1,0:T(8,128)(2,1)} %get-tuple-element.90), channel_id=1, source_target_pairs={{3,1},{0,2},{7,5},{4,6},{11,9},{8,10},{15,13},{12,14},{19,17},{16,... | collective-permute-start | bytes 1572872 | tf_op jit(solution)/shard_map/ppermute | solution.py:429
  72.9 0.7 copy-start
  72.9 0.8 copy-start.1
  76.0 11.3 %collective-permute-start.16 = (bf16[80,1024]{1,0:T(8,128)(2,1)}, bf16[80,1024]{1,0:T(8,128)(2,1)S(1)}, u32[]{:S(2)}, u32[]{:S(2)}) collective-permute-start(bf16[80,1024]{1,0:T(8,128)(2,1)} %get-tuple-element.76), channel_id=1, source_target_pairs={{0,8},{1,9},{2,10},{3,11},{4,12},{5,13},{6,14},{7,15},{8,16},{9,17... | collective-permute-start | bytes 491528 | tf_op jit(solution)/shard_map/ppermute | solution.py:292
  76.0 11.3 %collective-permute-start.17 = (bf16[80,1024]{1,0:T(8,128)(2,1)}, bf16[80,1024]{1,0:T(8,128)(2,1)S(1)}, u32[]{:S(2)}, u32[]{:S(2)}) collective-permute-start(bf16[80,1024]{1,0:T(8,128)(2,1)} %get-tuple-element.77), channel_id=1, source_target_pairs={{0,24},{1,25},{2,26},{3,27},{4,28},{5,29},{6,30},{7,31},{8,0},{9,1... | collective-permute-start | bytes 491528 | tf_op jit(solution)/shard_map/ppermute | solution.py:292
  79.7 14.8 %collective-permute-start.23 = (bf16[256,1024]{1,0:T(8,128)(2,1)}, bf16[256,1024]{1,0:T(8,128)(2,1)}, u32[]{:S(2)}, u32[]{:S(2)}) collective-permute-start(bf16[256,1024]{1,0:T(8,128)(2,1)} %get-tuple-element.85), channel_id=1, source_target_pairs={{0,31},{3,4},{4,3},{7,8},{8,7},{11,12},{12,11},{15,16},{16,15},{19... | collective-permute-start | bytes 1572872 | tf_op jit(solution)/shard_map/ppermute | solution.py:441
  81.1 29.6 %collective-permute-start.27 = (bf16[256,1024]{1,0:T(8,128)(2,1)}, bf16[256,1024]{1,0:T(8,128)(2,1)}, u32[]{:S(2)}, u32[]{:S(2)}) collective-permute-start(bf16[256,1024]{1,0:T(8,128)(2,1)} %get-tuple-element.90), channel_id=1, source_target_pairs={{30,0},{5,3},{2,4},{9,7},{6,8},{13,11},{10,12},{17,15},{14,16},{21... | collective-permute-start | bytes 1572872 | tf_op jit(solution)/shard_map/ppermute | solution.py:442
  87.4 0.7 copy-start.7
  87.4 0.7 copy-start.8
  90.2 4.3 %collective-permute-start.20 = (bf16[32,1024]{1,0:T(8,128)(2,1)}, bf16[32,1024]{1,0:T(8,128)(2,1)S(1)}, u32[]{:S(2)}, u32[]{:S(2)}) collective-permute-start(bf16[32,1024]{1,0:T(8,128)(2,1)} %get-tuple-element.82), channel_id=1, source_target_pairs={{0,1},{1,0},{2,3},{3,2},{4,5},{5,4},{6,7},{7,6},{8,9},{9,8},{10,11... | collective-permute-start | bytes 196616 | tf_op jit(solution)/shard_map/ppermute | solution.py:292
  91.0 9.1 %collective-permute-start.21 = (bf16[32,1024]{1,0:T(8,128)(2,1)}, bf16[32,1024]{1,0:T(8,128)(2,1)S(1)}, u32[]{:S(2)}, u32[]{:S(2)}) collective-permute-start(bf16[32,1024]{1,0:T(8,128)(2,1)} %get-tuple-element.83), channel_id=1, source_target_pairs={{0,2},{1,3},{2,0},{3,1},{4,6},{5,7},{6,4},{7,5},{8,10},{9,11},{10,... | collective-permute-start | bytes 196616 | tf_op jit(solution)/shard_map/ppermute | solution.py:292
  91.4 10.0 %collective-permute-start.22 = (bf16[32,1024]{1,0:T(8,128)(2,1)}, bf16[32,1024]{1,0:T(8,128)(2,1)S(1)}, u32[]{:S(2)}, u32[]{:S(2)}) collective-permute-start(bf16[32,1024]{1,0:T(8,128)(2,1)} %get-tuple-element.84), channel_id=1, source_target_pairs={{0,3},{1,2},{2,1},{3,0},{4,7},{5,6},{6,5},{7,4},{8,11},{9,10},{10,... | collective-permute-start | bytes 196616 | tf_op jit(solution)/shard_map/ppermute | solution.py:292
  94.5 7.0 %copy-start.13 = (bf16[32,1024]{1,0:T(8,128)(2,1)}, bf16[32,1024]{1,0:T(8,128)(2,1)S(1)}, u32[]{:S(2)}) copy-start(bf16[32,1024]{1,0:T(8,128)(2,1)S(1)} %collective-permute-done.20.core_ref) | copy-start | bytes 196612
  100.1 1.4 %copy-start.14 = (bf16[32,1024]{1,0:T(8,128)(2,1)}, bf16[32,1024]{1,0:T(8,128)(2,1)S(1)}, u32[]{:S(2)}) copy-start(bf16[32,1024]{1,0:T(8,128)(2,1)S(1)} %collective-permute-done.21.side_ref) | copy-start | bytes 196612
  103.9 6.8 %copy-start.18 = (f32[32,128]{1,0:T(8,128)S(1)}, f32[32,128]{1,0:T(8,128)}, u32[]{:S(2)}) copy-start(f32[32,128]{1,0:T(8,128)} %get-tuple-element.89) | copy-start | bytes 49156
  103.9 4.6 %collective-permute-start.26 = (f32[32,128]{1,0:T(8,128)}, f32[32,128]{1,0:T(8,128)S(1)}, u32[]{:S(2)}, u32[]{:S(2)}) collective-permute-start(f32[32,128]{1,0:T(8,128)} %get-tuple-element.89), channel_id=1, source_target_pairs={{0,96},{1,97},{2,98},{3,99},{4,100},{5,101},{6,102},{7,103},{8,104... | collective-permute-start | bytes 49160 | tf_op jit(solution)/shard_map/ppermute | solution.py:413
  106.4 4.3 %collective-permute-start.25 = (f32[32,128]{1,0:T(8,128)}, f32[32,128]{1,0:T(8,128)S(1)}, u32[]{:S(2)}, u32[]{:S(2)}) collective-permute-start(f32[32,128]{1,0:T(8,128)} %get-tuple-element.89), channel_id=1, source_target_pairs={{0,64},{1,65},{2,66},{3,67},{4,68},{5,69},{6,70},{7,71},{8,72},{9,... | collective-permute-start | bytes 49160 | tf_op jit(solution)/shard_map/ppermute | solution.py:413
  106.9 3.8 %collective-permute-start.24 = (f32[32,128]{1,0:T(8,128)}, f32[32,128]{1,0:T(8,128)S(1)}, u32[]{:S(2)}, u32[]{:S(2)}) collective-permute-start(f32[32,128]{1,0:T(8,128)} %get-tuple-element.89), channel_id=1, source_target_pairs={{0,32},{1,33},{2,34},{3,35},{4,36},{5,37},{6,38},{7,39},{8,40},{9,... | collective-permute-start | bytes 49160 | tf_op jit(solution)/shard_map/ppermute | solution.py:413
  110.7 4.8 %collective-permute-start.28 = (f32[32,128]{1,0:T(8,128)S(1)}, f32[32,128]{1,0:T(8,128)S(1)}, u32[]{:S(2)}, u32[]{:S(2)}) collective-permute-start(f32[32,128]{1,0:T(8,128)S(1)} %add_add_fusion), channel_id=1, source_target_pairs={{0,128},{1,129},{2,130},{3,131},{4,132},{5,133},{6,134},{7,135},{8... | collective-permute-start | bytes 49160 | tf_op jit(solution)/shard_map/ppermute | solution.py:413
  113.7 0.8 copy-start.12
  (2 other events, 1.3 us)
